TPU v7x, 32 devices: a whole 2x2x4 slice. The times are simulated.
32 devices in a mesh: district: 8 (over z, y), blk: 4 (over x, core).
Axes of the slice: x: 2, y: 2, z: 4, core: 2. Of those that a mesh axis runs over, the one named last changes fastest.
Arguments:
- view_factor: bfloat16 [192, 24, 128, 128], P(('district', 'blk')), may hold values from 0 to 0.00064849854
- view_cols: int32 [192, 24], P(('district', 'blk')), may hold values from 0 to 47, as said below
- border_list: int32 [96], P(('district', 'blk')), may hold values from 0 to 5, as said below
- radiosity: bfloat16 [16, 24576], P(None, ('district', 'blk')), may hold values from 0.05 to 7.5, as said below
- reflectance: bfloat16 [16, 24576], P(None, ('district', 'blk')), may hold values from 0.29882812 to 0.8984375
- emissivity: float32 [24576], P(('district', 'blk')), may hold values from 0.6 to 0.98
- band_weight: float32 [16], replicated, may hold values from 0.1 to 0.6
- surface_temp: float32 [24576], P(('district', 'blk')), may hold values from 0.8 to 1.3
- patch_cell: int32 [24576], P(('district', 'blk')), may hold values from 0 to 16383
- air: float32 [64, 128, 4096], P(None, 'district', 'blk'), may hold values from -6 to 6
Outputs:
- radiosity_next: float32 [16, 24576], P(None, ('district', 'blk'))
- surface_next: float32 [24576], P(('district', 'blk'))
- air_next: float32 [64, 128, 4096], P(None, 'district', 'blk')
Inputs may be any that keep to these rules, and one draw needn't show every extreme that they name: `view_cols`: within one block row the 24 column numbers are different. `border_list`: the 3 entries of one device are different local block numbers. `radiosity`: Positive; values vary strongly from block to block.
All inputs are finite; a program needn't handle non-finite values.
Results may differ from a plain program's by a relative error of at most 0.0003.
Values may be sent and summed in bfloat16 or wider, within the bound.
No kernel may reach another device: no remote copies, remote signals or barrier semaphores. Data moves between devices by JAX's collectives and lax.ppermute only.
A program may use at most 128 MiB of HBM per device.

v0:
```python
import jax
import jax.numpy as jnp
from jax import lax
from jax.sharding import PartitionSpec as P

STEPS = 2


KAPPA = 0.15
GAIN = 0.02
COUPLE = 0.2
HEAT = 1.0


def extended(block, sides, width):
    for axis, dim in sides:
        count = lax.axis_size(axis)
        forward = [(i, i + 1) for i in range(count - 1)]
        backward = [(target, source) for source, target in forward]
        low = lax.ppermute(
            lax.slice_in_dim(block, block.shape[dim] - width, None, axis=dim), axis, forward
        )
        high = lax.ppermute(lax.slice_in_dim(block, 0, width, axis=dim), axis, backward)
        block = jnp.concatenate([low, block, high], axis=dim)
    return block


def from_behind(value, axis, steps):
    count = lax.axis_size(axis)
    initial, last = (max(0, -steps), min(count, count - steps))
    return lax.ppermute(value, axis, [(source, source + steps) for source in range(initial, last)])


def stencil_step(padded):
    vertical = jnp.pad(padded, ((1, 1), (0, 0), (0, 0)))
    center = padded[:, 1:-1, 1:-1]
    beside_all = padded[:, 2:, 1:-1] + padded[:, :-2, 1:-1]
    beside_all = beside_all + padded[:, 1:-1, 2:] + padded[:, 1:-1, :-2]
    beside_all = beside_all + vertical[2:, 1:-1, 1:-1] + vertical[:-2, 1:-1, 1:-1]
    return center + KAPPA * (beside_all - 6.0 * center)


def diffuse(air):
    field = air
    for step in range(STEPS):
        padded = extended(field, (("district", 1), ("blk", 2)), 1)
        field = stencil_step(padded)
    return field


def body(
    view_factor,
    view_cols,
    border_list,
    radiosity,
    reflectance,
    emissivity,
    band_weight,
    surface_temp,
    patch_cell,
    air,
):
    bands = radiosity.shape[0]
    row_blocks = view_factor.shape[0]
    nonzero = view_factor.shape[1]
    block_size = view_factor.shape[2]
    border_count = border_list.shape[0]
    own_blocks = radiosity.reshape(bands, row_blocks, block_size)
    border = jnp.take(own_blocks, border_list, axis=1).reshape(bands, border_count * block_size)
    from_left = from_behind(border, "district", 1)
    from_right = from_behind(border, "district", -1)
    visible = jnp.concatenate([radiosity, from_left, from_right], axis=1)
    empty = jnp.zeros((bands, row_blocks, nonzero, block_size), radiosity.dtype)
    piece = lax.all_gather(visible, "blk", axis=1, tiled=True)
    count = piece.shape[1] // block_size
    inside = (view_cols >= 0) & (view_cols < count)
    picks = jnp.clip(view_cols, 0, count - 1)
    pieces = piece.reshape(bands, count, block_size)
    selected = jnp.take(pieces, picks, axis=1)
    gathered = jnp.where(inside[None, :, :, None], selected, empty)
    irradiance = jnp.einsum(
        "brkj,rkij->bri", gathered, view_factor, preferred_element_type=jnp.float32
    )
    irradiance = irradiance.reshape(bands, row_blocks * block_size)
    squared = surface_temp * surface_temp
    emission = emissivity[None, :] * band_weight[:, None] * (squared * squared)[None, :]
    albedo = reflectance.astype(jnp.float32)
    radiosity_next = emission + albedo * irradiance
    air_cell = jnp.take(air[0].reshape(-1), patch_cell)
    absorbed = jnp.sum((1.0 - albedo) * irradiance, axis=0)
    emitted = jnp.sum(emission, axis=0)
    surface_next = (
        surface_temp + GAIN * (absorbed - emitted) - COUPLE * (surface_temp - 1.0 - air_cell)
    )
    diffused = diffuse(air)
    flux = COUPLE * (surface_next - 1.0 - air_cell)
    source = jnp.zeros((air.shape[1] * air.shape[2],), jnp.float32).at[patch_cell].add(flux)
    air_next = diffused.at[0].add(HEAT * source.reshape(air.shape[1], air.shape[2]))
    return (radiosity_next, surface_next, air_next)


def solution(mesh):
    in_specs = (
        P(("district", "blk"), None, None, None),
        P(("district", "blk"), None),
        P(("district", "blk")),
        P(None, ("district", "blk")),
        P(None, ("district", "blk")),
        P(("district", "blk")),
        P(),
        P(("district", "blk")),
        P(("district", "blk")),
        P(None, "district", "blk"),
    )
    out_specs = (P(None, ("district", "blk")), P(("district", "blk")), P(None, "district", "blk"))
    return jax.shard_map(body, mesh=mesh, in_specs=in_specs, out_specs=out_specs, check_vma=False)
```

profile of v0, /device:TPU:13, one launch (start us, length us, event | category | flops | bytes accessed | tf_op | source)
XLA Modules:
  0.0 132.6 jit_solution(11105954761368071946)
XLA Ops:
  0.6 0.0 copy-start.4
  0.6 0.7 compare_select_fusion.2
  1.3 0.7 compare_and_fusion.2
  2.0 0.7 copy_bitcast_fusion.1
  2.7 0.1 broadcast_bitcast_fusion
  2.8 0.6 gather_fusion
  3.4 3.1 %collective-permute-start = (bf16[16,384]{1,0:T(8,128)(2,1)S(1)}, bf16[16,384]{1,0:T(8,128)(2,1)S(1)}, u32[]{:S(2)}, u32[]{:S(2)}) collective-permute-start(bf16[16,384]{1,0:T(8,128)(2,1)S(1)} %bitcast_select_fusion), channel_id=1, source_target_pairs={{0,4},{4,8},{8,12},{12,16},{16,20},{20,24},{24,28},{1,5},{5,9},{9,... | collective-permute-start | bytes 36872 | tf_op jit(solution)/shard_map/ppermute | solution.py:31
  6.5 2.1 %collective-permute-start.1 = (bf16[16,384]{1,0:T(8,128)(2,1)S(1)}, bf16[16,384]{1,0:T(8,128)(2,1)S(1)}, u32[]{:S(2)}, u32[]{:S(2)}) collective-permute-start(bf16[16,384]{1,0:T(8,128)(2,1)S(1)} %bitcast_select_fusion), channel_id=1, source_target_pairs={{4,0},{8,4},{12,8},{16,12},{20,16},{24,20},{28,24},{5,1},{9,5},{13... | collective-permute-start | bytes 36872 | tf_op jit(solution)/shard_map/ppermute | solution.py:31
  8.7 2.7 %fusion.35 = (f32[64,1,1024]{2,1,0:T(1,128)S(1)}, f32[64,1,1024]{2,1,0:T(1,128)S(1)}) fusion(f32[64,16,1024]{2,1,0:T(8,128)} %param.21), kind=kLoop, calls=%fused_computation.85 | loop fusion | bytes 1048576 | tf_op jit(solution)/shard_map/slice | solution.py:21
  11.5 3.0 %collective-permute-start.2 = (f32[64,1,1024]{2,0,1:T(8,128)S(1)}, f32[64,1,1024]{2,0,1:T(8,128)S(1)}, u32[]{:S(2)}, u32[]{:S(2)}) collective-permute-start(f32[64,1,1024]{2,0,1:T(8,128)S(1)} %copy.72), channel_id=1, source_target_pairs={{4,0},{8,4},{12,8},{16,12},{20,16},{24,20},{28,24},{5,1},{9,5},{13... | collective-permute-start | bytes 786440 | tf_op jit(solution)/shard_map/ppermute | solution.py:23
  14.6 3.1 %collective-permute-start.3 = (f32[64,1,1024]{2,0,1:T(8,128)S(1)}, f32[64,1,1024]{2,0,1:T(8,128)S(1)}, u32[]{:S(2)}, u32[]{:S(2)}) collective-permute-start(f32[64,1,1024]{2,0,1:T(8,128)S(1)} %copy.73), channel_id=1, source_target_pairs={{0,4},{4,8},{8,12},{12,16},{16,20},{20,24},{24,28},{1,5},{5,9},{9,... | collective-permute-start | bytes 786440 | tf_op jit(solution)/shard_map/ppermute | solution.py:20
  17.7 0.7 compare_select_fusion.1
  18.4 0.7 compare_and_fusion
  19.1 0.8 slice_bitcast_fusion
  20.0 0.1 reshape.85
  20.1 0.7 multiply_multiply_fusion.1
  20.7 0.7 compare_select_fusion
  21.5 4.5 %gather_fusion.2 = f32[768]{0:T(1024)S(1)} fusion(f32[16384]{0:T(1024)S(1)} %bitcast.35, s32[1024]{0:T(1024)S(1)} %pad_clamp_fusion), kind=kCustom, calls=%fused_computation.2 | custom fusion | bytes 9216 | tf_op jit(solution)/shard_map/jit(_take)/gather | solution.py:89
  25.9 0.0 collective-permute-done
  25.9 0.0 collective-permute-done.1
  26.0 7.2 %all_gather.3 = bf16[16,6144]{1,0:T(8,128)(2,1)S(1)} all-gather(bf16[16,1536]{1,0:T(8,128)(2,1)S(1)} %pad_maximum_fusion.18), channel_id=1, replica_groups=mesh['district'=8,'blk'=4] {'blk'}, dimensions={1}, use_global_device_ids=true | all-gather | bytes 245760 | tf_op jit(solution)/shard_map/all_gather | solution.py:74
  33.2 0.3 copy.48
  33.5 0.3 copy.50
  33.8 3.2 %pad_maximum_fusion = f32[64,18,1024]{2,1,0:T(8,128)S(1)} fusion(f32[64,1,1024]{2,1,0:T(1,128)S(1)} %copy.48, f32[64,16,1024]{2,1,0:T(8,128)} %param.21, f32[64,1,1024]{2,1,0:T(1,128)S(1)} %copy.50), kind=kLoop, calls=%fused_computation.8 | loop fusion | flops 2359296 | bytes 9437184 | tf_op jit(solution)/shard_map/concatenate | solution.py:24
  37.0 2.7 %copy-done.2 = f32[64,18,1024]{2,1,0:T(8,128)} copy-done((f32[64,18,1024]{2,1,0:T(8,128)}, f32[64,18,1024]{2,1,0:T(8,128)S(1)}, u32[]{:S(2)}) %copy-start.2) | copy-done | bytes 4718616
  39.7 0.3 fusion.33
  40.0 0.3 copy.53
  40.3 2.1 %collective-permute-start.4 = (f32[64,18,1]{0,1,2:T(8,128)S(1)}, f32[64,18,1]{0,1,2:T(8,128)S(1)}, u32[]{:S(2)}, u32[]{:S(2)}) collective-permute-start(f32[64,18,1]{0,1,2:T(8,128)S(1)} %copy.53), channel_id=1, source_target_pairs={{1,0},{2,1},{3,2},{5,4},{6,5},{7,6},{9,8},{10,9},{11,10},{13,12},{... | collective-permute-start | bytes 13832 | tf_op jit(solution)/shard_map/ppermute | solution.py:23
  42.3 0.3 copy.55
  42.6 3.5 %collective-permute-start.5 = (f32[64,18,1]{0,1,2:T(8,128)S(1)}, f32[64,18,1]{0,1,2:T(8,128)S(1)}, u32[]{:S(2)}, u32[]{:S(2)}) collective-permute-start(f32[64,18,1]{0,1,2:T(8,128)S(1)} %copy.55), channel_id=1, source_target_pairs={{0,1},{1,2},{2,3},{4,5},{5,6},{6,7},{8,9},{9,10},{10,11},{12,13},{... | collective-permute-start | bytes 13832 | tf_op jit(solution)/shard_map/ppermute | solution.py:20
  46.2 0.7 gather_fusion.1
  46.9 0.4 copy.54
  47.3 0.4 copy.56
  47.7 8.9 %concatenate.47 = f32[64,18,1026]{2,1,0:T(8,128)} concatenate(f32[64,18,1]{2,1,0:T(8,128)S(1)} %copy.56, f32[64,18,1024]{2,1,0:T(8,128)} %copy-done.2, f32[64,18,1]{2,1,0:T(8,128)S(1)} %copy.54), dimensions={2} | concatenate | bytes 9455616 | tf_op jit(solution)/shard_map/concatenate | solution.py:24
  56.5 15.9 %fusion.4 = f32[64,16,1024]{2,1,0:T(8,128)S(1)} fusion(f32[64,16,1024]{2,1,0:T(8,128)} %param.21, f32[64,18,1026]{2,1,0:T(8,128)} %concatenate.47, f32[64,18,1]{2,1,0:T(8,128)S(1)} %copy.56, f32[64,1,1024]{2,1,0:T(1,128)S(1)} %copy.48, f32[64,1,1024]{2,1,0:T(1,128)S(1)} %copy.50, f32[64,18,1]{2,1,0:T(8,128)S(1)} %copy.54), kind=kLoop, calls=%fused_computation.14 | loop fusion | flops 17825792 | bytes 13649920 | tf_op jit(solution)/shard_map/add | solution.py:40
  72.5 0.0 copy-start
  72.5 0.0 copy-start.5
  72.5 0.0 copy-start.8
  72.5 0.0 copy-start.9
  72.5 0.5 fusion.34
  73.1 2.1 %collective-permute-start.6 = (f32[64,1,1024]{2,0,1:T(8,128)S(1)}, f32[64,1,1024]{2,0,1:T(8,128)S(1)}, u32[]{:S(2)}, u32[]{:S(2)}) collective-permute-start(f32[64,1,1024]{2,0,1:T(8,128)S(1)} %copy.59), channel_id=1, source_target_pairs={{4,0},{8,4},{12,8},{16,12},{20,16},{24,20},{28,24},{5,1},{9,5},{13... | collective-permute-start | bytes 786440 | tf_op jit(solution)/shard_map/ppermute | solution.py:23
  75.3 4.2 %collective-permute-start.7 = (f32[64,1,1024]{2,0,1:T(8,128)S(1)}, f32[64,1,1024]{2,0,1:T(8,128)S(1)}, u32[]{:S(2)}, u32[]{:S(2)}) collective-permute-start(f32[64,1,1024]{2,0,1:T(8,128)S(1)} %copy.61), channel_id=1, source_target_pairs={{0,4},{4,8},{8,12},{12,16},{16,20},{20,24},{24,28},{1,5},{5,9},{9,... | collective-permute-start | bytes 786440 | tf_op jit(solution)/shard_map/ppermute | solution.py:20
  79.5 3.2 %convolution_bitcast_fusion = f32[6,2,8,128]{3,2,1,0:T(8,128)S(1)} fusion(bf16[6,24,128,128]{3,2,1,0:T(8,128)(2,1)} %param.12, bf16[6,24,16,128]{3,2,1,0:T(8,128)(2,1)S(1)} %bitcast.36, pred[6,24]{1,0:T(8,128)(4,1)S(1)} %get-tuple-element.32, pred[6,24]{1,0:T(8,128)(4,1)S(1)} %get-tuple-element.31), kind=kOutput, calls=%fused_computation.42 | convolution fusion | flops 76087296 | bytes 5357856 | tf_op jit(solution)/shard_map/brkj,rkij->bri/dot_general | solution.py:81
  82.8 0.0 copy-done.8
  82.8 0.7 fusion.26
  83.5 2.9 %collective-permute-done.6 = f32[64,1,1024]{2,0,1:T(8,128)S(1)} collective-permute-done((f32[64,1,1024]{2,0,1:T(8,128)S(1)}, f32[64,1,1024]{2,0,1:T(8,128)S(1)}, u32[]{:S(2)}, u32[]{:S(2)}) %collective-permute-start.6) | collective-permute-done | bytes 262176 | tf_op jit(solution)/shard_map/ppermute | solution.py:23
  86.4 0.3 copy.60
  86.6 2.6 %collective-permute-done.7 = f32[64,1,1024]{2,0,1:T(8,128)S(1)} collective-permute-done((f32[64,1,1024]{2,0,1:T(8,128)S(1)}, f32[64,1,1024]{2,0,1:T(8,128)S(1)}, u32[]{:S(2)}, u32[]{:S(2)}) %collective-permute-start.7) | collective-permute-done | bytes 262176 | tf_op jit(solution)/shard_map/ppermute | solution.py:20
  89.2 0.3 copy.62
  89.5 1.1 pad_maximum_fusion.1
  90.6 2.7 %copy-done.1 = f32[64,18,1024]{2,1,0:T(8,128)} copy-done((f32[64,18,1024]{2,1,0:T(8,128)}, f32[64,18,1024]{2,1,0:T(8,128)S(1)}, u32[]{:S(2)}) %copy-start.1) | copy-done | bytes 4718616
  93.2 0.3 fusion.32
  93.5 0.3 copy.65
  93.8 2.3 %collective-permute-start.8 = (f32[64,18,1]{0,1,2:T(8,128)S(1)}, f32[64,18,1]{0,1,2:T(8,128)S(1)}, u32[]{:S(2)}, u32[]{:S(2)}) collective-permute-start(f32[64,18,1]{0,1,2:T(8,128)S(1)} %copy.65), channel_id=1, source_target_pairs={{1,0},{2,1},{3,2},{5,4},{6,5},{7,6},{9,8},{10,9},{11,10},{13,12},{... | collective-permute-start | bytes 13832 | tf_op jit(solution)/shard_map/ppermute | solution.py:23
  96.2 0.3 copy.67
  96.5 3.3 %collective-permute-start.9 = (f32[64,18,1]{0,1,2:T(8,128)S(1)}, f32[64,18,1]{0,1,2:T(8,128)S(1)}, u32[]{:S(2)}, u32[]{:S(2)}) collective-permute-start(f32[64,18,1]{0,1,2:T(8,128)S(1)} %copy.67), channel_id=1, source_target_pairs={{0,1},{1,2},{2,3},{4,5},{5,6},{6,7},{8,9},{9,10},{10,11},{12,13},{... | collective-permute-start | bytes 13832 | tf_op jit(solution)/shard_map/ppermute | solution.py:20
  99.7 0.6 subtract_multiply_fusion
  100.4 4.6 %scatter_custom_fusion = f32[16384]{0:T(1024)S(1)} fusion(s32[768]{0:T(1024)S(1)} %compare_select_fusion, f32[768]{0:T(1024)S(1)} %get-tuple-element.18, f32[]{:T(128)} %constant.88.clone.1), kind=kCustom, calls=%fused_computation.62 | custom fusion | flops 768 | bytes 65540 | tf_op jit(solution)/shard_map/scatter-add | solution.py:97
  105.0 0.4 copy.66
  105.4 0.4 copy.68
  105.7 8.9 %concatenate.53 = f32[64,18,1026]{2,1,0:T(8,128)} concatenate(f32[64,18,1]{2,1,0:T(8,128)S(1)} %copy.68, f32[64,18,1024]{2,1,0:T(8,128)} %copy-done.1, f32[64,18,1]{2,1,0:T(8,128)S(1)} %copy.66), dimensions={2} | concatenate | bytes 9455616 | tf_op jit(solution)/shard_map/concatenate | solution.py:24
  114.6 16.0 %fusion.9 = f32[64,16,1024]{2,1,0:T(8,128)S(1)} fusion(f32[64,16,1024]{2,1,0:T(8,128)} %copy-done, f32[64,18,1026]{2,1,0:T(8,128)} %concatenate.53, f32[64,18,1]{2,1,0:T(8,128)S(1)} %copy.68, f32[64,1,1024]{2,1,0:T(1,128)S(1)} %copy.60, f32[64,1,1024]{2,1,0:T(1,128)S(1)} %copy.62, f32[64,18,1]{2,1,0:T(8,128)S(1)} %copy.66), kind=kLoop, calls=%fused_computation.19 | loop fusion | flops 17825792 | bytes 13649920 | tf_op jit(solution)/shard_map/add | solution.py:40
  130.6 0.0 copy-start.3
  130.6 2.0 %copy-done.3 = f32[64,16,1024]{2,1,0:T(8,128)} copy-done((f32[64,16,1024]{2,1,0:T(8,128)}, f32[64,16,1024]{2,1,0:T(8,128)S(1)}, u32[]{:S(2)}) %copy-start.3) | copy-done | bytes 4194328
  (29 shorter events, 0.4 us)
Async XLA Ops:
  0.6 25.3 %copy-start.4 = (bf16[16,768]{1,0:T(8,128)(2,1)S(1)}, bf16[16,768]{1,0:T(8,128)(2,1)}, u32[]{:S(2)}) copy-start(bf16[16,768]{1,0:T(8,128)(2,1)} %param.15) | copy-start | bytes 73732
  3.4 22.6 %collective-permute-start = (bf16[16,384]{1,0:T(8,128)(2,1)S(1)}, bf16[16,384]{1,0:T(8,128)(2,1)S(1)}, u32[]{:S(2)}, u32[]{:S(2)}) collective-permute-start(bf16[16,384]{1,0:T(8,128)(2,1)S(1)} %bitcast_select_fusion), channel_id=1, source_target_pairs={{0,4},{4,8},{8,12},{12,16},{16,20},{20,24},{24,28},{1,5},{5,9},{9,... | collective-permute-start | bytes 36872 | tf_op jit(solution)/shard_map/ppermute | solution.py:31
  6.5 19.4 %collective-permute-start.1 = (bf16[16,384]{1,0:T(8,128)(2,1)S(1)}, bf16[16,384]{1,0:T(8,128)(2,1)S(1)}, u32[]{:S(2)}, u32[]{:S(2)}) collective-permute-start(bf16[16,384]{1,0:T(8,128)(2,1)S(1)} %bitcast_select_fusion), channel_id=1, source_target_pairs={{4,0},{8,4},{12,8},{16,12},{20,16},{24,20},{28,24},{5,1},{9,5},{13... | collective-permute-start | bytes 36872 | tf_op jit(solution)/shard_map/ppermute | solution.py:31
  11.5 21.7 %collective-permute-start.2 = (f32[64,1,1024]{2,0,1:T(8,128)S(1)}, f32[64,1,1024]{2,0,1:T(8,128)S(1)}, u32[]{:S(2)}, u32[]{:S(2)}) collective-permute-start(f32[64,1,1024]{2,0,1:T(8,128)S(1)} %copy.72), channel_id=1, source_target_pairs={{4,0},{8,4},{12,8},{16,12},{20,16},{24,20},{28,24},{5,1},{9,5},{13... | collective-permute-start | bytes 786440 | tf_op jit(solution)/shard_map/ppermute | solution.py:23
  14.6 18.9 %collective-permute-start.3 = (f32[64,1,1024]{2,0,1:T(8,128)S(1)}, f32[64,1,1024]{2,0,1:T(8,128)S(1)}, u32[]{:S(2)}, u32[]{:S(2)}) collective-permute-start(f32[64,1,1024]{2,0,1:T(8,128)S(1)} %copy.73), channel_id=1, source_target_pairs={{0,4},{4,8},{8,12},{12,16},{16,20},{20,24},{24,28},{1,5},{5,9},{9,... | collective-permute-start | bytes 786440 | tf_op jit(solution)/shard_map/ppermute | solution.py:20
  37.0 2.7 %copy-start.2 = (f32[64,18,1024]{2,1,0:T(8,128)}, f32[64,18,1024]{2,1,0:T(8,128)S(1)}, u32[]{:S(2)}) copy-start(f32[64,18,1024]{2,1,0:T(8,128)S(1)} %pad_maximum_fusion) | copy-start | bytes 14155780
  40.3 6.7 %collective-permute-start.4 = (f32[64,18,1]{0,1,2:T(8,128)S(1)}, f32[64,18,1]{0,1,2:T(8,128)S(1)}, u32[]{:S(2)}, u32[]{:S(2)}) collective-permute-start(f32[64,18,1]{0,1,2:T(8,128)S(1)} %copy.53), channel_id=1, source_target_pairs={{1,0},{2,1},{3,2},{5,4},{6,5},{7,6},{9,8},{10,9},{11,10},{13,12},{... | collective-permute-start | bytes 13832 | tf_op jit(solution)/shard_map/ppermute | solution.py:23
  42.6 4.6 %collective-permute-start.5 = (f32[64,18,1]{0,1,2:T(8,128)S(1)}, f32[64,18,1]{0,1,2:T(8,128)S(1)}, u32[]{:S(2)}, u32[]{:S(2)}) collective-permute-start(f32[64,18,1]{0,1,2:T(8,128)S(1)} %copy.55), channel_id=1, source_target_pairs={{0,1},{1,2},{2,3},{4,5},{5,6},{6,7},{8,9},{9,10},{10,11},{12,13},{... | collective-permute-start | bytes 13832 | tf_op jit(solution)/shard_map/ppermute | solution.py:20
  72.5 17.0 %copy-start = (f32[64,16,1024]{2,1,0:T(8,128)}, f32[64,16,1024]{2,1,0:T(8,128)S(1)}, u32[]{:S(2)}) copy-start(f32[64,16,1024]{2,1,0:T(8,128)S(1)} %fusion.4) | copy-start | bytes 12582916
  72.5 10.3 %copy-start.5 = (bf16[16,768]{1,0:T(8,128)(2,1)S(1)}, bf16[16,768]{1,0:T(8,128)(2,1)}, u32[]{:S(2)}) copy-start(bf16[16,768]{1,0:T(8,128)(2,1)} %param.16) | copy-start | bytes 73732
  72.5 10.3 %copy-start.8 = (f32[768]{0:T(1024)S(1)}, f32[768]{0:T(1024)}, u32[]{:S(2)}) copy-start(f32[768]{0:T(1024)} %param.17) | copy-start | bytes 9220
  72.5 10.3 %copy-start.9 = (f32[16]{0:T(128)S(1)}, f32[16]{0:T(128)}, u32[]{:S(2)}) copy-start(f32[16]{0:T(128)} %param.18) | copy-start | bytes 196
  73.1 13.3 %collective-permute-start.6 = (f32[64,1,1024]{2,0,1:T(8,128)S(1)}, f32[64,1,1024]{2,0,1:T(8,128)S(1)}, u32[]{:S(2)}, u32[]{:S(2)}) collective-permute-start(f32[64,1,1024]{2,0,1:T(8,128)S(1)} %copy.59), channel_id=1, source_target_pairs={{4,0},{8,4},{12,8},{16,12},{20,16},{24,20},{28,24},{5,1},{9,5},{13... | collective-permute-start | bytes 786440 | tf_op jit(solution)/shard_map/ppermute | solution.py:23
  75.3 13.9 %collective-permute-start.7 = (f32[64,1,1024]{2,0,1:T(8,128)S(1)}, f32[64,1,1024]{2,0,1:T(8,128)S(1)}, u32[]{:S(2)}, u32[]{:S(2)}) collective-permute-start(f32[64,1,1024]{2,0,1:T(8,128)S(1)} %copy.61), channel_id=1, source_target_pairs={{0,4},{4,8},{8,12},{12,16},{16,20},{20,24},{24,28},{1,5},{5,9},{9,... | collective-permute-start | bytes 786440 | tf_op jit(solution)/shard_map/ppermute | solution.py:20
  90.6 2.7 %copy-start.1 = (f32[64,18,1024]{2,1,0:T(8,128)}, f32[64,18,1024]{2,1,0:T(8,128)S(1)}, u32[]{:S(2)}) copy-start(f32[64,18,1024]{2,1,0:T(8,128)S(1)} %pad_maximum_fusion.1) | copy-start | bytes 14155780
  93.2 6.5 %copy-start.6 = (f32[768]{0:T(1024)S(1)}, f32[768]{0:T(1024)}, u32[]{:S(2)}) copy-start(f32[768]{0:T(1024)} %param.19) | copy-start | bytes 9220
  93.2 6.5 %copy-start.7 = (s32[768]{0:T(1024)S(1)}, s32[768]{0:T(1024)}, u32[]{:S(2)}) copy-start(s32[768]{0:T(1024)} %param.20) | copy-start | bytes 9220
  93.8 11.2 %collective-permute-start.8 = (f32[64,18,1]{0,1,2:T(8,128)S(1)}, f32[64,18,1]{0,1,2:T(8,128)S(1)}, u32[]{:S(2)}, u32[]{:S(2)}) collective-permute-start(f32[64,18,1]{0,1,2:T(8,128)S(1)} %copy.65), channel_id=1, source_target_pairs={{1,0},{2,1},{3,2},{5,4},{6,5},{7,6},{9,8},{10,9},{11,10},{13,12},{... | collective-permute-start | bytes 13832 | tf_op jit(solution)/shard_map/ppermute | solution.py:23
  96.5 8.9 %collective-permute-start.9 = (f32[64,18,1]{0,1,2:T(8,128)S(1)}, f32[64,18,1]{0,1,2:T(8,128)S(1)}, u32[]{:S(2)}, u32[]{:S(2)}) collective-permute-start(f32[64,18,1]{0,1,2:T(8,128)S(1)} %copy.67), channel_id=1, source_target_pairs={{0,1},{1,2},{2,3},{4,5},{5,6},{6,7},{8,9},{9,10},{10,11},{12,13},{... | collective-permute-start | bytes 13832 | tf_op jit(solution)/shard_map/ppermute | solution.py:20
  130.6 2.0 %copy-start.3 = (f32[64,16,1024]{2,1,0:T(8,128)}, f32[64,16,1024]{2,1,0:T(8,128)S(1)}, u32[]{:S(2)}) copy-start(f32[64,16,1024]{2,1,0:T(8,128)S(1)} %fusion.23) | copy-start | bytes 12582916
where the time goes:
time: 134 us; the launch traced here: 133 us
  other arithmetic  46.2 us (34%)
  local copies, waits for them, and re-layouts  40.5 us (30%)
  starting transfers between devices  29 us (22%)
  blocking collectives  7.24 us (5%)
  waiting for transfers between devices  5.47 us (4%)
  matrix products  3.21 us (2%)
    add x2, other arithmetic, stencil_step(): return center + KAPPA * (beside_all - 6.0 * center)  31.9 us
    concatenate x2, local copies, waits for them, and re-layouts, extended(): block = jnp.concatenate([low, block, high], axis=dim)  17.8 us
    ppermute x4, starting transfers between devices, extended(): lax.ppermute(lax.slice_in_dim(block, block.shape[dim] - width, None, axis...  14.1 us
    ppermute x4, starting transfers between devices, extended(): lax.ppermute(lax.slice_in_dim(block, 0, width, axis=dim), axis, backward)  9.55 us
    unnamed x24, local copies, waits for them, and re-layouts  8.37 us
    all_gather x1, blocking collectives, body(): piece = lax.all_gather(visible, 'blk', axis=1, tiled=True)  7.24 us
    ppermute x2, starting transfers between devices, from_behind(): lax.ppermute(value, axis, [(source, source + steps) for source in range(i...  5.28 us
    scatter-add x1, other arithmetic, body(): jnp.zeros((air.shape[1] * air.shape[2],), jnp.float32).at[patch_cell]  4.61 us
  transfers between devices with their start and end apart: 10, of which 2 were waited for; matrix products, arithmetic and copies ran while one was open for 17% of the time, Pallas kernels for 0%

commit v1 on v0

v1 whole, which is shorter than its diff:
```python
import functools

import jax
import jax.numpy as jnp
from jax import lax
from jax.experimental import pallas as pl
from jax.experimental.pallas import tpu as pltpu
from jax.sharding import PartitionSpec as P

KAPPA = 0.15
GAIN = 0.02
COUPLE = 0.2
HEAT = 1.0
CENTRE = (1.0 - 6.0 * KAPPA) / KAPPA
SQUARE = KAPPA * KAPPA

F32 = jnp.float32
BF16 = jnp.bfloat16
LANES = 128
VMEM = pltpu.VMEM
SMEM = pltpu.SMEM
DMA = pltpu.SemaphoreType.DMA
PACK_COST, ROWS_COST, JOIN_COST, MAIN_COST = 2, 2, 1, 8


def params(mebibytes):
    return pltpu.CompilerParams(vmem_limit_bytes=mebibytes << 20)


def cost(microseconds):
    return pl.CostEstimate(flops=0, bytes_accessed=microseconds * 3_000_000, transcendentals=0)


def in_hbm(value):
    return pltpu.with_memory_space_constraint(value, pltpu.HBM)


WHOLE = pl.BlockSpec(memory_space=VMEM)
PLACE = pl.BlockSpec(memory_space=pl.ANY)


def iota(shape, axis):
    return lax.broadcasted_iota(jnp.int32, shape, axis)


def split(value, pieces):
    out = []
    for _ in range(pieces):
        piece = value.astype(BF16)
        out.append(piece)
        value = value - piece.astype(F32)
    return out


def plane_neighbours(load, tiles):
    centre = [load(i) for i in range(tiles)]
    rows = centre[0].shape[0]
    lane = iota((rows, LANES), 1)
    row = iota((rows, LANES), 0)
    right = [pltpu.roll(c, 1, 1) for c in centre]
    left = [pltpu.roll(c, LANES - 1, 1) for c in centre]
    zero = jnp.zeros((rows, LANES), F32)
    for i, c in enumerate(centre):
        total = jnp.where(lane == 0, right[i - 1] if i else zero, right[i])
        total = total + jnp.where(
            lane == LANES - 1, left[i + 1] if i + 1 < tiles else zero, left[i]
        )
        total = total + jnp.where(row == 0, 0.0, pltpu.roll(c, 1, 0))
        total = total + jnp.where(row == rows - 1, 0.0, pltpu.roll(c, rows - 1, 0))
        yield c, total


def pack_kernel(
    border_ref,
    radiosity_ref,
    air_ref,
    near_small,
    far_small,
    own_ref,
    border,
    blocks_of,
    ends,
    sem,
    end_sem,
):
    levels, depth, width = air_ref.shape
    blocks = radiosity_ref.shape[1] // LANES
    borders = border_ref.shape[0]
    odd = lax.rem(lax.axis_index("district"), 2)
    edge = [
        pltpu.make_async_copy(
            air_ref.at[:, :, pl.ds(at, LANES)], ends.at[j], end_sem.at[j]
        )
        for j, at in enumerate((0, width - LANES))
    ]
    first = [
        pltpu.make_async_copy(border_ref, border, sem.at[0]),
        pltpu.make_async_copy(radiosity_ref, blocks_of, sem.at[1]),
    ]
    for c in edge + first:
        c.start()
    for c in first:
        c.wait()
    for s in range(blocks):
        own_ref[s] = blocks_of[:, s * LANES : (s + 1) * LANES]
    for s in range(borders):
        tile = own_ref[border[s]]
        near_small[s] = tile
        far_small[s] = tile
    place = iota((depth, LANES), 1) // 2
    corner_rows = [[], []]
    for j in range(2):
        edge[j].wait()
        packed = jnp.zeros((depth, LANES), F32)
        for z in range(levels):
            tile = ends[j, z]
            turn = (2 * z + 2 * j) % LANES
            packed = jnp.where(place == z, pltpu.roll(tile, turn, 1) if turn else tile, packed)
        for n, piece in enumerate(split(packed, 2)):
            own_ref[blocks + 2 * j + n] = piece
            wide = piece.astype(F32)
            corner_rows[0].append(wide[0:1])
            corner_rows[1].append(wide[depth - 1 : depth])
    sub = iota((16, LANES), 0)
    for which, small in enumerate((near_small, far_small)):
        last = (odd == 0) if which == 0 else (odd == 1)
        corner = jnp.zeros((16, LANES), F32)
        for n in range(4):
            row = jnp.where(last, corner_rows[1][n], corner_rows[0][n])
            corner = jnp.where(sub == n, row, corner)
        small[borders] = corner.astype(BF16)


def pack(border_list, radiosity, air):
    levels, depth, _ = air.shape
    blocks = radiosity.shape[1] // LANES
    borders = border_list.shape[0]
    small = jax.ShapeDtypeStruct((borders + 1, 16, LANES), BF16)
    own = jax.ShapeDtypeStruct((blocks + 4, 16, LANES), BF16)
    return pl.pallas_call(
        pack_kernel,
        out_shape=(small, small, own),
        in_specs=[PLACE] * 3,
        out_specs=(WHOLE,) * 3,
        scratch_shapes=[
            SMEM(border_list.shape, border_list.dtype),
            VMEM(radiosity.shape, BF16),
            VMEM((2, levels, depth, LANES), F32),
            DMA((2,)),
            DMA((2,)),
        ],
        compiler_params=params(8),
        cost_estimate=cost(PACK_COST),
        name="pack",
    )(in_hbm(border_list), in_hbm(radiosity), in_hbm(air))


def rows_kernel(air_ref, near_rows, far_rows, slabs, sem):
    levels, depth, width = air_ref.shape
    tiles = width // LANES
    odd = lax.rem(lax.axis_index("district"), 2)
    copies = [
        pltpu.make_async_copy(air_ref.at[:, r, :], slabs.at[i], sem.at[i])
        for i, r in enumerate((depth - 1, depth - 2, 0, 1))
    ]
    for c in copies:
        c.start()
    for c in copies:
        c.wait()
    for which, rows in enumerate((near_rows, far_rows)):
        base = 2 * (odd if which == 0 else 1 - odd)

        def lost(i):
            value = slabs[base, :, i * LANES : (i + 1) * LANES]
            return value - value.astype(BF16).astype(F32)

        for i, (c, around) in enumerate(plane_neighbours(lost, tiles)):
            at = slice(i * LANES, (i + 1) * LANES)
            rows[0, :, at] = slabs[base, :, at].astype(BF16)
            rows[1, :, at] = (slabs[base + 1, :, at] + CENTRE * 2.0 * c + 2.0 * around).astype(BF16)


def rows(air):
    levels, _, width = air.shape
    out = jax.ShapeDtypeStruct((2, levels, width), BF16)
    return pl.pallas_call(
        rows_kernel,
        out_shape=(out, out),
        in_specs=[PLACE],
        out_specs=(WHOLE, WHOLE),
        scratch_shapes=[VMEM((4, levels, width), F32), DMA((4,))],
        compiler_params=params(8),
        cost_estimate=cost(ROWS_COST),
        name="rows",
    )(in_hbm(air))


def join_kernel(own_ref, near_ref, far_ref, rows_ref, out_ref, rows_out):
    odd = lax.rem(lax.axis_index("district"), 2)
    borders = near_ref.shape[0] - 1
    blocks = own_ref.shape[0] - 4
    rows_out[...] = rows_ref[...]
    for s in range(blocks):
        out_ref[s] = own_ref[s]
    for s in range(4):
        out_ref[blocks + 2 * borders + 2 + s] = own_ref[blocks + s]
    for s in range(borders + 1):
        before = jnp.where(odd == 1, near_ref[s].astype(F32), far_ref[s].astype(F32)).astype(BF16)
        after = jnp.where(odd == 1, far_ref[s].astype(F32), near_ref[s].astype(F32)).astype(BF16)
        at = blocks + s if s < borders else blocks + 2 * borders
        out_ref[at] = before
        out_ref[at + (borders if s < borders else 1)] = after


def join(own, near, far, rows):
    count = own.shape[0] + 2 * near.shape[0]
    return pl.pallas_call(
        join_kernel,
        out_shape=(
            jax.ShapeDtypeStruct((count, 16, LANES), BF16),
            jax.ShapeDtypeStruct(rows.shape, BF16),
        ),
        in_specs=[WHOLE] * 4,
        out_specs=(WHOLE, WHOLE),
        compiler_params=params(8),
        cost_estimate=cost(JOIN_COST),
        name="join",
    )(own, near, far, rows)


def main_kernel(
    cols_ref,
    weight_ref,
    own_ref,
    one_ref,
    two_ref,
    three_ref,
    reflectance_ref,
    emissivity_ref,
    temp_ref,
    cell_ref,
    view_ref,
    air_ref,
    radiosity_out,
    surface_out,
    air_out,
    edge_out,
    once,
    twice,
    pieces,
    ends,
    surface_buf,
    out_sem,
    edge_sem,
    surface_sem,
    *,
    chunk,
):
    levels, depth, width = air_ref.shape
    tiles = width // LANES
    row_blocks, nonzero = view_ref.shape[0], view_ref.shape[1]
    chunks = levels // chunk
    district = lax.axis_index("district")
    blk = lax.axis_index("blk")
    districts = lax.axis_size("district")
    blks = lax.axis_size("blk")
    flag = lambda cond: jnp.where(cond, 1.0, 0.0).astype(F32)
    has_top, has_bottom = flag(district > 0), flag(district < districts - 1)
    has_left, has_right = flag(blk > 0), flag(blk < blks - 1)

    visible = own_ref.shape[0] - 6
    for n, ref in enumerate((own_ref, one_ref, two_ref, three_ref)):
        for s in range(visible):
            pieces[n * visible + s] = ref[s]

    def pair(ref, at):
        return ref[at].astype(F32) + ref[at + 1].astype(F32)

    sub = iota((depth, LANES), 0)
    lane = iota((depth, LANES), 1)
    even = lax.rem(blk, 2) == 0
    col_at = visible + 2
    left_cols = jnp.where(even, pair(three_ref, col_at + 2), pair(one_ref, col_at + 2)) * has_left
    right_cols = jnp.where(even, pair(one_ref, col_at), pair(three_ref, col_at)) * has_right

    def corner(left_side, top):
        at = visible + (0 if top else 1)
        one, three = one_ref[at].astype(F32), three_ref[at].astype(F32)
        value = jnp.where(even, three, one) if left_side else jnp.where(even, one, three)
        value = value * (has_left if left_side else has_right)
        k = 2 if left_side else 0
        row = value[k : k + 1] + value[k + 1 : k + 2]
        return pltpu.roll(row, LANES - 1, 1) if left_side else row

    own_left, own_right = pair(own_ref, col_at), pair(own_ref, col_at + 2)
    for side in range(2):
        if side == 0:
            first, second = pltpu.roll(left_cols, LANES - 1, 1), left_cols
            inner, has = own_left, has_left
        else:
            first, second = right_cols, pltpu.roll(right_cols, LANES - 1, 1)
            inner, has = pltpu.roll(own_right, LANES - 1, 1), has_right
        top, bottom = (corner(side == 0, up) for up in (True, False))
        around = jnp.where(sub == 0, 2.0 * top, pltpu.roll(first, 1, 0))
        around = around + jnp.where(sub == depth - 1, 2.0 * bottom, pltpu.roll(first, depth - 1, 0))
        around = around + jnp.where(lane < 2, 0.0, pltpu.roll(first, 2, 1))
        around = around + jnp.where(lane >= 2 * levels - 2, 0.0, pltpu.roll(first, LANES - 2, 1))
        ends[side, 0] = first
        ends[side, 1] = CENTRE * first + around + second + inner * has

    half = depth // 2
    halves = depth // half
    sub8 = iota((half, LANES), 0)
    lane8 = iota((half, LANES), 1)
    first_lane, last_lane = lane8 == 0, lane8 == LANES - 1
    first_row, last_row = sub8 == 0, sub8 == half - 1
    zero = jnp.zeros((half, LANES), F32)

    def stencil(z, src, dst, which):
        turn = lax.rem(LANES - 2 * z, LANES)
        below, above = jnp.maximum(z - 1, 0), jnp.minimum(z + 1, levels - 1)
        under, over = flag(z > 0), flag(z < levels - 1)
        at = [slice(t * LANES, (t + 1) * LANES) for t in range(tiles)]
        at_x = [slice(x * half, (x + 1) * half) for x in range(halves)]
        centre = [[src[z, i, j] for j in at] for i in at_x]
        down = [[pltpu.roll(c, 1, 0) for c in row] for row in centre]
        up = [[pltpu.roll(c, half - 1, 0) for c in row] for row in centre]
        for x in range(halves):
            fore = [pltpu.roll(c, 1, 1) for c in centre[x]]
            back = [pltpu.roll(c, LANES - 1, 1) for c in centre[x]]
            column = [ends[s, which, at_x[x]] for s in range(2)]
            enter = pltpu.roll(column[0], turn, 1)
            leave = pltpu.roll(column[1], lax.rem(turn + LANES - 1, LANES), 1)
            for t in range(tiles):
                before, after = zero, zero
                if x:
                    before = down[x - 1][t]
                elif which:
                    before = air_ref[z, at_x[x], at[t]] * has_top
                if x + 1 < halves:
                    after = up[x + 1][t]
                elif which:
                    after = air_ref[z, at_x[x], at[t]] * has_bottom
                total = src[below, at_x[x], at[t]] * under + src[above, at_x[x], at[t]] * over
                total = total + jnp.where(first_row, before, down[x][t])
                total = total + jnp.where(last_row, after, up[x][t])
                total = total + jnp.where(first_lane, fore[t - 1] if t else enter, fore[t])
                total = total + jnp.where(
                    last_lane, back[t + 1] if t + 1 < tiles else leave, back[t]
                )
                total = total + CENTRE * centre[x][t]
                dst[z, at_x[x], at[t]] = SQUARE * total if which else total

    def first_step(z, carry):
        stencil(z, air_ref, once, 0)
        return carry

    def second_step(z, carry):
        stencil(z, once, twice, 1)
        return carry

    writes = []

    def write(k):
        c = pltpu.make_async_copy(
            twice.at[pl.ds(k * chunk, chunk)], air_out.at[pl.ds(k * chunk, chunk)], out_sem.at[k]
        )
        c.start()
        writes.append(c)

    lax.fori_loop(0, levels, first_step, 0, unroll=UNROLL)
    for k in range(chunks):
        lax.fori_loop(k * chunk, (k + 1) * chunk, second_step, 0, unroll=UNROLL)
        if k:
            write(k)

    blocks = []
    for r in range(row_blocks):
        picked = []
        for k in range(nonzero):
            c = cols_ref[r, k]
            owner = c // visible
            picked.append(pieces[jnp.bitwise_xor(owner, blk) * visible + (c - owner * visible)])
        blocks.append(
            lax.dot_general(
                jnp.concatenate(picked, axis=1),
                jnp.concatenate([view_ref[r, k] for k in range(nonzero)], axis=1),
                (((1,), (1,)), ((), ())),
                preferred_element_type=F32,
            )
        )
    irradiance = jnp.concatenate(blocks, axis=1)

    ground = jnp.concatenate([air_ref[0, :, t * LANES : (t + 1) * LANES] for t in range(tiles)], axis=0)
    cell = cell_ref[...]
    patches = cell.shape[1]
    x_of, y_of = cell // width, cell % width
    high = (y_of // LANES) * depth + x_of
    low = y_of % LANES
    spots = iota((LANES, patches), 0)
    at_low = jnp.where(spots == low, 1.0, 0.0).astype(BF16)
    at_high = spots == high
    picked = sum(
        jnp.dot(piece, at_low, preferred_element_type=F32) for piece in split(ground, 3)
    )
    air_cell = jnp.sum(jnp.where(at_high, picked, 0.0), axis=0, keepdims=True)
    temp = temp_ref[...]
    squared = temp * temp
    emission = weight_ref[...] * (emissivity_ref[...] * (squared * squared))
    albedo = reflectance_ref[...].astype(F32)
    radiosity_out[...] = emission + albedo * irradiance
    absorbed = jnp.sum((1.0 - albedo) * irradiance, axis=0, keepdims=True)
    emitted = jnp.sum(emission, axis=0, keepdims=True)
    surface = temp + GAIN * (absorbed - emitted) - COUPLE * (temp - 1.0 - air_cell)
    surface_buf[...] = surface
    surface_copy = pltpu.make_async_copy(surface_buf.at[0], surface_out, surface_sem)
    surface_copy.start()
    writes.append(surface_copy)
    flux = HEAT * (COUPLE * (surface - 1.0 - air_cell))
    source = sum(
        lax.dot_general(
            jnp.where(at_high, piece.astype(F32), 0.0).astype(BF16),
            at_low,
            (((1,), (1,)), ((), ())),
            preferred_element_type=F32,
        )
        for piece in split(flux, 3)
    )
    for t in range(tiles):
        at = slice(t * LANES, (t + 1) * LANES)
        twice[0, :, at] = twice[0, :, at] + source[t * depth : (t + 1) * depth]
    write(0)
    for i, x in enumerate((0, 1, depth - 2, depth - 1)):
        c = pltpu.make_async_copy(twice.at[:, x, :], edge_out.at[i], edge_sem.at[i])
        c.start()
        writes.append(c)
    for c in writes:
        c.wait()


UNROLL = 4


def main(cols, weight, own, one, two, three, reflectance, emissivity, temp, cell, view, air):
    levels, depth, width = air.shape
    chunk = levels // 4
    bands, patches = reflectance.shape
    visible = own.shape[0] - 6
    return pl.pallas_call(
        functools.partial(main_kernel, chunk=chunk),
        out_shape=(
            jax.ShapeDtypeStruct((bands, patches), F32),
            jax.ShapeDtypeStruct((patches,), F32),
            jax.ShapeDtypeStruct(air.shape, F32),
            jax.ShapeDtypeStruct((4, levels, width), F32),
        ),
        in_specs=[pl.BlockSpec(memory_space=SMEM)] + [WHOLE] * 11,
        out_specs=(WHOLE, PLACE, PLACE, WHOLE),
        scratch_shapes=[
            VMEM(air.shape, F32),
            VMEM(air.shape, F32),
            VMEM((4 * visible, 16, LANES), BF16),
            VMEM((2, 2, depth, LANES), F32),
            VMEM((1, patches), F32),
            DMA((levels // chunk,)),
            DMA((4,)),
            DMA,
        ],
        compiler_params=params(32),
        cost_estimate=cost(MAIN_COST),
        name="main",
    )(cols, weight, own, one, two, three, reflectance, emissivity, temp, cell, view, air)


def finish_kernel(air_ref, edge_ref, near_ref, far_ref, out_ref, slabs, sem):
    del air_ref
    levels, width = near_ref.shape[1], near_ref.shape[2]
    depth = out_ref.shape[1]
    tiles = width // LANES
    odd = lax.rem(lax.axis_index("district"), 2)
    copies = []
    for side in range(2):
        use_near = (odd == 1) if side == 0 else (odd == 0)

        def received(k, i):
            at = slice(i * LANES, (i + 1) * LANES)
            return jnp.where(use_near, near_ref[k, :, at].astype(F32), far_ref[k, :, at].astype(F32))

        outer, inner = (0, 1) if side == 0 else (3, 2)
        for i, (c, around) in enumerate(plane_neighbours(functools.partial(received, 0), tiles)):
            at = slice(i * LANES, (i + 1) * LANES)
            reach = (2.0 * CENTRE) * c + 2.0 * around + received(1, i)
            slabs[outer, :, at] = edge_ref[outer, :, at] + SQUARE * reach
            slabs[inner, :, at] = edge_ref[inner, :, at] + SQUARE * c
        for i in (outer, inner):
            x = (0, 1, depth - 2, depth - 1)[i]
            c = pltpu.make_async_copy(slabs.at[i], out_ref.at[:, x, :], sem.at[i])
            c.start()
            copies.append(c)
    for c in copies:
        c.wait()


def finish(air, edge, near, far):
    return pl.pallas_call(
        finish_kernel,
        out_shape=jax.ShapeDtypeStruct(air.shape, F32),
        in_specs=[PLACE, WHOLE, WHOLE, WHOLE],
        out_specs=PLACE,
        scratch_shapes=[VMEM(edge.shape, F32), DMA((4,))],
        input_output_aliases={0: 0},
        compiler_params=params(8),
        name="finish",
    )(in_hbm(air), edge, near, far)


def swap(value, axis, pairs):
    return lax.ppermute(value, axis, [p for a, b in pairs for p in ((a, b), (b, a))])


def body(
    view_factor,
    view_cols,
    border_list,
    radiosity,
    reflectance,
    emissivity,
    band_weight,
    surface_temp,
    patch_cell,
    air,
):
    districts, blks = lax.axis_size("district"), lax.axis_size("blk")
    near_pairs = [(i, i + 1) for i in range(0, districts - 1, 2)]
    far_pairs = [(i, i + 1) for i in range(1, districts - 1, 2)]
    near_small, far_small, own = pack(border_list, radiosity, air)
    near_rows, far_rows = rows(air)
    near_small = swap(near_small, "district", near_pairs)
    far_small = swap(far_small, "district", far_pairs)
    near_rows = swap(near_rows, "district", near_pairs)
    own, far_rows = join(own, near_small, far_small, far_rows)
    far_rows = swap(far_rows, "district", far_pairs)
    one, two, three = (
        swap(own, "blk", [(i, i ^ k) for i in range(blks) if i < i ^ k]) for k in (1, 2, 3)
    )
    radiosity_next, surface_next, air_next, edge = main(
        view_cols,
        band_weight.reshape(-1, 1),
        own,
        one,
        two,
        three,
        reflectance,
        emissivity.reshape(1, -1),
        surface_temp.reshape(1, -1),
        patch_cell.reshape(1, -1),
        view_factor,
        air,
    )
    air_next = finish(air_next, edge, near_rows, far_rows)
    return radiosity_next, surface_next, air_next


def solution(mesh):
    in_specs = (
        P(("district", "blk"), None, None, None),
        P(("district", "blk"), None),
        P(("district", "blk")),
        P(None, ("district", "blk")),
        P(None, ("district", "blk")),
        P(("district", "blk")),
        P(),
        P(("district", "blk")),
        P(("district", "blk")),
        P(None, "district", "blk"),
    )
    out_specs = (P(None, ("district", "blk")), P(("district", "blk")), P(None, "district", "blk"))
    return jax.shard_map(body, mesh=mesh, in_specs=in_specs, out_specs=out_specs, check_vma=False)
```

time: 134 us -> 38.3 us (0.29)
  other arithmetic: 46.2 us -> 0 us
  local copies, waits for them, and re-layouts: 40.5 us -> 4.64 us
  starting transfers between devices: 29 us -> 12.3 us
  Pallas kernels: 0 us -> 16.3 us
  blocking collectives: 7.24 us -> 0 us
  matrix products: 3.21 us -> 0 us
  waiting for transfers between devices: 5.47 us -> 4 us
    add x2 -> x0, other arithmetic: 31.9 us -> none  [stencil_step(): return center + KAPPA * (beside_all - 6.0 * center)]
    concatenate x2 -> x0, local copies, waits for them, and re-layouts: 17.8 us -> none  [extended(): block = jnp.concatenate([low, block, high], axis=dim)]
    ppermute x10 -> x7, starting transfers between devices: 29 us -> 12.3 us  [swap(): lax.ppermute(value, axis, [p for a, b in pairs for p in ((a, b), (b, a))])]
    pallas_call x0 -> x5, Pallas kernels: none -> 16.3 us  [the longest x1 11.6 us: main(): pl.pallas_call(functools.partial(main_kernel, chunk=chunk), out_shape=(ja...]
    all_gather x1 -> x0, blocking collectives: 7.24 us -> none  [body(): piece = lax.all_gather(visible, 'blk', axis=1, tiled=True)]
    gather x3 -> x0, local copies, waits for them, and re-layouts: 5.75 us -> none  [the longest x1 4.46 us: body(): air_cell = jnp.take(air[0].reshape(-1), patch_cell)]
    slice x10 -> x0, local copies, waits for them, and re-layouts: 5.16 us -> none  [the longest x5 3.94 us: extended(): lax.slice_in_dim(block, block.shape[dim] - width, None, axis=dim)]
    scatter-add x2 -> x0, other arithmetic: 4.63 us -> none  [the longest x1 4.61 us: body(): jnp.zeros((air.shape[1] * air.shape[2],), jnp.float32).at[patch_cell]]
  transfers between devices with their start and end apart: 10 -> 7, of which waited for: 2 -> 2; matrix products, arithmetic and copies ran while one was open for 17% -> 0% of each run, Pallas kernels for 0% -> 35%
where the time goes in v1:
time: 38.3 us; the launch traced here: 38 us
  Pallas kernels  16.3 us (43%)
  starting transfers between devices  12.3 us (32%)
  local copies, waits for them, and re-layouts  4.64 us (12%)
  waiting for transfers between devices  4 us (10%)
  between operations  0.82 us (2%)
    ppermute x7, starting transfers between devices, swap(): lax.ppermute(value, axis, [p for a, b in pairs for p in ((a, b), (b, a))])  12.3 us
    pallas_call x1, Pallas kernels, main(): pl.pallas_call(functools.partial(main_kernel, chunk=chunk), out_shape=(ja...  11.6 us
    unnamed x16, local copies, waits for them, and re-layouts  4.54 us
    ppermute x7, waiting for transfers between devices, swap(): lax.ppermute(value, axis, [p for a, b in pairs for p in ((a, b), (b, a))])  4 us
    pallas_call x1, Pallas kernels, rows(): pl.pallas_call(rows_kernel, out_shape=(out, out), in_specs=[PLACE], out_s...  1.74 us
    pallas_call x1, Pallas kernels, pack(): pl.pallas_call(pack_kernel, out_shape=(small, small, own), in_specs=[PLAC...  1.57 us
    pallas_call x1, Pallas kernels, finish(): pl.pallas_call(finish_kernel, out_shape=jax.ShapeDtypeStruct(air.shape, F...  1.35 us
  transfers between devices with their start and end apart: 7, of which 2 were waited for; matrix products, arithmetic and copies ran while one was open for 0% of the time, Pallas kernels for 35%

profile of v1, /device:TPU:13, one launch (start us, length us, event | category | flops | bytes accessed | tf_op | source)
XLA Modules:
  0.0 38.0 jit_solution(11434697637352813211)
XLA Ops:
  0.6 0.0 copy-start.4
  0.6 0.0 copy-start.5
  0.7 0.0 copy-start.6
  0.7 0.0 copy-start.7
  0.7 0.0 copy-start.2
  0.7 0.0 copy-start.3
  0.7 1.6 %pack.1 = (bf16[4,16,128]{2,1,0:T(8,128)(2,1)S(1)}, bf16[4,16,128]{2,1,0:T(8,128)(2,1)S(1)}, bf16[10,16,128]{2,1,0:T(8,128)(2,1)S(1)}) custom-call(s32[3]{0:T(128)} %border_ref.1, bf16[16,768]{1,0:T(8,128)(2,1)} %radiosity_ref.1, f32[64,16,1024]{2,1,0:T(8,128)} %air_ref.5), custom_call_target="tpu_custom_call" | custom-call | bytes 6000000 | tf_op jit(solution)/shard_map/pack/pallas_call | solution.py:140
  2.3 0.3 collective-permute-start
  2.6 4.2 %collective-permute-start.1 = (bf16[4,16,128]{2,1,0:T(8,128)(2,1)S(1)}, bf16[4,16,128]{2,1,0:T(8,128)(2,1)S(1)}, u32[]{:S(2)}, u32[]{:S(2)}) collective-permute-start(bf16[4,16,128]{2,1,0:T(8,128)(2,1)S(1)} %get-tuple-element.16), channel_id=1, source_target_pairs={{4,8},{8,4},{12,16},{16,12},{20,24},{24,20},{5,9},{9,5},{13,17},{1... | collective-permute-start | bytes 49160 | tf_op jit(solution)/shard_map/ppermute | solution.py:518
  6.7 1.7 %rows.1 = (bf16[2,64,1024]{2,1,0:T(8,128)(2,1)S(1)}, bf16[2,64,1024]{2,1,0:T(8,128)(2,1)S(1)}) custom-call(f32[64,16,1024]{2,1,0:T(8,128)} %air_ref.5), custom_call_target="tpu_custom_call" | custom-call | bytes 6000000 | tf_op jit(solution)/shard_map/rows/pallas_call | solution.py:186
  8.5 0.1 collective-permute-start.5
  8.6 0.0 collective-permute-done.near_ref
  8.6 0.0 collective-permute-done.1.far_ref
  8.6 4.4 %collective-permute-start.6 = (bf16[2,64,1024]{2,1,0:T(8,128)(2,1)S(1)}, bf16[2,64,1024]{2,1,0:T(8,128)(2,1)S(1)}, u32[]{:S(2)}, u32[]{:S(2)}) collective-permute-start(bf16[2,64,1024]{2,1,0:T(8,128)(2,1)S(1)} %get-tuple-element.24), channel_id=1, source_target_pairs={{4,8},{8,4},{12,16},{16,12},{20,24},{24,20},{5,9},{9,5},{13,17},{1... | collective-permute-start | bytes 786440 | tf_op jit(solution)/shard_map/ppermute | solution.py:518
  13.0 3.0 %collective-permute-start.4 = (bf16[18,16,128]{2,1,0:T(8,128)(2,1)S(1)}, bf16[18,16,128]{2,1,0:T(8,128)(2,1)S(1)}, u32[]{:S(2)}, u32[]{:S(2)}) collective-permute-start(bf16[18,16,128]{2,1,0:T(8,128)(2,1)S(1)} %get-tuple-element.18.own_ref), channel_id=1, source_target_pairs={{0,3},{3,0},{1,2},{2,1},{4,7},{7,4},{5,6},{6,5},{8,11},{11,8},{9,1... | collective-permute-start | bytes 221192 | tf_op jit(solution)/shard_map/ppermute | solution.py:518
  15.9 0.3 collective-permute-start.3
  16.2 0.2 collective-permute-start.2
  16.4 0.0 copy-done.4
  16.4 0.0 copy-done.5
  16.4 0.0 copy-done.6
  16.5 0.0 copy-done.7
  16.5 0.1 copy.14.weight_ref
  16.5 2.5 %collective-permute-done.4.three_ref = bf16[18,16,128]{2,1,0:T(8,128)(2,1)S(1)} collective-permute-done((bf16[18,16,128]{2,1,0:T(8,128)(2,1)S(1)}, bf16[18,16,128]{2,1,0:T(8,128)(2,1)S(1)}, u32[]{:S(2)}, u32[]{:S(2)}) %collective-permute-start.4) | collective-permute-done | bytes 73760 | tf_op jit(solution)/shard_map/ppermute | solution.py:518
  19.1 1.5 %collective-permute-done.3.two_ref = bf16[18,16,128]{2,1,0:T(8,128)(2,1)S(1)} collective-permute-done((bf16[18,16,128]{2,1,0:T(8,128)(2,1)S(1)}, bf16[18,16,128]{2,1,0:T(8,128)(2,1)S(1)}, u32[]{:S(2)}, u32[]{:S(2)}) %collective-permute-start.3) | collective-permute-done | bytes 73760 | tf_op jit(solution)/shard_map/ppermute | solution.py:518
  20.5 0.0 collective-permute-done.2.one_ref
  20.5 0.0 copy-done.2
  20.5 0.0 copy-done.3
  20.6 0.0 copy-start
  20.6 2.2 %copy-done = f32[64,16,1024]{2,1,0:T(8,128)S(1)} copy-done((f32[64,16,1024]{2,1,0:T(8,128)S(1)}, f32[64,16,1024]{2,1,0:T(8,128)}, u32[]{:S(2)}) %copy-start) | copy-done | bytes 4194328
  22.7 0.0 copy-start.1
  22.7 2.3 %copy-done.1 = bf16[6,24,128,128]{3,2,1,0:T(8,128)(2,1)S(1)} copy-done((bf16[6,24,128,128]{3,2,1,0:T(8,128)(2,1)S(1)}, bf16[6,24,128,128]{3,2,1,0:T(8,128)(2,1)}, u32[]{:S(2)}) %copy-start.1) | copy-done | bytes 4718616
  25.1 11.6 %main.1 = (f32[16,768]{1,0:T(8,128)}, f32[768]{0:T(1024)}, f32[64,16,1024]{2,1,0:T(8,128)}, f32[4,64,1024]{2,1,0:T(8,128)S(1)}) custom-call(s32[6,24]{1,0:T(8,128)S(1)} %copy-done.3, f32[16,1]{1,0:T(8,128)S(1)} %copy.14.weight_ref, bf16[18,16,128]{2,1,0:T(8,128)(2,1)S(1)} %get-tuple-element.18.own_ref, ...), custom_call_target="tpu_custom_call" | custom-call | bytes 24000000 | tf_op jit(solution)/shard_map/main/pallas_call | solution.py:449
  36.7 0.0 collective-permute-done.5.near_ref
  36.7 0.0 collective-permute-done.6.far_ref
  36.7 1.4 %finish.1 = f32[64,16,1024]{2,1,0:T(8,128)} custom-call(f32[64,16,1024]{2,1,0:T(8,128)} %get-tuple-element.21.air_ref, f32[4,64,1024]{2,1,0:T(8,128)S(1)} %get-tuple-element.22.edge_ref, bf16[2,64,1024]{2,1,0:T(8,128)(2,1)S(1)} %collective-permute-done.5.near_ref, bf16[2,64,1024]{2,1,0:T(8,128)(2,1)S(1)} %collective-permute-done.6.far_ref), custom_call_target="tpu_custom_call", output_to_operand_aliasing={{}: (0, {})} | custom-call | tf_op jit(solution)/shard_map/finish/pallas_call | solution.py:505
  (4 shorter events, 0.0 us)
Async XLA Ops:
  0.6 15.8 %copy-start.4 = (f32[768]{0:T(1024)S(1)}, f32[768]{0:T(1024)}, u32[]{:S(2)}) copy-start(f32[768]{0:T(1024)} %param.15) | copy-start | bytes 9220
  0.6 15.8 %copy-start.5 = (f32[768]{0:T(1024)S(1)}, f32[768]{0:T(1024)}, u32[]{:S(2)}) copy-start(f32[768]{0:T(1024)} %param.17) | copy-start | bytes 9220
  0.7 15.8 %copy-start.6 = (s32[768]{0:T(1024)S(1)}, s32[768]{0:T(1024)}, u32[]{:S(2)}) copy-start(s32[768]{0:T(1024)} %param.18) | copy-start | bytes 9220
  0.7 15.8 %copy-start.7 = (f32[16]{0:T(128)S(1)}, f32[16]{0:T(128)}, u32[]{:S(2)}) copy-start(f32[16]{0:T(128)} %param.16) | copy-start | bytes 196
  0.7 19.9 %copy-start.2 = (bf16[16,768]{1,0:T(8,128)(2,1)S(1)}, bf16[16,768]{1,0:T(8,128)(2,1)}, u32[]{:S(2)}) copy-start(bf16[16,768]{1,0:T(8,128)(2,1)} %reflectance_ref.1) | copy-start | bytes 73732
  0.7 19.9 %copy-start.3 = (s32[6,24]{1,0:T(8,128)S(1)}, s32[6,24]{1,0:T(8,128)}, u32[]{:S(2)}) copy-start(s32[6,24]{1,0:T(8,128)} %cols_ref.1) | copy-start | bytes 1732
  2.3 6.3 %collective-permute-start = (bf16[4,16,128]{2,1,0:T(8,128)(2,1)S(1)}, bf16[4,16,128]{2,1,0:T(8,128)(2,1)S(1)}, u32[]{:S(2)}, u32[]{:S(2)}) collective-permute-start(bf16[4,16,128]{2,1,0:T(8,128)(2,1)S(1)} %get-tuple-element.15), channel_id=1, source_target_pairs={{0,4},{4,0},{8,12},{12,8},{16,20},{20,16},{24,28},{28,24},{1,5},{5... | collective-permute-start | bytes 49160 | tf_op jit(solution)/shard_map/ppermute | solution.py:518
  2.6 6.0 %collective-permute-start.1 = (bf16[4,16,128]{2,1,0:T(8,128)(2,1)S(1)}, bf16[4,16,128]{2,1,0:T(8,128)(2,1)S(1)}, u32[]{:S(2)}, u32[]{:S(2)}) collective-permute-start(bf16[4,16,128]{2,1,0:T(8,128)(2,1)S(1)} %get-tuple-element.16), channel_id=1, source_target_pairs={{4,8},{8,4},{12,16},{16,12},{20,24},{24,20},{5,9},{9,5},{13,17},{1... | collective-permute-start | bytes 49160 | tf_op jit(solution)/shard_map/ppermute | solution.py:518
  8.5 28.2 %collective-permute-start.5 = (bf16[2,64,1024]{2,1,0:T(8,128)(2,1)S(1)}, bf16[2,64,1024]{2,1,0:T(8,128)(2,1)S(1)}, u32[]{:S(2)}, u32[]{:S(2)}) collective-permute-start(bf16[2,64,1024]{2,1,0:T(8,128)(2,1)S(1)} %get-tuple-element.23), channel_id=1, source_target_pairs={{0,4},{4,0},{8,12},{12,8},{16,20},{20,16},{24,28},{28,24},{1,5},{5... | collective-permute-start | bytes 786440 | tf_op jit(solution)/shard_map/ppermute | solution.py:518
  8.6 28.1 %collective-permute-start.6 = (bf16[2,64,1024]{2,1,0:T(8,128)(2,1)S(1)}, bf16[2,64,1024]{2,1,0:T(8,128)(2,1)S(1)}, u32[]{:S(2)}, u32[]{:S(2)}) collective-permute-start(bf16[2,64,1024]{2,1,0:T(8,128)(2,1)S(1)} %get-tuple-element.24), channel_id=1, source_target_pairs={{4,8},{8,4},{12,16},{16,12},{20,24},{24,20},{5,9},{9,5},{13,17},{1... | collective-permute-start | bytes 786440 | tf_op jit(solution)/shard_map/ppermute | solution.py:518
  13.0 6.1 %collective-permute-start.4 = (bf16[18,16,128]{2,1,0:T(8,128)(2,1)S(1)}, bf16[18,16,128]{2,1,0:T(8,128)(2,1)S(1)}, u32[]{:S(2)}, u32[]{:S(2)}) collective-permute-start(bf16[18,16,128]{2,1,0:T(8,128)(2,1)S(1)} %get-tuple-element.18.own_ref), channel_id=1, source_target_pairs={{0,3},{3,0},{1,2},{2,1},{4,7},{7,4},{5,6},{6,5},{8,11},{11,8},{9,1... | collective-permute-start | bytes 221192 | tf_op jit(solution)/shard_map/ppermute | solution.py:518
  15.9 4.6 %collective-permute-start.3 = (bf16[18,16,128]{2,1,0:T(8,128)(2,1)S(1)}, bf16[18,16,128]{2,1,0:T(8,128)(2,1)S(1)}, u32[]{:S(2)}, u32[]{:S(2)}) collective-permute-start(bf16[18,16,128]{2,1,0:T(8,128)(2,1)S(1)} %get-tuple-element.18.own_ref), channel_id=1, source_target_pairs={{0,2},{2,0},{1,3},{3,1},{4,6},{6,4},{5,7},{7,5},{8,10},{10,8},{9,1... | collective-permute-start | bytes 221192 | tf_op jit(solution)/shard_map/ppermute | solution.py:518
  16.2 4.4 %collective-permute-start.2 = (bf16[18,16,128]{2,1,0:T(8,128)(2,1)S(1)}, bf16[18,16,128]{2,1,0:T(8,128)(2,1)S(1)}, u32[]{:S(2)}, u32[]{:S(2)}) collective-permute-start(bf16[18,16,128]{2,1,0:T(8,128)(2,1)S(1)} %get-tuple-element.18.own_ref), channel_id=1, source_target_pairs={{0,1},{1,0},{2,3},{3,2},{4,5},{5,4},{6,7},{7,6},{8,9},{9,8},{10,11... | collective-permute-start | bytes 221192 | tf_op jit(solution)/shard_map/ppermute | solution.py:518
  20.6 2.2 %copy-start = (f32[64,16,1024]{2,1,0:T(8,128)S(1)}, f32[64,16,1024]{2,1,0:T(8,128)}, u32[]{:S(2)}) copy-start(f32[64,16,1024]{2,1,0:T(8,128)} %air_ref.5) | copy-start | bytes 12582916
  22.7 2.3 %copy-start.1 = (bf16[6,24,128,128]{3,2,1,0:T(8,128)(2,1)S(1)}, bf16[6,24,128,128]{3,2,1,0:T(8,128)(2,1)}, u32[]{:S(2)}) copy-start(bf16[6,24,128,128]{3,2,1,0:T(8,128)(2,1)} %view_ref.1) | copy-start | bytes 14155780

commit v2 on v1

v2 whole, which is shorter than its diff:
```python
import functools

import jax
import jax.numpy as jnp
from jax import lax
from jax.experimental import pallas as pl
from jax.experimental.pallas import tpu as pltpu
from jax.sharding import PartitionSpec as P

KAPPA = 0.15
GAIN = 0.02
COUPLE = 0.2
HEAT = 1.0
CENTRE = (1.0 - 6.0 * KAPPA) / KAPPA
SQUARE = KAPPA * KAPPA

F32 = jnp.float32
BF16 = jnp.bfloat16
LANES = 128
VMEM = pltpu.VMEM
SMEM = pltpu.SMEM
DMA = pltpu.SemaphoreType.DMA
PACK_COST, ROWS_COST, JOIN_COST, FIRST_COST, SECOND_COST, MAIN_COST = 2, 2, 1, 3, 3, 4


def params(mebibytes):
    return pltpu.CompilerParams(vmem_limit_bytes=mebibytes << 20)


def cost(microseconds):
    return pl.CostEstimate(flops=int(microseconds * 1_000_000_000), bytes_accessed=0, transcendentals=0)


def in_hbm(value):
    return pltpu.with_memory_space_constraint(value, pltpu.HBM)


WHOLE = pl.BlockSpec(memory_space=VMEM)
PLACE = pl.BlockSpec(memory_space=pl.ANY)


def iota(shape, axis):
    return lax.broadcasted_iota(jnp.int32, shape, axis)


def flag(condition):
    return jnp.where(condition, 1.0, 0.0).astype(F32)


def split(value, pieces):
    out = []
    for _ in range(pieces):
        piece = value.astype(BF16)
        out.append(piece)
        value = value - piece.astype(F32)
    return out


def plane_neighbours(load, tiles):
    centre = [load(i) for i in range(tiles)]
    rows = centre[0].shape[0]
    lane = iota((rows, LANES), 1)
    row = iota((rows, LANES), 0)
    right = [pltpu.roll(c, 1, 1) for c in centre]
    left = [pltpu.roll(c, LANES - 1, 1) for c in centre]
    zero = jnp.zeros((rows, LANES), F32)
    for i, c in enumerate(centre):
        total = jnp.where(lane == 0, right[i - 1] if i else zero, right[i])
        total = total + jnp.where(
            lane == LANES - 1, left[i + 1] if i + 1 < tiles else zero, left[i]
        )
        total = total + jnp.where(row == 0, 0.0, pltpu.roll(c, 1, 0))
        total = total + jnp.where(row == rows - 1, 0.0, pltpu.roll(c, rows - 1, 0))
        yield c, total


def pack_kernel(
    border_ref,
    radiosity_ref,
    air_ref,
    near_small,
    far_small,
    own_ref,
    border,
    blocks_of,
    ends,
    spread,
    sem,
    end_sem,
):
    levels, depth, width = air_ref.shape
    blocks = radiosity_ref.shape[1] // LANES
    borders = border_ref.shape[0]
    odd = lax.rem(lax.axis_index("district"), 2)
    first = [
        pltpu.make_async_copy(border_ref, border, sem.at[0]),
        pltpu.make_async_copy(radiosity_ref, blocks_of, sem.at[1]),
    ]
    edge = [
        pltpu.make_async_copy(
            air_ref.at[:, x, pl.ds(y, LANES)], ends.at[i, j], end_sem.at[i, j]
        )
        for i, x in enumerate((0, depth - 1))
        for j, y in enumerate((0, width - LANES))
    ]
    for c in first + edge:
        c.start()
    spread[...] = jnp.zeros(spread.shape, F32)
    for c in first:
        c.wait()
    for s in range(blocks):
        own_ref[s] = blocks_of[:, s * LANES : (s + 1) * LANES]
    for s in range(borders):
        tile = own_ref[border[s]]
        near_small[s] = tile
        far_small[s] = tile
    for c in edge:
        c.wait()
    lane = iota((levels, LANES), 1)
    sub = iota((16, LANES), 0)
    corner = []
    for i in range(2):
        spread[i, pl.ds(0, levels, 2), :] = jnp.where(lane < LANES // 2, ends[i, 0], ends[i, 1])
        turned = spread[i].T
        tile = jnp.zeros((16, LANES), F32)
        for n, row in enumerate((turned[0:1], turned[LANES - 1 : LANES])):
            high = row.astype(BF16).astype(F32)
            tile = jnp.where(sub == 2 * n, high, tile)
            tile = jnp.where(sub == 2 * n + 1, row - high, tile)
        corner.append(tile)
    near_small[borders] = jnp.where(odd == 0, corner[1], corner[0]).astype(BF16)
    far_small[borders] = jnp.where(odd == 0, corner[0], corner[1]).astype(BF16)


def pack(border_list, radiosity, air):
    levels = air.shape[0]
    blocks = radiosity.shape[1] // LANES
    borders = border_list.shape[0]
    small = jax.ShapeDtypeStruct((borders + 1, 16, LANES), BF16)
    own = jax.ShapeDtypeStruct((blocks, 16, LANES), BF16)
    return pl.pallas_call(
        pack_kernel,
        out_shape=(small, small, own),
        in_specs=[PLACE] * 3,
        out_specs=(WHOLE,) * 3,
        scratch_shapes=[
            SMEM(border_list.shape, border_list.dtype),
            VMEM(radiosity.shape, BF16),
            VMEM((2, 2, levels, LANES), F32),
            VMEM((2, LANES, LANES), F32),
            DMA((2,)),
            DMA((2, 2)),
        ],
        compiler_params=params(8),
        cost_estimate=cost(PACK_COST),
        name="pack",
    )(in_hbm(border_list), in_hbm(radiosity), in_hbm(air))


def rows_kernel(air_ref, after_ref, near_rows, far_rows, columns, slabs, ends, sem, end_sem):
    del after_ref
    levels, depth, width = air_ref.shape
    tiles = width // LANES
    odd = lax.rem(lax.axis_index("district"), 2)
    edge = [
        pltpu.make_async_copy(air_ref.at[:, :, pl.ds(y, LANES)], ends.at[j], end_sem.at[j])
        for j, y in enumerate((0, width - LANES))
    ]
    copies = [
        pltpu.make_async_copy(air_ref.at[:, r, :], slabs.at[i], sem.at[i])
        for i, r in enumerate((depth - 1, depth - 2, 0, 1))
    ]
    for c in edge + copies:
        c.start()
    place = iota((depth, LANES), 1) // 2
    for j in range(2):
        edge[j].wait()
        packed = jnp.zeros((depth, LANES), F32)
        for z in range(levels):
            tile = ends[j, z]
            turn = (2 * z + 2 * j) % LANES
            packed = jnp.where(place == z, pltpu.roll(tile, turn, 1) if turn else tile, packed)
        for n, piece in enumerate(split(packed, 2)):
            columns[2 * j + n] = piece
    for c in copies:
        c.wait()
    for which, rows in enumerate((near_rows, far_rows)):
        base = 2 * (odd if which == 0 else 1 - odd)

        def lost(i):
            value = slabs[base, :, i * LANES : (i + 1) * LANES]
            return value - value.astype(BF16).astype(F32)

        for i, (c, around) in enumerate(plane_neighbours(lost, tiles)):
            at = slice(i * LANES, (i + 1) * LANES)
            rows[0, :, at] = slabs[base, :, at].astype(BF16)
            rows[1, :, at] = (slabs[base + 1, :, at] + CENTRE * 2.0 * c + 2.0 * around).astype(BF16)


def rows(air, after):
    levels, depth, width = air.shape
    out = jax.ShapeDtypeStruct((2, levels, width), BF16)
    return pl.pallas_call(
        rows_kernel,
        out_shape=(out, out, jax.ShapeDtypeStruct((4, depth, LANES), BF16)),
        in_specs=[PLACE, PLACE],
        out_specs=(WHOLE,) * 3,
        scratch_shapes=[
            VMEM((4, levels, width), F32),
            VMEM((2, levels, depth, LANES), F32),
            DMA((4,)),
            DMA((2,)),
        ],
        compiler_params=params(8),
        cost_estimate=cost(ROWS_COST),
        name="rows",
    )(in_hbm(air), after)


def join_kernel(own_ref, columns_ref, near_ref, far_ref, out_ref):
    odd = lax.rem(lax.axis_index("district"), 2)
    borders = near_ref.shape[0] - 1
    blocks = own_ref.shape[0]
    for s in range(blocks):
        out_ref[s] = own_ref[s]
    for s in range(4):
        out_ref[blocks + 2 * borders + 2 + s] = columns_ref[s]
    for s in range(borders + 1):
        before = jnp.where(odd == 1, near_ref[s].astype(F32), far_ref[s].astype(F32)).astype(BF16)
        after = jnp.where(odd == 1, far_ref[s].astype(F32), near_ref[s].astype(F32)).astype(BF16)
        at = blocks + s if s < borders else blocks + 2 * borders
        out_ref[at] = before
        out_ref[at + (borders if s < borders else 1)] = after


def join(own, columns, near, far):
    count = own.shape[0] + columns.shape[0] + 2 * near.shape[0]
    return pl.pallas_call(
        join_kernel,
        out_shape=jax.ShapeDtypeStruct((count, 16, LANES), BF16),
        in_specs=[WHOLE] * 4,
        out_specs=WHOLE,
        compiler_params=params(8),
        cost_estimate=cost(JOIN_COST),
        name="join",
    )(own, columns, near, far)


def stack_kernel(one_ref, two_ref, out_ref):
    part = one_ref.shape[0]
    for s in range(part):
        out_ref[s] = one_ref[s]
        out_ref[part + s] = two_ref[s]


def stack(one, two):
    return pl.pallas_call(
        stack_kernel,
        out_shape=jax.ShapeDtypeStruct((2 * one.shape[0], 16, LANES), BF16),
        in_specs=[WHOLE] * 2,
        out_specs=WHOLE,
        compiler_params=params(8),
        cost_estimate=cost(JOIN_COST),
        name="stack",
    )(one, two)


def cell_masks(cell_ref, depth, width):
    patches = cell_ref.shape[0]
    cell = cell_ref[...].reshape(1, patches)
    x_of, y_of = cell // width, cell % width
    spots = iota((LANES, patches), 0)
    at_low = jnp.where(spots == y_of % LANES, 1.0, 0.0).astype(BF16)
    return at_low, spots == (y_of // LANES) * depth + x_of


def stencil_level(z, src, store, beyond):
    levels, depth, width = src.shape
    tiles = width // LANES
    half = depth // 2
    sub = iota((half, LANES), 0)
    lane = iota((half, LANES), 1)
    zero = jnp.zeros((half, LANES), F32)
    below, above = jnp.maximum(z - 1, 0), jnp.minimum(z + 1, levels - 1)
    under, over = flag(z > 0), flag(z < levels - 1)
    at = [slice(t * LANES, (t + 1) * LANES) for t in range(tiles)]
    at_x = [slice(x * half, (x + 1) * half) for x in range(2)]
    centre = [[src[z, i, j] for j in at] for i in at_x]
    for x in range(2):
        fore = [pltpu.roll(c, 1, 1) for c in centre[x]]
        back = [pltpu.roll(c, LANES - 1, 1) for c in centre[x]]
        for t in range(tiles):
            c = centre[x][t]
            before = pltpu.roll(centre[0][t], 1, 0) if x else beyond(0, t)
            after = beyond(1, t) if x else pltpu.roll(centre[1][t], half - 1, 0)
            total = src[below, at_x[x], at[t]] * under + src[above, at_x[x], at[t]] * over
            total = total + jnp.where(sub == 0, before, pltpu.roll(c, 1, 0))
            total = total + jnp.where(sub == half - 1, after, pltpu.roll(c, half - 1, 0))
            total = total + jnp.where(lane == 0, fore[t - 1] if t else zero, fore[t])
            total = total + jnp.where(
                lane == LANES - 1, back[t + 1] if t + 1 < tiles else zero, back[t]
            )
            store(x, t, total + CENTRE * c)


def first_kernel(air_ref, after_ref, once):
    del after_ref
    levels, depth, _ = air_ref.shape
    half = depth // 2
    zero = jnp.zeros((half, LANES), F32)

    def level(z, carry):
        def store(x, t, total):
            once[z, x * half : (x + 1) * half, t * LANES : (t + 1) * LANES] = total

        stencil_level(z, air_ref, store, lambda x, t: zero)
        return carry

    lax.fori_loop(0, levels, level, 0, unroll=8)


def first(air, after):
    return pl.pallas_call(
        first_kernel,
        out_shape=jax.ShapeDtypeStruct(air.shape, F32),
        in_specs=[WHOLE, PLACE],
        out_specs=WHOLE,
        compiler_params=params(12),
        cost_estimate=cost(FIRST_COST),
        name="first",
    )(air, after)


def second_kernel(
    air_ref,
    once,
    cell_ref,
    air_out,
    ground_out,
    sides_out,
    edge_out,
    cell_out,
    result,
    out_sem,
    edge_sem,
    *,
    chunk,
):
    levels, depth, width = once.shape
    tiles = width // LANES
    half = depth // 2
    district = lax.axis_index("district")
    has_top, has_bottom = flag(district > 0), flag(district < lax.axis_size("district") - 1)
    at = [slice(t * LANES, (t + 1) * LANES) for t in range(tiles)]
    at_x = [slice(x * half, (x + 1) * half) for x in range(2)]

    def level(z, carry):
        def beyond(x, t):
            return air_ref[z, at_x[x], at[t]] * (has_bottom if x else has_top)

        def store(x, t, total):
            total = SQUARE * total
            result[z, at_x[x], at[t]] = total
            if t in (0, tiles - 1):
                sides_out[0 if t == 0 else 1, z, at_x[x]] = total

        stencil_level(z, once, store, beyond)
        return carry

    writes = []
    for k in range(levels // chunk):
        lax.fori_loop(k * chunk, (k + 1) * chunk, level, 0, unroll=8)
        span = pl.ds(k * chunk, chunk)
        lanes = pl.ds(LANES, width - 2 * LANES)
        fresh = [
            pltpu.make_async_copy(
                result.at[span, :, lanes], air_out.at[span, :, lanes], out_sem.at[k]
            )
        ]
        for i, x in enumerate((0, 1, depth - 2, depth - 1)):
            fresh.append(
                pltpu.make_async_copy(
                    result.at[span, x, lanes], edge_out.at[i, span], edge_sem.at[k, i]
                )
            )
        for c in fresh:
            c.start()
        writes += fresh
    ground_out[...] = result[0]
    at_low, at_high = cell_masks(cell_ref, depth, width)
    ground = jnp.concatenate([air_ref[0, :, j] for j in at], axis=0)
    picked = sum(
        jnp.dot(piece, at_low, preferred_element_type=F32) for piece in split(ground, 3)
    )
    cell_out[...] = jnp.sum(jnp.where(at_high, picked, 0.0), axis=0, keepdims=True)
    for c in writes:
        c.wait()


def second(air, once, cell):
    levels, depth, width = air.shape
    chunk = levels // 8
    return pl.pallas_call(
        functools.partial(second_kernel, chunk=chunk),
        out_shape=(
            jax.ShapeDtypeStruct(air.shape, F32),
            jax.ShapeDtypeStruct((depth, width), F32),
            jax.ShapeDtypeStruct((2, levels, depth, LANES), F32),
            jax.ShapeDtypeStruct((4, levels, width - 2 * LANES), F32),
            jax.ShapeDtypeStruct((1, cell.shape[0]), F32),
        ),
        in_specs=[WHOLE] * 3,
        out_specs=(PLACE,) + (WHOLE,) * 4,
        scratch_shapes=[VMEM(air.shape, F32), DMA((levels // chunk,)), DMA((levels // chunk, 4))],
        compiler_params=params(20),
        cost_estimate=cost(SECOND_COST),
        name="second",
    )(air, once, cell)


def main_kernel(
    cols_ref,
    weight_ref,
    mine_ref,
    theirs_ref,
    reflectance_ref,
    emissivity_ref,
    temp_ref,
    cell_ref,
    view_ref,
    air_cell_ref,
    ground_ref,
    sides_ref,
    next_ref,
    radiosity_out,
    surface_out,
    air_out,
    side_edge_out,
    source_out,
    ground_out,
    sides,
    pieces,
    radiosity_buf,
    surface_buf,
    out_sem,
    edge_sem,
    surface_sem,
):
    del next_ref
    levels, depth = sides_ref.shape[1:3]
    width = ground_ref.shape[1]
    tiles = width // LANES
    row_blocks, nonzero = view_ref.shape[0], view_ref.shape[1]
    blk = lax.axis_index("blk")
    blks = lax.axis_size("blk")
    has_left, has_right = flag(blk > 0), flag(blk < blks - 1)
    part = mine_ref.shape[0] // 2
    visible = part - 6
    for n, (ref, base) in enumerate(
        ((mine_ref, 0), (theirs_ref, 0), (mine_ref, part), (theirs_ref, part))
    ):
        for s in range(visible):
            pieces[n * visible + s] = ref[base + s]

    writes = []
    even = lax.rem(blk, 2) == 0

    def pair(ref, at):
        return ref[at].astype(F32) + ref[at + 1].astype(F32)

    def received(load):
        one, three = load(0), load(part)
        return jnp.where(even, three, one) * has_left, jnp.where(even, one, three) * has_right

    columns = [received(lambda base, n=n: pair(theirs_ref, base + visible + 2 + n)) for n in (0, 2)]
    corners = [received(lambda base, n=n: theirs_ref[base + visible + n].astype(F32)) for n in (0, 1)]
    sub = iota((depth, LANES), 0)
    lane = iota((depth, LANES), 1)
    half = depth // 2
    beside = []
    for side in range(2):
        k = 2 if side == 0 else 0
        shift = LANES - 1 if side == 0 else 0
        turn = lambda v: pltpu.roll(v, shift, 1) if shift else v
        near = turn(columns[1 - side][side])
        beyond = columns[1][0] if side == 0 else pltpu.roll(columns[0][1], LANES - 1, 1)
        own = pair(mine_ref, visible + 2 + 2 * side)
        own = own if side == 0 else pltpu.roll(own, LANES - 1, 1)
        top, bottom = (c[side][k : k + 1] + c[side][k + 1 : k + 2] for c in corners)
        around = jnp.where(sub == 0, top, pltpu.roll(near, 1, 0))
        around = around + jnp.where(sub == depth - 1, bottom, pltpu.roll(near, depth - 1, 0))
        around = around + jnp.where(lane < 2, 0.0, pltpu.roll(near, 2, 1))
        around = around + jnp.where(lane >= 2 * levels - 2, 0.0, pltpu.roll(near, LANES - 2, 1))
        outer = 2.0 * CENTRE * near + 2.0 * around + beyond + own * (has_right if side else has_left)
        if side == 0:
            value = jnp.where(lane % 2 == 0, outer, pltpu.roll(near, 1, 1))
        else:
            value = jnp.where(lane % 2 == 0, near, pltpu.roll(outer, 1, 1))
        beside.append(SQUARE * value)

    lane8 = iota((half, LANES), 1)
    both = [lane8 < 2, lane8 >= LANES - 2]

    def edges(z, carry):
        for side in range(2):
            turn = lax.rem(2 * LANES - 2 * z - 2 * side, LANES)
            for x in range(2):
                at = slice(x * half, (x + 1) * half)
                value = pltpu.roll(beside[side][at], turn, 1)
                sides[side, z, at] = sides_ref[side, z, at] + jnp.where(both[side], value, 0.0)
        return carry

    lax.fori_loop(0, levels, edges, 0, unroll=8)
    for side in range(2):
        lanes = pl.ds(side * (width - LANES), LANES)
        c = pltpu.make_async_copy(
            sides.at[side, pl.ds(1, levels - 1)],
            air_out.at[pl.ds(1, levels - 1), :, lanes],
            out_sem.at[side],
        )
        c.start()
        writes.append(c)
        for i, x in enumerate((0, 1, depth - 2, depth - 1)):
            c = pltpu.make_async_copy(
                sides.at[side, :, x, :], side_edge_out.at[side, i], edge_sem.at[side, i]
            )
            c.start()
            writes.append(c)
    blocks = []
    for r in range(row_blocks):
        picked = []
        for k in range(nonzero):
            c = cols_ref[r, k]
            owner = c // visible
            picked.append(pieces[jnp.bitwise_xor(owner, blk) * visible + (c - owner * visible)])
        blocks.append(
            lax.dot_general(
                jnp.concatenate(picked, axis=1),
                jnp.concatenate([view_ref[r, k] for k in range(nonzero)], axis=1),
                (((1,), (1,)), ((), ())),
                preferred_element_type=F32,
            )
        )
    irradiance = jnp.concatenate(blocks, axis=1)

    patches = cell_ref.shape[0]
    at_low, at_high = cell_masks(cell_ref, depth, width)
    air_cell = air_cell_ref[...]
    temp = temp_ref[...].reshape(1, patches)
    squared = temp * temp
    bands = reflectance_ref.shape[0]
    weight = jnp.zeros((bands, LANES), F32)
    for n in range(bands):
        weight = jnp.where(iota((bands, LANES), 0) == n, weight_ref[n], weight)
    weight = jnp.concatenate([weight] * (patches // LANES), axis=1)
    emission = weight * (emissivity_ref[...].reshape(1, patches) * (squared * squared))
    albedo = reflectance_ref[...].astype(F32)
    radiosity_buf[...] = emission + albedo * irradiance
    c = pltpu.make_async_copy(radiosity_buf, radiosity_out, surface_sem.at[1])
    c.start()
    writes.append(c)
    absorbed = jnp.sum((1.0 - albedo) * irradiance, axis=0, keepdims=True)
    emitted = jnp.sum(emission, axis=0, keepdims=True)
    surface = temp + GAIN * (absorbed - emitted) - COUPLE * (temp - 1.0 - air_cell)
    surface_buf[...] = surface
    c = pltpu.make_async_copy(surface_buf.at[0], surface_out, surface_sem.at[0])
    c.start()
    writes.append(c)
    flux = HEAT * (COUPLE * (surface - 1.0 - air_cell))
    source = sum(
        lax.dot_general(
            jnp.where(at_high, piece.astype(F32), 0.0).astype(BF16),
            at_low,
            (((1,), (1,)), ((), ())),
            preferred_element_type=F32,
        )
        for piece in split(flux, 3)
    )

    for t in range(tiles):
        at = slice(t * LANES, (t + 1) * LANES)
        here = source[t * depth : (t + 1) * depth]
        before = sides[0 if t == 0 else 1, 0] if t in (0, tiles - 1) else ground_ref[:, at]
        ground_out[:, at] = before + here
        for i, x in enumerate((0, 1, depth - 2, depth - 1)):
            source_out[i : i + 1, at] = here[x : x + 1]
    for c in writes:
        c.wait()


def main(
    cols, weight, mine, theirs, reflectance, emissivity, temp, cell, view, air_cell, ground, sides, following
):
    levels, depth = sides.shape[1:3]
    width = ground.shape[1]
    bands, patches = reflectance.shape
    visible = mine.shape[0] // 2 - 6
    return pl.pallas_call(
        main_kernel,
        out_shape=(
            jax.ShapeDtypeStruct((bands, patches), F32),
            jax.ShapeDtypeStruct((patches,), F32),
            jax.ShapeDtypeStruct(following.shape, F32),
            jax.ShapeDtypeStruct((2, 4, levels, LANES), F32),
            jax.ShapeDtypeStruct((4, width), F32),
            jax.ShapeDtypeStruct((depth, width), F32),
        ),
        in_specs=[pl.BlockSpec(memory_space=SMEM)] * 2 + [WHOLE] * 10 + [PLACE],
        out_specs=(PLACE, PLACE, PLACE, WHOLE, WHOLE, WHOLE),
        scratch_shapes=[
            VMEM(sides.shape, F32),
            VMEM((4 * visible, 16, LANES), BF16),
            VMEM((bands, patches), F32),
            VMEM((1, patches), F32),
            DMA((2,)),
            DMA((2, 4)),
            DMA((2,)),
        ],
        input_output_aliases={12: 2},
        compiler_params=params(20),
        cost_estimate=cost(MAIN_COST),
        name="main",
    )(
        cols,
        weight,
        mine,
        theirs,
        reflectance,
        emissivity,
        temp,
        cell,
        view,
        air_cell,
        ground,
        sides,
        in_hbm(following),
    )


def finish_kernel(
    air_ref, edge_ref, side_ref, source_ref, ground_ref, near_ref, far_ref, out_ref, slabs, sem
):
    del air_ref
    levels, width = near_ref.shape[1], near_ref.shape[2]
    depth = out_ref.shape[1]
    tiles = width // LANES
    odd = lax.rem(lax.axis_index("district"), 2)
    ground = iota((levels, LANES), 0) == 0
    copies = [
        pltpu.make_async_copy(ground_ref.at[x], out_ref.at[0, x], sem.at[2 + x])
        for x in range(2, depth - 2)
    ]
    for c in copies:
        c.start()
    for side in range(2):
        use_near = (odd == 1) if side == 0 else (odd == 0)

        def received(k, i):
            at = slice(i * LANES, (i + 1) * LANES)
            return jnp.where(use_near, near_ref[k, :, at].astype(F32), far_ref[k, :, at].astype(F32))

        def base(n, i):
            if i in (0, tiles - 1):
                value = side_ref[0 if i == 0 else 1, n]
            else:
                value = edge_ref[n, :, (i - 1) * LANES : i * LANES]
            return value + jnp.where(ground, source_ref[n : n + 1, i * LANES : (i + 1) * LANES], 0.0)

        outer, inner = (0, 1) if side == 0 else (3, 2)
        for i, (c, around) in enumerate(plane_neighbours(functools.partial(received, 0), tiles)):
            at = slice(i * LANES, (i + 1) * LANES)
            reach = (2.0 * CENTRE) * c + 2.0 * around + received(1, i)
            slabs[outer, :, at] = base(outer, i) + SQUARE * reach
            slabs[inner, :, at] = base(inner, i) + SQUARE * c
        for i in (outer, inner):
            x = (0, 1, depth - 2, depth - 1)[i]
            c = pltpu.make_async_copy(slabs.at[i], out_ref.at[:, x, :], sem.at[i])
            c.start()
            copies.append(c)
    for c in copies:
        c.wait()


def finish(air, edge, side, source, ground, near, far):
    levels, width = near.shape[1:]
    return pl.pallas_call(
        finish_kernel,
        out_shape=jax.ShapeDtypeStruct(air.shape, F32),
        in_specs=[PLACE] + [WHOLE] * 6,
        out_specs=PLACE,
        scratch_shapes=[VMEM((4, levels, width), F32), DMA((air.shape[1],))],
        input_output_aliases={0: 0},
        compiler_params=params(8),
        name="finish",
    )(in_hbm(air), edge, side, source, ground, near, far)


def swap(value, axis, pairs):
    return lax.ppermute(value, axis, [p for a, b in pairs for p in ((a, b), (b, a))])


def body(
    view_factor,
    view_cols,
    border_list,
    radiosity,
    reflectance,
    emissivity,
    band_weight,
    surface_temp,
    patch_cell,
    air,
):
    districts, blks = lax.axis_size("district"), lax.axis_size("blk")
    near_pairs = [(i, i + 1) for i in range(0, districts - 1, 2)]
    far_pairs = [(i, i + 1) for i in range(1, districts - 1, 2)]
    near_small, far_small, own = pack(border_list, radiosity, air)
    near_rows, far_rows, columns = rows(air, own)
    near_small = swap(near_small, "district", near_pairs)
    far_small = swap(far_small, "district", far_pairs)
    near_rows = swap(near_rows, "district", near_pairs)
    far_rows = swap(far_rows, "district", far_pairs)
    once = first(air, own)
    following, ground, sides, edge, air_cell = second(air, once, patch_cell)
    own = join(own, columns, near_small, far_small)
    across = swap(own, "blk", [(i, i ^ 2) for i in range(blks) if i < i ^ 2])
    mine = stack(own, across)
    theirs = swap(mine, "blk", [(i, i ^ 1) for i in range(blks) if i < i ^ 1])
    radiosity_next, surface_next, air_next, side, source, ground = main(
        view_cols,
        band_weight,
        mine,
        theirs,
        reflectance,
        emissivity,
        surface_temp,
        patch_cell,
        view_factor,
        air_cell,
        ground,
        sides,
        following,
    )
    air_next = finish(air_next, edge, side, source, ground, near_rows, far_rows)
    return radiosity_next, surface_next, air_next


def solution(mesh):
    in_specs = (
        P(("district", "blk"), None, None, None),
        P(("district", "blk"), None),
        P(("district", "blk")),
        P(None, ("district", "blk")),
        P(None, ("district", "blk")),
        P(("district", "blk")),
        P(),
        P(("district", "blk")),
        P(("district", "blk")),
        P(None, "district", "blk"),
    )
    out_specs = (P(None, ("district", "blk")), P(("district", "blk")), P(None, "district", "blk"))
    return jax.shard_map(body, mesh=mesh, in_specs=in_specs, out_specs=out_specs, check_vma=False)
```

time: 38.3 us -> 29.8 us (0.78)
  local copies, waits for them, and re-layouts: 4.64 us -> 0.06 us
  waiting for transfers between devices: 4 us -> 0.02 us
    unnamed x16 -> x18, local copies, waits for them, and re-layouts: 4.54 us -> 0.06 us
    ppermute x7 -> x6, waiting for transfers between devices: 4 us -> 0.02 us  [swap(): lax.ppermute(value, axis, [p for a, b in pairs for p in ((a, b), (b, a))])]
    pallas_call x1, Pallas kernels: 1.57 us -> 1.01 us  [pack(): pl.pallas_call(pack_kernel, out_shape=(small, small, own), in_specs=[PLAC...]
    pallas_call x3 -> x6, Pallas kernels: 13.3 us -> 13.8 us  [the longest x1 4.67 us: second(): pl.pallas_call(functools.partial(second_kernel, chunk=chunk), out_shape=(...]
    ppermute x7 -> x6, starting transfers between devices: 12.3 us -> 12.3 us  [swap(): lax.ppermute(value, axis, [p for a, b in pairs for p in ((a, b), (b, a))])]
  transfers between devices with their start and end apart: 7 -> 6, of which waited for: 2 -> 0; matrix products, arithmetic and copies ran while one was open for 0% -> 0% of each run, Pallas kernels for 35% -> 47%
where the time goes in v2:
time: 29.8 us; the launch traced here: 29.5 us
  Pallas kernels  16.3 us (55%)
  starting transfers between devices  12.3 us (41%)
  between operations  0.89 us (3%)
    ppermute x6, starting transfers between devices, swap(): lax.ppermute(value, axis, [p for a, b in pairs for p in ((a, b), (b, a))])  12.3 us
    pallas_call x1, Pallas kernels, second(): pl.pallas_call(functools.partial(second_kernel, chunk=chunk), out_shape=(...  4.67 us
    pallas_call x1, Pallas kernels, main(): pl.pallas_call(main_kernel, out_shape=(jax.ShapeDtypeStruct((bands, patch...  4.02 us
    pallas_call x1, Pallas kernels, first(): pl.pallas_call(first_kernel, out_shape=jax.ShapeDtypeStruct(air.shape, F3...  2.81 us
    pallas_call x1, Pallas kernels, rows(): pl.pallas_call(rows_kernel, out_shape=(out, out, jax.ShapeDtypeStruct((4,...  2.23 us
    pallas_call x1, Pallas kernels, finish(): pl.pallas_call(finish_kernel, out_shape=jax.ShapeDtypeStruct(air.shape, F...  1.5 us
    pallas_call x1, Pallas kernels, pack(): pl.pallas_call(pack_kernel, out_shape=(small, small, own), in_specs=[PLAC...  1.01 us
  transfers between devices with their start and end apart: 6, of which 0 were waited for; matrix products, arithmetic and copies ran while one was open for 0% of the time, Pallas kernels for 47%

profile of v2, /device:TPU:13, one launch (start us, length us, event | category | flops | bytes accessed | tf_op | source)
XLA Modules:
  0.0 29.5 jit_solution(2068299737091541607)
XLA Ops:
  0.6 1.0 %pack.1 = (bf16[4,16,128]{2,1,0:T(8,128)(2,1)S(1)}, bf16[4,16,128]{2,1,0:T(8,128)(2,1)S(1)}, bf16[6,16,128]{2,1,0:T(8,128)(2,1)S(1)}) custom-call(s32[3]{0:T(128)} %border_ref.1, bf16[16,768]{1,0:T(8,128)(2,1)} %radiosity_ref.1, f32[64,16,1024]{2,1,0:T(8,128)} %air_ref.7), custom_call_target="tpu_custom_call" | custom-call | flops 2000000000 | tf_op jit(solution)/shard_map/pack/pallas_call | solution.py:141
  1.6 0.3 collective-permute-start
  1.9 4.1 %collective-permute-start.1 = (bf16[4,16,128]{2,1,0:T(8,128)(2,1)S(1)}, bf16[4,16,128]{2,1,0:T(8,128)(2,1)S(1)}, u32[]{:S(2)}, u32[]{:S(2)}) collective-permute-start(bf16[4,16,128]{2,1,0:T(8,128)(2,1)S(1)} %get-tuple-element.23), channel_id=1, source_target_pairs={{4,8},{8,4},{12,16},{16,12},{20,24},{24,20},{5,9},{9,5},{13,17},{1... | collective-permute-start | bytes 49160 | tf_op jit(solution)/shard_map/ppermute | solution.py:699
  6.1 0.0 copy-start
  6.1 2.2 %rows.1 = (bf16[2,64,1024]{2,1,0:T(8,128)(2,1)S(1)}, bf16[2,64,1024]{2,1,0:T(8,128)(2,1)S(1)}, bf16[4,16,128]{2,1,0:T(8,128)(2,1)S(1)}) custom-call(f32[64,16,1024]{2,1,0:T(8,128)} %air_ref.7, bf16[6,16,128]{2,1,0:T(8,128)(2,1)S(1)} %get-tuple-element.20.after_ref.own_ref), custom_call_target="tpu_custom_call" | custom-call | flops 2000000000 | tf_op jit(solution)/shard_map/rows/pallas_call | solution.py:203
  8.3 0.1 collective-permute-start.4
  8.4 4.4 %collective-permute-start.5 = (bf16[2,64,1024]{2,1,0:T(8,128)(2,1)S(1)}, bf16[2,64,1024]{2,1,0:T(8,128)(2,1)S(1)}, u32[]{:S(2)}, u32[]{:S(2)}) collective-permute-start(bf16[2,64,1024]{2,1,0:T(8,128)(2,1)S(1)} %get-tuple-element.36), channel_id=1, source_target_pairs={{4,8},{8,4},{12,16},{16,12},{20,24},{24,20},{5,9},{9,5},{13,17},{1... | collective-permute-start | bytes 786440 | tf_op jit(solution)/shard_map/ppermute | solution.py:699
  12.8 0.0 collective-permute-done.near_ref
  12.8 0.0 collective-permute-done.1.far_ref
  12.8 0.0 copy-start.5
  12.9 1.3 %collective-permute-start.2 = (bf16[18,16,128]{2,1,0:T(8,128)(2,1)S(1)}, bf16[18,16,128]{2,1,0:T(8,128)(2,1)S(1)}, u32[]{:S(2)}, u32[]{:S(2)}) collective-permute-start(bf16[18,16,128]{2,1,0:T(8,128)(2,1)S(1)} %join.1.one_ref), channel_id=1, source_target_pairs={{0,2},{2,0},{1,3},{3,1},{4,6},{6,4},{5,7},{7,5},{8,10},{10,8},{9,1... | collective-permute-start | bytes 221192 | tf_op jit(solution)/shard_map/ppermute | solution.py:699
  14.1 0.0 copy-done
  14.1 2.8 %first.1.once = f32[64,16,1024]{2,1,0:T(8,128)S(1)} custom-call(f32[64,16,1024]{2,1,0:T(8,128)S(1)} %copy-done, bf16[6,16,128]{2,1,0:T(8,128)(2,1)S(1)} %get-tuple-element.20.after_ref.own_ref), custom_call_target="tpu_custom_call" | custom-call | flops 3000000000 | tf_op jit(solution)/shard_map/first/pallas_call | solution.py:323
  17.0 0.0 collective-permute-done.2.two_ref
  17.0 0.0 slice-start
  17.0 0.0 slice-start.1
  17.0 0.0 copy-start.1
  17.0 0.0 copy-start.2
  17.0 0.0 copy-start.3
  17.0 0.0 copy-start.4
  17.1 0.0 copy-start.6
  17.1 2.2 %collective-permute-start.3 = (bf16[36,16,128]{2,1,0:T(8,128)(2,1)S(1)}, bf16[36,16,128]{2,1,0:T(8,128)(2,1)S(1)}, u32[]{:S(2)}, u32[]{:S(2)}) collective-permute-start(bf16[36,16,128]{2,1,0:T(8,128)(2,1)S(1)} %stack.1.mine_ref), channel_id=1, source_target_pairs={{0,1},{1,0},{2,3},{3,2},{4,5},{5,4},{6,7},{7,6},{8,9},{9,8},{10,11... | collective-permute-start | bytes 442376 | tf_op jit(solution)/shard_map/ppermute | solution.py:699
  19.2 0.0 copy-done.5
  19.2 4.7 %second.1 = (f32[64,16,1024]{2,1,0:T(8,128)}, f32[16,1024]{1,0:T(8,128)S(1)}, f32[2,64,16,128]{3,2,1,0:T(8,128)S(1)}, f32[4,64,768]{2,1,0:T(8,128)S(1)}, f32[1,768]{1,0:T(1,128)S(1)}) custom-call(f32[64,16,1024]{2,1,0:T(8,128)S(1)} %copy-done, f32[64,16,1024]{2,1,0:T(8,128)S(1)} %first.1.once, s32[768]{0:T(1024)S(1)} %copy-done.5), custom_call_target="tpu_custom_call" | custom-call | flops 3000000000 | tf_op jit(solution)/shard_map/second/pallas_call | solution.py:403
  23.9 0.0 collective-permute-done.3.theirs_ref
  23.9 0.0 slice-done
  23.9 0.0 slice-done.1
  23.9 0.0 copy-done.1
  23.9 0.0 copy-done.2
  24.0 0.0 copy-done.3
  24.0 0.0 copy-done.4
  24.0 0.0 copy-done.6
  24.0 4.0 %main.1 = (f32[16,768]{1,0:T(8,128)}, f32[768]{0:T(1024)}, f32[64,16,1024]{2,1,0:T(8,128)}, f32[2,4,64,128]{3,2,1,0:T(8,128)S(1)}, f32[4,1024]{1,0:T(4,128)S(1)}, /*index=5*/f32[16,1024]{1,0:T(8,128)S(1)}) custom-call(s32[6,24]{1,0:T(8,128)S(1)} %copy-done.2, f32[16]{0:T(128)S(1)} %copy-done.6, ...), custom_call_target="tpu_custom_call", output_to_operand_aliasing={{2}: (12, {})} | custom-call | flops 4000000000 | tf_op jit(solution)/shard_map/main/pallas_call | solution.py:598
  28.0 0.0 collective-permute-done.4.near_ref
  28.0 0.0 collective-permute-done.5.far_ref
  28.0 1.5 %finish.1 = f32[64,16,1024]{2,1,0:T(8,128)} custom-call(f32[64,16,1024]{2,1,0:T(8,128)} %get-tuple-element.30.air_ref, f32[4,64,768]{2,1,0:T(8,128)S(1)} %get-tuple-element.31.edge_ref, f32[2,4,64,128]{3,2,1,0:T(8,128)S(1)} %get-tuple-element.32.side_ref, f32[4,1024]{1,0:T(4,128)S(1)} %get-tuple-element.33.source_ref, ...), custom_call_target="tpu_custom_call", output_to_operand_aliasing={{}: (0, {})} | custom-call | tf_op jit(solution)/shard_map/finish/pallas_call | solution.py:686
  (3 shorter events, 0.0 us)
Async XLA Ops:
  1.6 11.1 %collective-permute-start = (bf16[4,16,128]{2,1,0:T(8,128)(2,1)S(1)}, bf16[4,16,128]{2,1,0:T(8,128)(2,1)S(1)}, u32[]{:S(2)}, u32[]{:S(2)}) collective-permute-start(bf16[4,16,128]{2,1,0:T(8,128)(2,1)S(1)} %get-tuple-element.22), channel_id=1, source_target_pairs={{0,4},{4,0},{8,12},{12,8},{16,20},{20,16},{24,28},{28,24},{1,5},{5... | collective-permute-start | bytes 49160 | tf_op jit(solution)/shard_map/ppermute | solution.py:699
  1.9 10.9 %collective-permute-start.1 = (bf16[4,16,128]{2,1,0:T(8,128)(2,1)S(1)}, bf16[4,16,128]{2,1,0:T(8,128)(2,1)S(1)}, u32[]{:S(2)}, u32[]{:S(2)}) collective-permute-start(bf16[4,16,128]{2,1,0:T(8,128)(2,1)S(1)} %get-tuple-element.23), channel_id=1, source_target_pairs={{4,8},{8,4},{12,16},{16,12},{20,24},{24,20},{5,9},{9,5},{13,17},{1... | collective-permute-start | bytes 49160 | tf_op jit(solution)/shard_map/ppermute | solution.py:699
  6.1 8.0 %copy-start = (f32[64,16,1024]{2,1,0:T(8,128)S(1)}, f32[64,16,1024]{2,1,0:T(8,128)}, u32[]{:S(2)}) copy-start(f32[64,16,1024]{2,1,0:T(8,128)} %air_ref.7) | copy-start | bytes 12582916
  8.3 19.7 %collective-permute-start.4 = (bf16[2,64,1024]{2,1,0:T(8,128)(2,1)S(1)}, bf16[2,64,1024]{2,1,0:T(8,128)(2,1)S(1)}, u32[]{:S(2)}, u32[]{:S(2)}) collective-permute-start(bf16[2,64,1024]{2,1,0:T(8,128)(2,1)S(1)} %get-tuple-element.35), channel_id=1, source_target_pairs={{0,4},{4,0},{8,12},{12,8},{16,20},{20,16},{24,28},{28,24},{1,5},{5... | collective-permute-start | bytes 786440 | tf_op jit(solution)/shard_map/ppermute | solution.py:699
  8.4 19.6 %collective-permute-start.5 = (bf16[2,64,1024]{2,1,0:T(8,128)(2,1)S(1)}, bf16[2,64,1024]{2,1,0:T(8,128)(2,1)S(1)}, u32[]{:S(2)}, u32[]{:S(2)}) collective-permute-start(bf16[2,64,1024]{2,1,0:T(8,128)(2,1)S(1)} %get-tuple-element.36), channel_id=1, source_target_pairs={{4,8},{8,4},{12,16},{16,12},{20,24},{24,20},{5,9},{9,5},{13,17},{1... | collective-permute-start | bytes 786440 | tf_op jit(solution)/shard_map/ppermute | solution.py:699
  12.8 6.4 %copy-start.5 = (s32[768]{0:T(1024)S(1)}, s32[768]{0:T(1024)}, u32[]{:S(2)}) copy-start(s32[768]{0:T(1024)} %cell_ref.3) | copy-start | bytes 9220
  12.9 4.1 %collective-permute-start.2 = (bf16[18,16,128]{2,1,0:T(8,128)(2,1)S(1)}, bf16[18,16,128]{2,1,0:T(8,128)(2,1)S(1)}, u32[]{:S(2)}, u32[]{:S(2)}) collective-permute-start(bf16[18,16,128]{2,1,0:T(8,128)(2,1)S(1)} %join.1.one_ref), channel_id=1, source_target_pairs={{0,2},{2,0},{1,3},{3,1},{4,6},{6,4},{5,7},{7,5},{8,10},{10,8},{9,1... | collective-permute-start | bytes 221192 | tf_op jit(solution)/shard_map/ppermute | solution.py:699
  17.0 7.0 %slice-start = ((s8[4718592]{0:T(1024)(128)(4,1)}), s8[4194304]{0:T(1024)(128)(4,1)S(1)}, s32[]{:S(2)}) async-start(s8[4718592]{0:T(1024)(128)(4,1)} %bitcast), calls=%async_computation | async-start | bytes 8388608
  17.0 6.9 %slice-start.1 = ((s8[4718592]{0:T(1024)(128)(4,1)}), s8[524288]{0:T(1024)(128)(4,1)S(1)}, s32[]{:S(2)}) async-start(s8[4718592]{0:T(1024)(128)(4,1)} %bitcast), calls=%async_computation.1 | async-start | bytes 1048576
  17.0 6.9 %copy-start.1 = (bf16[16,768]{1,0:T(8,128)(2,1)S(1)}, bf16[16,768]{1,0:T(8,128)(2,1)}, u32[]{:S(2)}) copy-start(bf16[16,768]{1,0:T(8,128)(2,1)} %reflectance_ref.1) | copy-start | bytes 73732
  17.0 6.9 %copy-start.2 = (s32[6,24]{1,0:T(8,128)S(1)}, s32[6,24]{1,0:T(8,128)}, u32[]{:S(2)}) copy-start(s32[6,24]{1,0:T(8,128)} %cols_ref.1) | copy-start | bytes 1732
  17.0 6.9 %copy-start.3 = (f32[768]{0:T(1024)S(1)}, f32[768]{0:T(1024)}, u32[]{:S(2)}) copy-start(f32[768]{0:T(1024)} %emissivity_ref.1) | copy-start | bytes 9220
  17.0 6.9 %copy-start.4 = (f32[768]{0:T(1024)S(1)}, f32[768]{0:T(1024)}, u32[]{:S(2)}) copy-start(f32[768]{0:T(1024)} %temp_ref.1) | copy-start | bytes 9220
  17.1 6.9 %copy-start.6 = (f32[16]{0:T(128)S(1)}, f32[16]{0:T(128)}, u32[]{:S(2)}) copy-start(f32[16]{0:T(128)} %weight_ref.1) | copy-start | bytes 196
  17.1 6.8 %collective-permute-start.3 = (bf16[36,16,128]{2,1,0:T(8,128)(2,1)S(1)}, bf16[36,16,128]{2,1,0:T(8,128)(2,1)S(1)}, u32[]{:S(2)}, u32[]{:S(2)}) collective-permute-start(bf16[36,16,128]{2,1,0:T(8,128)(2,1)S(1)} %stack.1.mine_ref), channel_id=1, source_target_pairs={{0,1},{1,0},{2,3},{3,2},{4,5},{5,4},{6,7},{7,6},{8,9},{9,8},{10,11... | collective-permute-start | bytes 442376 | tf_op jit(solution)/shard_map/ppermute | solution.py:699

commit v3 on v2

--- a/solution.py
+++ b/solution.py
@@ -20,7 +20,7 @@
 VMEM = pltpu.VMEM
 SMEM = pltpu.SMEM
 DMA = pltpu.SemaphoreType.DMA
-PACK_COST, ROWS_COST, JOIN_COST, FIRST_COST, SECOND_COST, MAIN_COST = 2, 2, 1, 3, 3, 4
+PACK_COST, COLUMNS_COST, ROWS_COST, JOIN_COST, HOLD_COST, FIRST_COST, SECOND_COST, MAIN_COST = 2, 0.1, 1, 1, 0.1, 1, 1, 1
 
 
 def params(mebibytes):
@@ -74,24 +74,64 @@
         yield c, total
 
 
+def start_rows(air_ref, slabs, sem, last):
+    depth = air_ref.shape[1]
+    for i, r in enumerate((depth - 1, depth - 2) if last else (0, 1)):
+        pltpu.make_async_copy(air_ref.at[:, r, :], slabs.at[i], sem.at[i]).start()
+
+
+def wait_rows(air_ref, slabs, sem):
+    for i in range(2):
+        pltpu.make_async_copy(air_ref.at[:, i, :], slabs.at[i], sem.at[i]).wait()
+
+
+def put_rows(slabs, out_ref):
+    levels, width = slabs.shape[1:]
+    tiles, parts = width // LANES, levels // 16
+
+    def lost(i):
+        value = slabs[0, :, i * LANES : (i + 1) * LANES]
+        return value - value.astype(BF16).astype(F32)
+
+    for i, (c, around) in enumerate(plane_neighbours(lost, tiles)):
+        at = slice(i * LANES, (i + 1) * LANES)
+        values = slabs[0, :, at], slabs[1, :, at] + CENTRE * 2.0 * c + 2.0 * around
+        for k, value in enumerate(values):
+            value = value.astype(BF16)
+            for q in range(parts):
+                out_ref[(k * tiles + i) * parts + q] = value[16 * q : 16 * q + 16]
+
+
 def pack_kernel(
     border_ref,
     radiosity_ref,
     air_ref,
-    near_small,
+    near_out,
     far_small,
     own_ref,
     border,
     blocks_of,
     ends,
     spread,
+    slabs,
     sem,
     end_sem,
+    row_sem,
 ):
     levels, depth, width = air_ref.shape
     blocks = radiosity_ref.shape[1] // LANES
     borders = border_ref.shape[0]
+    at_small = near_out.shape[0] - far_small.shape[0]
     odd = lax.rem(lax.axis_index("district"), 2)
+
+    @pl.when(odd == 0)
+    def _():
+        start_rows(air_ref, slabs, row_sem, True)
+
+    @pl.when(odd == 1)
+    def _():
+        start_rows(air_ref, slabs, row_sem, False)
+
     first = [
         pltpu.make_async_copy(border_ref, border, sem.at[0]),
         pltpu.make_async_copy(radiosity_ref, blocks_of, sem.at[1]),
@@ -112,7 +152,7 @@
         own_ref[s] = blocks_of[:, s * LANES : (s + 1) * LANES]
     for s in range(borders):
         tile = own_ref[border[s]]
-        near_small[s] = tile
+        near_out[at_small + s] = tile
         far_small[s] = tile
     for c in edge:
         c.wait()
@@ -128,19 +168,21 @@
             tile = jnp.where(sub == 2 * n, high, tile)
             tile = jnp.where(sub == 2 * n + 1, row - high, tile)
         corner.append(tile)
-    near_small[borders] = jnp.where(odd == 0, corner[1], corner[0]).astype(BF16)
+    near_out[at_small + borders] = jnp.where(odd == 0, corner[1], corner[0]).astype(BF16)
     far_small[borders] = jnp.where(odd == 0, corner[0], corner[1]).astype(BF16)
+    wait_rows(air_ref, slabs, row_sem)
+    put_rows(slabs, near_out)
 
 
 def pack(border_list, radiosity, air):
-    levels = air.shape[0]
+    levels, _, width = air.shape
     blocks = radiosity.shape[1] // LANES
     borders = border_list.shape[0]
-    small = jax.ShapeDtypeStruct((borders + 1, 16, LANES), BF16)
-    own = jax.ShapeDtypeStruct((blocks, 16, LANES), BF16)
+    row_tiles = 2 * (width // LANES) * (levels // 16)
+    tile = lambda n: jax.ShapeDtypeStruct((n, 16, LANES), BF16)
     return pl.pallas_call(
         pack_kernel,
-        out_shape=(small, small, own),
+        out_shape=(tile(row_tiles + borders + 1), tile(borders + 1), tile(blocks)),
         in_specs=[PLACE] * 3,
         out_specs=(WHOLE,) * 3,
         scratch_shapes=[
@@ -148,8 +190,10 @@
             VMEM(radiosity.shape, BF16),
             VMEM((2, 2, levels, LANES), F32),
             VMEM((2, LANES, LANES), F32),
+            VMEM((2, levels, width), F32),
             DMA((2,)),
             DMA((2, 2)),
+            DMA((2,)),
         ],
         compiler_params=params(8),
         cost_estimate=cost(PACK_COST),
@@ -157,112 +201,130 @@
     )(in_hbm(border_list), in_hbm(radiosity), in_hbm(air))
 
 
-def rows_kernel(air_ref, after_ref, near_rows, far_rows, columns, slabs, ends, sem, end_sem):
+def columns_kernel(air_ref, after_ref, columns):
     del after_ref
     levels, depth, width = air_ref.shape
-    tiles = width // LANES
-    odd = lax.rem(lax.axis_index("district"), 2)
-    edge = [
-        pltpu.make_async_copy(air_ref.at[:, :, pl.ds(y, LANES)], ends.at[j], end_sem.at[j])
-        for j, y in enumerate((0, width - LANES))
-    ]
-    copies = [
-        pltpu.make_async_copy(air_ref.at[:, r, :], slabs.at[i], sem.at[i])
-        for i, r in enumerate((depth - 1, depth - 2, 0, 1))
-    ]
-    for c in edge + copies:
-        c.start()
     place = iota((depth, LANES), 1) // 2
     for j in range(2):
-        edge[j].wait()
         packed = jnp.zeros((depth, LANES), F32)
         for z in range(levels):
-            tile = ends[j, z]
+            tile = air_ref[z, :, j * (width - LANES) : j * (width - LANES) + LANES]
             turn = (2 * z + 2 * j) % LANES
             packed = jnp.where(place == z, pltpu.roll(tile, turn, 1) if turn else tile, packed)
         for n, piece in enumerate(split(packed, 2)):
             columns[2 * j + n] = piece
-    for c in copies:
-        c.wait()
-    for which, rows in enumerate((near_rows, far_rows)):
-        base = 2 * (odd if which == 0 else 1 - odd)
-
-        def lost(i):
-            value = slabs[base, :, i * LANES : (i + 1) * LANES]
-            return value - value.astype(BF16).astype(F32)
-
-        for i, (c, around) in enumerate(plane_neighbours(lost, tiles)):
-            at = slice(i * LANES, (i + 1) * LANES)
-            rows[0, :, at] = slabs[base, :, at].astype(BF16)
-            rows[1, :, at] = (slabs[base + 1, :, at] + CENTRE * 2.0 * c + 2.0 * around).astype(BF16)
+
+
+def end_columns(air, after):
+    return pl.pallas_call(
+        columns_kernel,
+        out_shape=jax.ShapeDtypeStruct((4, air.shape[1], LANES), BF16),
+        in_specs=[WHOLE, PLACE],
+        out_specs=WHOLE,
+        compiler_params=params(8),
+        cost_estimate=cost(COLUMNS_COST),
+        name="columns",
+    )(air, after)
+
+
+def hold_kernel(value_ref, after_ref, out_ref):
+    del after_ref
+    out_ref[...] = value_ref[...]
+
+
+def hold(value, after):
+    return pl.pallas_call(
+        hold_kernel,
+        out_shape=jax.ShapeDtypeStruct(value.shape, value.dtype),
+        in_specs=[WHOLE, PLACE],
+        out_specs=WHOLE,
+        compiler_params=params(8),
+        cost_estimate=cost(HOLD_COST),
+        name="hold",
+    )(value, after)
+
+
+def rows_kernel(air_ref, after_ref, out_ref, slabs, sem):
+    del after_ref
+    odd = lax.rem(lax.axis_index("district"), 2)
+
+    @pl.when(odd == 1)
+    def _():
+        start_rows(air_ref, slabs, sem, True)
+
+    @pl.when(odd == 0)
+    def _():
+        start_rows(air_ref, slabs, sem, False)
+
+    wait_rows(air_ref, slabs, sem)
+    put_rows(slabs, out_ref)
 
 
 def rows(air, after):
-    levels, depth, width = air.shape
-    out = jax.ShapeDtypeStruct((2, levels, width), BF16)
+    levels, _, width = air.shape
+    count = 2 * (width // LANES) * (levels // 16)
     return pl.pallas_call(
         rows_kernel,
-        out_shape=(out, out, jax.ShapeDtypeStruct((4, depth, LANES), BF16)),
-        in_specs=[PLACE, PLACE],
-        out_specs=(WHOLE,) * 3,
-        scratch_shapes=[
-            VMEM((4, levels, width), F32),
-            VMEM((2, levels, depth, LANES), F32),
-            DMA((4,)),
-            DMA((2,)),
-        ],
+        out_shape=jax.ShapeDtypeStruct((count, 16, LANES), BF16),
+        in_specs=[WHOLE, PLACE],
+        out_specs=WHOLE,
+        scratch_shapes=[VMEM((2, levels, width), F32), DMA((2,))],
         compiler_params=params(8),
         cost_estimate=cost(ROWS_COST),
         name="rows",
-    )(in_hbm(air), after)
-
-
-def join_kernel(own_ref, columns_ref, near_ref, far_ref, out_ref):
+    )(air, after)
+
+
+def join_kernel(own_ref, columns_ref, near_ref, far_ref, after_ref, out_ref):
+    del after_ref
     odd = lax.rem(lax.axis_index("district"), 2)
-    borders = near_ref.shape[0] - 1
+    borders = far_ref.shape[0] - 1
     blocks = own_ref.shape[0]
+    at_small = near_ref.shape[0] - far_ref.shape[0]
     for s in range(blocks):
         out_ref[s] = own_ref[s]
     for s in range(4):
         out_ref[blocks + 2 * borders + 2 + s] = columns_ref[s]
     for s in range(borders + 1):
-        before = jnp.where(odd == 1, near_ref[s].astype(F32), far_ref[s].astype(F32)).astype(BF16)
-        after = jnp.where(odd == 1, far_ref[s].astype(F32), near_ref[s].astype(F32)).astype(BF16)
+        near, far = near_ref[at_small + s].astype(F32), far_ref[s].astype(F32)
+        before = jnp.where(odd == 1, near, far).astype(BF16)
+        after = jnp.where(odd == 1, far, near).astype(BF16)
         at = blocks + s if s < borders else blocks + 2 * borders
         out_ref[at] = before
         out_ref[at + (borders if s < borders else 1)] = after
 
 
-def join(own, columns, near, far):
-    count = own.shape[0] + columns.shape[0] + 2 * near.shape[0]
+def join(own, columns, near, far, after):
+    count = own.shape[0] + columns.shape[0] + 2 * far.shape[0]
     return pl.pallas_call(
         join_kernel,
         out_shape=jax.ShapeDtypeStruct((count, 16, LANES), BF16),
-        in_specs=[WHOLE] * 4,
+        in_specs=[WHOLE] * 4 + [PLACE],
         out_specs=WHOLE,
         compiler_params=params(8),
         cost_estimate=cost(JOIN_COST),
         name="join",
-    )(own, columns, near, far)
-
-
-def stack_kernel(one_ref, two_ref, out_ref):
+    )(own, columns, near, far, after)
+
+
+def stack_kernel(one_ref, two_ref, after_ref, out_ref):
+    del after_ref
     part = one_ref.shape[0]
     for s in range(part):
         out_ref[s] = one_ref[s]
         out_ref[part + s] = two_ref[s]
 
 
-def stack(one, two):
+def stack(one, two, after):
     return pl.pallas_call(
         stack_kernel,
         out_shape=jax.ShapeDtypeStruct((2 * one.shape[0], 16, LANES), BF16),
-        in_specs=[WHOLE] * 2,
+        in_specs=[WHOLE] * 2 + [PLACE],
         out_specs=WHOLE,
         compiler_params=params(8),
         cost_estimate=cost(JOIN_COST),
         name="stack",
-    )(one, two)
+    )(one, two, after)
 
 
 def cell_masks(cell_ref, depth, width):
@@ -316,7 +378,7 @@
         stencil_level(z, air_ref, store, lambda x, t: zero)
         return carry
 
-    lax.fori_loop(0, levels, level, 0, unroll=8)
+    lax.fori_loop(0, levels, level, 0, unroll=levels // 2)
 
 
 def first(air, after):
@@ -344,7 +406,7 @@
     out_sem,
     edge_sem,
     *,
-    chunk,
+    spans,
 ):
     levels, depth, width = once.shape
     tiles = width // LANES
@@ -368,24 +430,21 @@
         return carry
 
     writes = []
-    for k in range(levels // chunk):
-        lax.fori_loop(k * chunk, (k + 1) * chunk, level, 0, unroll=8)
-        span = pl.ds(k * chunk, chunk)
+    done = 0
+    for k, count in enumerate(spans):
+        lax.fori_loop(done, done + count, level, 0, unroll=count)
+        span = pl.ds(done, count)
+        done += count
         lanes = pl.ds(LANES, width - 2 * LANES)
-        fresh = [
-            pltpu.make_async_copy(
-                result.at[span, :, lanes], air_out.at[span, :, lanes], out_sem.at[k]
-            )
-        ]
-        for i, x in enumerate((0, 1, depth - 2, depth - 1)):
-            fresh.append(
-                pltpu.make_async_copy(
-                    result.at[span, x, lanes], edge_out.at[i, span], edge_sem.at[k, i]
-                )
-            )
-        for c in fresh:
-            c.start()
-        writes += fresh
+        c = pltpu.make_async_copy(
+            result.at[span, :, lanes], air_out.at[span, :, lanes], out_sem.at[k]
+        )
+        c.start()
+        writes.append(c)
+    for i, x in enumerate((0, 1, depth - 2, depth - 1)):
+        c = pltpu.make_async_copy(result.at[:, x, lanes], edge_out.at[i], edge_sem.at[i])
+        c.start()
+        writes.append(c)
     ground_out[...] = result[0]
     at_low, at_high = cell_masks(cell_ref, depth, width)
     ground = jnp.concatenate([air_ref[0, :, j] for j in at], axis=0)
@@ -399,9 +458,9 @@
 
 def second(air, once, cell):
     levels, depth, width = air.shape
-    chunk = levels // 8
-    return pl.pallas_call(
-        functools.partial(second_kernel, chunk=chunk),
+    spans = (levels // 2, levels // 4, levels // 8, levels // 8)
+    return pl.pallas_call(
+        functools.partial(second_kernel, spans=spans),
         out_shape=(
             jax.ShapeDtypeStruct(air.shape, F32),
             jax.ShapeDtypeStruct((depth, width), F32),
@@ -411,7 +470,7 @@
         ),
         in_specs=[WHOLE] * 3,
         out_specs=(PLACE,) + (WHOLE,) * 4,
-        scratch_shapes=[VMEM(air.shape, F32), DMA((levels // chunk,)), DMA((levels // chunk, 4))],
+        scratch_shapes=[VMEM(air.shape, F32), DMA((len(spans),)), DMA((4,))],
         compiler_params=params(20),
         cost_estimate=cost(SECOND_COST),
         name="second",
@@ -440,11 +499,7 @@
     ground_out,
     sides,
     pieces,
-    radiosity_buf,
-    surface_buf,
     out_sem,
-    edge_sem,
-    surface_sem,
 ):
     del next_ref
     levels, depth = sides_ref.shape[1:3]
@@ -501,16 +556,16 @@
     lane8 = iota((half, LANES), 1)
     both = [lane8 < 2, lane8 >= LANES - 2]
 
-    def edges(z, carry):
+    for z in range(levels):
         for side in range(2):
-            turn = lax.rem(2 * LANES - 2 * z - 2 * side, LANES)
+            turn = (2 * LANES - 2 * z - 2 * side) % LANES
             for x in range(2):
                 at = slice(x * half, (x + 1) * half)
-                value = pltpu.roll(beside[side][at], turn, 1)
-                sides[side, z, at] = sides_ref[side, z, at] + jnp.where(both[side], value, 0.0)
-        return carry
-
-    lax.fori_loop(0, levels, edges, 0, unroll=8)
+                value = pltpu.roll(beside[side][at], turn, 1) if turn else beside[side][at]
+                value = sides_ref[side, z, at] + jnp.where(both[side], value, 0.0)
+                sides[side, z, at] = value
+                for i, row in ((2, half - 2), (3, half - 1)) if x else ((0, 0), (1, 1)):
+                    side_edge_out[side, i, z : z + 1] = value[row : row + 1]
     for side in range(2):
         lanes = pl.ds(side * (width - LANES), LANES)
         c = pltpu.make_async_copy(
@@ -520,12 +575,6 @@
         )
         c.start()
         writes.append(c)
-        for i, x in enumerate((0, 1, depth - 2, depth - 1)):
-            c = pltpu.make_async_copy(
-                sides.at[side, :, x, :], side_edge_out.at[side, i], edge_sem.at[side, i]
-            )
-            c.start()
-            writes.append(c)
     blocks = []
     for r in range(row_blocks):
         picked = []
@@ -555,17 +604,11 @@
     weight = jnp.concatenate([weight] * (patches // LANES), axis=1)
     emission = weight * (emissivity_ref[...].reshape(1, patches) * (squared * squared))
     albedo = reflectance_ref[...].astype(F32)
-    radiosity_buf[...] = emission + albedo * irradiance
-    c = pltpu.make_async_copy(radiosity_buf, radiosity_out, surface_sem.at[1])
-    c.start()
-    writes.append(c)
+    radiosity_out[...] = emission + albedo * irradiance
     absorbed = jnp.sum((1.0 - albedo) * irradiance, axis=0, keepdims=True)
     emitted = jnp.sum(emission, axis=0, keepdims=True)
     surface = temp + GAIN * (absorbed - emitted) - COUPLE * (temp - 1.0 - air_cell)
-    surface_buf[...] = surface
-    c = pltpu.make_async_copy(surface_buf.at[0], surface_out, surface_sem.at[0])
-    c.start()
-    writes.append(c)
+    surface_out[...] = surface
     flux = HEAT * (COUPLE * (surface - 1.0 - air_cell))
     source = sum(
         lax.dot_general(
@@ -599,21 +642,17 @@
         main_kernel,
         out_shape=(
             jax.ShapeDtypeStruct((bands, patches), F32),
-            jax.ShapeDtypeStruct((patches,), F32),
+            jax.ShapeDtypeStruct((1, patches), F32),
             jax.ShapeDtypeStruct(following.shape, F32),
             jax.ShapeDtypeStruct((2, 4, levels, LANES), F32),
             jax.ShapeDtypeStruct((4, width), F32),
             jax.ShapeDtypeStruct((depth, width), F32),
         ),
         in_specs=[pl.BlockSpec(memory_space=SMEM)] * 2 + [WHOLE] * 10 + [PLACE],
-        out_specs=(PLACE, PLACE, PLACE, WHOLE, WHOLE, WHOLE),
+        out_specs=(WHOLE, WHOLE, PLACE, WHOLE, WHOLE, WHOLE),
         scratch_shapes=[
             VMEM(sides.shape, F32),
             VMEM((4 * visible, 16, LANES), BF16),
-            VMEM((bands, patches), F32),
-            VMEM((1, patches), F32),
-            DMA((2,)),
-            DMA((2, 4)),
             DMA((2,)),
         ],
         input_output_aliases={12: 2},
@@ -638,11 +677,25 @@
 
 
 def finish_kernel(
-    air_ref, edge_ref, side_ref, source_ref, ground_ref, near_ref, far_ref, out_ref, slabs, sem
+    air_ref,
+    edge_ref,
+    side_ref,
+    source_ref,
+    ground_ref,
+    radiosity_ref,
+    surface_ref,
+    near_ref,
+    far_ref,
+    out_ref,
+    radiosity_out,
+    surface_out,
+    slabs,
+    sem,
+    value_sem,
 ):
     del air_ref
-    levels, width = near_ref.shape[1], near_ref.shape[2]
-    depth = out_ref.shape[1]
+    levels, depth, width = out_ref.shape
+    parts = levels // 16
     tiles = width // LANES
     odd = lax.rem(lax.axis_index("district"), 2)
     ground = iota((levels, LANES), 0) == 0
@@ -650,14 +703,19 @@
         pltpu.make_async_copy(ground_ref.at[x], out_ref.at[0, x], sem.at[2 + x])
         for x in range(2, depth - 2)
     ]
+    copies += [
+        pltpu.make_async_copy(radiosity_ref, radiosity_out, value_sem.at[0]),
+        pltpu.make_async_copy(surface_ref.at[0], surface_out, value_sem.at[1]),
+    ]
     for c in copies:
         c.start()
     for side in range(2):
         use_near = (odd == 1) if side == 0 else (odd == 0)
 
         def received(k, i):
-            at = slice(i * LANES, (i + 1) * LANES)
-            return jnp.where(use_near, near_ref[k, :, at].astype(F32), far_ref[k, :, at].astype(F32))
+            at = [(k * tiles + i) * parts + q for q in range(parts)]
+            near, far = (jnp.concatenate([ref[n] for n in at]) for ref in (near_ref, far_ref))
+            return jnp.where(use_near, near.astype(F32), far.astype(F32))
 
         def base(n, i):
             if i in (0, tiles - 1):
@@ -681,18 +739,22 @@
         c.wait()
 
 
-def finish(air, edge, side, source, ground, near, far):
-    levels, width = near.shape[1:]
+def finish(air, edge, side, source, ground, radiosity, surface, near, far):
+    levels, depth, width = air.shape
     return pl.pallas_call(
         finish_kernel,
-        out_shape=jax.ShapeDtypeStruct(air.shape, F32),
-        in_specs=[PLACE] + [WHOLE] * 6,
-        out_specs=PLACE,
-        scratch_shapes=[VMEM((4, levels, width), F32), DMA((air.shape[1],))],
+        out_shape=(
+            jax.ShapeDtypeStruct(air.shape, F32),
+            jax.ShapeDtypeStruct(radiosity.shape, F32),
+            jax.ShapeDtypeStruct(surface.shape[1:], F32),
+        ),
+        in_specs=[PLACE] + [WHOLE] * 8,
+        out_specs=(PLACE,) * 3,
+        scratch_shapes=[VMEM((4, levels, width), F32), DMA((depth,)), DMA((2,))],
         input_output_aliases={0: 0},
         compiler_params=params(8),
         name="finish",
-    )(in_hbm(air), edge, side, source, ground, near, far)
+    )(in_hbm(air), edge, side, source, ground, radiosity, surface, near, far)
 
 
 def swap(value, axis, pairs):
@@ -714,19 +776,20 @@
     districts, blks = lax.axis_size("district"), lax.axis_size("blk")
     near_pairs = [(i, i + 1) for i in range(0, districts - 1, 2)]
     far_pairs = [(i, i + 1) for i in range(1, districts - 1, 2)]
-    near_small, far_small, own = pack(border_list, radiosity, air)
-    near_rows, far_rows, columns = rows(air, own)
-    near_small = swap(near_small, "district", near_pairs)
-    far_small = swap(far_small, "district", far_pairs)
-    near_rows = swap(near_rows, "district", near_pairs)
-    far_rows = swap(far_rows, "district", far_pairs)
-    once = first(air, own)
+    near, far_small, own = pack(border_list, radiosity, air)
+    near = swap(near, "district", near_pairs)
+    far_small = swap(hold(far_small, own), "district", far_pairs)
+    columns = end_columns(air, own)
+    once = first(air, columns)
     following, ground, sides, edge, air_cell = second(air, once, patch_cell)
-    own = join(own, columns, near_small, far_small)
+    far = rows(air, once)
+    own = join(own, columns, near, far_small, far)
+    far = hold(far, own)
     across = swap(own, "blk", [(i, i ^ 2) for i in range(blks) if i < i ^ 2])
-    mine = stack(own, across)
+    mine = stack(own, across, far)
+    far = swap(far, "district", far_pairs)
     theirs = swap(mine, "blk", [(i, i ^ 1) for i in range(blks) if i < i ^ 1])
-    radiosity_next, surface_next, air_next, side, source, ground = main(
+    radiosity, surface, air_next, side, source, ground = main(
         view_cols,
         band_weight,
         mine,
@@ -741,7 +804,9 @@
         sides,
         following,
     )
-    air_next = finish(air_next, edge, side, source, ground, near_rows, far_rows)
+    air_next, radiosity_next, surface_next = finish(
+        air_next, edge, side, source, ground, radiosity, surface, near, far
+    )
     return radiosity_next, surface_next, air_next
 
 

time: 29.8 us -> 25.4 us (0.85)
  Pallas kernels: 16.3 us -> 13.2 us
  starting transfers between devices: 12.3 us -> 11 us
    pallas_call x4 -> x7, Pallas kernels: 9.41 us -> 7.64 us  [the longest x1 3.51 us: second(): pl.pallas_call(functools.partial(second_kernel, spans=spans), out_shape=(...]
    ppermute x6 -> x5, starting transfers between devices: 12.3 us -> 11 us  [swap(): lax.ppermute(value, axis, [p for a, b in pairs for p in ((a, b), (b, a))])]
    pallas_call x1, Pallas kernels: 4.02 us -> 3.18 us  [main(): pl.pallas_call(main_kernel, out_shape=(jax.ShapeDtypeStruct((bands, patch...]
    pallas_call x1, Pallas kernels: 2.81 us -> 2.33 us  [first(): pl.pallas_call(first_kernel, out_shape=jax.ShapeDtypeStruct(air.shape, F3...]
  transfers between devices with their start and end apart: 6 -> 5, of which waited for: 0 -> 1; matrix products, arithmetic and copies ran while one was open for 0% -> 0% of each run, Pallas kernels for 47% -> 40%
where the time goes in v3:
time: 25.4 us; the launch traced here: 25.3 us
  Pallas kernels  13.2 us (52%)
  starting transfers between devices  11 us (43%)
  between operations  0.88 us (3%)
    ppermute x5, starting transfers between devices, swap(): lax.ppermute(value, axis, [p for a, b in pairs for p in ((a, b), (b, a))])  11 us
    pallas_call x1, Pallas kernels, second(): pl.pallas_call(functools.partial(second_kernel, spans=spans), out_shape=(...  3.51 us
    pallas_call x1, Pallas kernels, main(): pl.pallas_call(main_kernel, out_shape=(jax.ShapeDtypeStruct((bands, patch...  3.18 us
    pallas_call x1, Pallas kernels, first(): pl.pallas_call(first_kernel, out_shape=jax.ShapeDtypeStruct(air.shape, F3...  2.33 us
    pallas_call x1, Pallas kernels, pack(): pl.pallas_call(pack_kernel, out_shape=(tile(row_tiles + borders + 1), til...  1.63 us
    pallas_call x1, Pallas kernels, finish(): pl.pallas_call(finish_kernel, out_shape=(jax.ShapeDtypeStruct(air.shape,...  1.5 us
    pallas_call x1, Pallas kernels, rows(): pl.pallas_call(rows_kernel, out_shape=jax.ShapeDtypeStruct((count, 16, LA...  0.64 us
  transfers between devices with their start and end apart: 5, of which 1 were waited for; matrix products, arithmetic and copies ran while one was open for 0% of the time, Pallas kernels for 40%

profile of v3, /device:TPU:13, one launch (start us, length us, event | category | flops | bytes accessed | tf_op | source)
XLA Modules:
  0.0 25.3 jit_solution(9147005261885746917)
XLA Ops:
  0.6 0.0 copy-start
  0.6 1.6 %pack.1 = (bf16[68,16,128]{2,1,0:T(8,128)(2,1)S(1)}, bf16[4,16,128]{2,1,0:T(8,128)(2,1)S(1)}, bf16[6,16,128]{2,1,0:T(8,128)(2,1)S(1)}) custom-call(s32[3]{0:T(128)} %border_ref.1, bf16[16,768]{1,0:T(8,128)(2,1)} %radiosity_ref.1, f32[64,16,1024]{2,1,0:T(8,128)} %air_ref.9), custom_call_target="tpu_custom_call" | custom-call | flops 2000000000 | tf_op jit(solution)/shard_map/pack/pallas_call | solution.py:183
  2.3 0.3 %collective-permute-start = (bf16[68,16,128]{2,1,0:T(8,128)(2,1)S(1)}, bf16[68,16,128]{2,1,0:T(8,128)(2,1)S(1)}, u32[]{:S(2)}, u32[]{:S(2)}) collective-permute-start(bf16[68,16,128]{2,1,0:T(8,128)(2,1)S(1)} %get-tuple-element.21), channel_id=1, source_target_pairs={{0,4},{4,0},{8,12},{12,8},{16,20},{20,16},{24,28},{28,24},{1,5},{5... | collective-permute-start | bytes 835592 | tf_op jit(solution)/shard_map/ppermute | solution.py:761
  2.6 4.2 %collective-permute-start.1 = (bf16[4,16,128]{2,1,0:T(8,128)(2,1)S(1)}, bf16[4,16,128]{2,1,0:T(8,128)(2,1)S(1)}, u32[]{:S(2)}, u32[]{:S(2)}) collective-permute-start(bf16[4,16,128]{2,1,0:T(8,128)(2,1)S(1)} %hold.2), channel_id=1, source_target_pairs={{4,8},{8,4},{12,16},{16,12},{20,24},{24,20},{5,9},{9,5},{13,17},{1... | collective-permute-start | bytes 49160 | tf_op jit(solution)/shard_map/ppermute | solution.py:761
  6.7 0.0 copy-done
  6.7 0.3 %columns.1.after_ref.columns_ref = bf16[4,16,128]{2,1,0:T(8,128)(2,1)S(1)} custom-call(f32[64,16,1024]{2,1,0:T(8,128)S(1)} %copy-done, bf16[6,16,128]{2,1,0:T(8,128)(2,1)S(1)} %get-tuple-element.20.after_ref.own_ref), custom_call_target="tpu_custom_call" | custom-call | flops 100000000 | tf_op jit(solution)/shard_map/columns/pallas_call | solution.py:219
  7.1 2.3 %first.1.after_ref.once = f32[64,16,1024]{2,1,0:T(8,128)S(1)} custom-call(f32[64,16,1024]{2,1,0:T(8,128)S(1)} %copy-done, bf16[4,16,128]{2,1,0:T(8,128)(2,1)S(1)} %columns.1.after_ref.columns_ref), custom_call_target="tpu_custom_call" | custom-call | flops 1000000000 | tf_op jit(solution)/shard_map/first/pallas_call | solution.py:385
  9.4 0.6 %rows.1.after_ref.value_ref = bf16[64,16,128]{2,1,0:T(8,128)(2,1)S(1)} custom-call(f32[64,16,1024]{2,1,0:T(8,128)S(1)} %copy-done, f32[64,16,1024]{2,1,0:T(8,128)S(1)} %first.1.after_ref.once), custom_call_target="tpu_custom_call" | custom-call | flops 1000000000 | tf_op jit(solution)/shard_map/rows/pallas_call | solution.py:266
  10.1 0.0 copy-start.2
  10.1 0.0 collective-permute-done.1.far_ref
  10.1 0.1 collective-permute-done.near_ref
  10.2 1.3 %collective-permute-start.2 = (bf16[18,16,128]{2,1,0:T(8,128)(2,1)S(1)}, bf16[18,16,128]{2,1,0:T(8,128)(2,1)S(1)}, u32[]{:S(2)}, u32[]{:S(2)}) collective-permute-start(bf16[18,16,128]{2,1,0:T(8,128)(2,1)S(1)} %join.1.after_ref.one_ref), channel_id=1, source_target_pairs={{0,2},{2,0},{1,3},{3,1},{4,6},{6,4},{5,7},{7,5},{8,10},{10,8},{9,1... | collective-permute-start | bytes 221192 | tf_op jit(solution)/shard_map/ppermute | solution.py:761
  11.5 3.0 %collective-permute-start.4 = (bf16[64,16,128]{2,1,0:T(8,128)(2,1)S(1)}, bf16[64,16,128]{2,1,0:T(8,128)(2,1)S(1)}, u32[]{:S(2)}, u32[]{:S(2)}) collective-permute-start(bf16[64,16,128]{2,1,0:T(8,128)(2,1)S(1)} %hold.3.after_ref), channel_id=1, source_target_pairs={{4,8},{8,4},{12,16},{16,12},{20,24},{24,20},{5,9},{9,5},{13,17},{1... | collective-permute-start | bytes 786440 | tf_op jit(solution)/shard_map/ppermute | solution.py:761
  14.5 0.0 collective-permute-done.2.two_ref
  14.5 0.0 slice-start
  14.5 0.0 slice-start.1
  14.6 0.0 copy-start.1
  14.6 0.0 copy-start.3
  14.6 0.0 copy-start.4
  14.6 0.0 copy-start.5
  14.6 0.0 copy-start.6
  14.6 2.3 %collective-permute-start.3 = (bf16[36,16,128]{2,1,0:T(8,128)(2,1)S(1)}, bf16[36,16,128]{2,1,0:T(8,128)(2,1)S(1)}, u32[]{:S(2)}, u32[]{:S(2)}) collective-permute-start(bf16[36,16,128]{2,1,0:T(8,128)(2,1)S(1)} %stack.1.mine_ref), channel_id=1, source_target_pairs={{0,1},{1,0},{2,3},{3,2},{4,5},{5,4},{6,7},{7,6},{8,9},{9,8},{10,11... | collective-permute-start | bytes 442376 | tf_op jit(solution)/shard_map/ppermute | solution.py:761
  17.0 0.0 copy-done.2
  17.0 3.5 %second.1 = (f32[64,16,1024]{2,1,0:T(8,128)}, f32[16,1024]{1,0:T(8,128)S(1)}, f32[2,64,16,128]{3,2,1,0:T(8,128)S(1)}, f32[4,64,768]{2,1,0:T(8,128)S(1)}, f32[1,768]{1,0:T(1,128)S(1)}) custom-call(f32[64,16,1024]{2,1,0:T(8,128)S(1)} %copy-done, f32[64,16,1024]{2,1,0:T(8,128)S(1)} %first.1.after_ref.once, s32[768]{0:T(1024)S(1)} %copy-done.2), custom_call_target="tpu_custom_call" | custom-call | flops 1000000000 | tf_op jit(solution)/shard_map/second/pallas_call | solution.py:462
  20.5 0.0 collective-permute-done.3.theirs_ref
  20.5 0.0 slice-done
  20.5 0.0 slice-done.1
  20.5 0.0 copy-done.1
  20.5 0.0 copy-done.3
  20.5 0.0 copy-done.4
  20.5 0.0 copy-done.5
  20.6 0.0 copy-done.6
  20.6 3.2 %main.1 = (f32[16,768]{1,0:T(8,128)S(1)}, f32[1,768]{1,0:T(1,128)S(1)}, f32[64,16,1024]{2,1,0:T(8,128)}, f32[2,4,64,128]{3,2,1,0:T(8,128)S(1)}, f32[4,1024]{1,0:T(4,128)S(1)}, /*index=5*/f32[16,1024]{1,0:T(8,128)S(1)}) custom-call(s32[6,24]{1,0:T(8,128)S(1)} %copy-done.3, f32[16]{0:T(128)S(1)} %copy-done.6, ...), custom_call_target="tpu_custom_call", output_to_operand_aliasing={{2}: (12, {})} | custom-call | flops 1000000000 | tf_op jit(solution)/shard_map/main/pallas_call | solution.py:641
  23.8 0.0 collective-permute-done.4.far_ref
  23.8 1.5 %finish.1 = (f32[64,16,1024]{2,1,0:T(8,128)}, f32[16,768]{1,0:T(8,128)}, f32[768]{0:T(1024)}) custom-call(f32[64,16,1024]{2,1,0:T(8,128)} %get-tuple-element.27.air_ref, f32[4,64,768]{2,1,0:T(8,128)S(1)} %get-tuple-element.28.edge_ref, f32[2,4,64,128]{3,2,1,0:T(8,128)S(1)} %get-tuple-element.29.side_ref, ...), custom_call_target="tpu_custom_call", output_to_operand_aliasing={{0}: (0, {})} | custom-call | tf_op jit(solution)/shard_map/finish/pallas_call | solution.py:744
  (5 shorter events, 0.0 us)
Async XLA Ops:
  0.6 6.1 %copy-start = (f32[64,16,1024]{2,1,0:T(8,128)S(1)}, f32[64,16,1024]{2,1,0:T(8,128)}, u32[]{:S(2)}) copy-start(f32[64,16,1024]{2,1,0:T(8,128)} %air_ref.9) | copy-start | bytes 12582916
  2.3 7.9 %collective-permute-start = (bf16[68,16,128]{2,1,0:T(8,128)(2,1)S(1)}, bf16[68,16,128]{2,1,0:T(8,128)(2,1)S(1)}, u32[]{:S(2)}, u32[]{:S(2)}) collective-permute-start(bf16[68,16,128]{2,1,0:T(8,128)(2,1)S(1)} %get-tuple-element.21), channel_id=1, source_target_pairs={{0,4},{4,0},{8,12},{12,8},{16,20},{20,16},{24,28},{28,24},{1,5},{5... | collective-permute-start | bytes 835592 | tf_op jit(solution)/shard_map/ppermute | solution.py:761
  2.6 7.5 %collective-permute-start.1 = (bf16[4,16,128]{2,1,0:T(8,128)(2,1)S(1)}, bf16[4,16,128]{2,1,0:T(8,128)(2,1)S(1)}, u32[]{:S(2)}, u32[]{:S(2)}) collective-permute-start(bf16[4,16,128]{2,1,0:T(8,128)(2,1)S(1)} %hold.2), channel_id=1, source_target_pairs={{4,8},{8,4},{12,16},{16,12},{20,24},{24,20},{5,9},{9,5},{13,17},{1... | collective-permute-start | bytes 49160 | tf_op jit(solution)/shard_map/ppermute | solution.py:761
  10.1 6.9 %copy-start.2 = (s32[768]{0:T(1024)S(1)}, s32[768]{0:T(1024)}, u32[]{:S(2)}) copy-start(s32[768]{0:T(1024)} %cell_ref.3) | copy-start | bytes 9220
  10.2 4.3 %collective-permute-start.2 = (bf16[18,16,128]{2,1,0:T(8,128)(2,1)S(1)}, bf16[18,16,128]{2,1,0:T(8,128)(2,1)S(1)}, u32[]{:S(2)}, u32[]{:S(2)}) collective-permute-start(bf16[18,16,128]{2,1,0:T(8,128)(2,1)S(1)} %join.1.after_ref.one_ref), channel_id=1, source_target_pairs={{0,2},{2,0},{1,3},{3,1},{4,6},{6,4},{5,7},{7,5},{8,10},{10,8},{9,1... | collective-permute-start | bytes 221192 | tf_op jit(solution)/shard_map/ppermute | solution.py:761
  11.5 12.2 %collective-permute-start.4 = (bf16[64,16,128]{2,1,0:T(8,128)(2,1)S(1)}, bf16[64,16,128]{2,1,0:T(8,128)(2,1)S(1)}, u32[]{:S(2)}, u32[]{:S(2)}) collective-permute-start(bf16[64,16,128]{2,1,0:T(8,128)(2,1)S(1)} %hold.3.after_ref), channel_id=1, source_target_pairs={{4,8},{8,4},{12,16},{16,12},{20,24},{24,20},{5,9},{9,5},{13,17},{1... | collective-permute-start | bytes 786440 | tf_op jit(solution)/shard_map/ppermute | solution.py:761
  14.5 6.0 %slice-start = ((s8[4718592]{0:T(1024)(128)(4,1)}), s8[4194304]{0:T(1024)(128)(4,1)S(1)}, s32[]{:S(2)}) async-start(s8[4718592]{0:T(1024)(128)(4,1)} %bitcast), calls=%async_computation | async-start | bytes 8388608
  14.5 6.0 %slice-start.1 = ((s8[4718592]{0:T(1024)(128)(4,1)}), s8[524288]{0:T(1024)(128)(4,1)S(1)}, s32[]{:S(2)}) async-start(s8[4718592]{0:T(1024)(128)(4,1)} %bitcast), calls=%async_computation.1 | async-start | bytes 1048576
  14.6 6.0 %copy-start.1 = (bf16[16,768]{1,0:T(8,128)(2,1)S(1)}, bf16[16,768]{1,0:T(8,128)(2,1)}, u32[]{:S(2)}) copy-start(bf16[16,768]{1,0:T(8,128)(2,1)} %reflectance_ref.1) | copy-start | bytes 73732
  14.6 6.0 %copy-start.3 = (s32[6,24]{1,0:T(8,128)S(1)}, s32[6,24]{1,0:T(8,128)}, u32[]{:S(2)}) copy-start(s32[6,24]{1,0:T(8,128)} %cols_ref.1) | copy-start | bytes 1732
  14.6 6.0 %copy-start.4 = (f32[768]{0:T(1024)S(1)}, f32[768]{0:T(1024)}, u32[]{:S(2)}) copy-start(f32[768]{0:T(1024)} %emissivity_ref.1) | copy-start | bytes 9220
  14.6 6.0 %copy-start.5 = (f32[768]{0:T(1024)S(1)}, f32[768]{0:T(1024)}, u32[]{:S(2)}) copy-start(f32[768]{0:T(1024)} %temp_ref.1) | copy-start | bytes 9220
  14.6 6.0 %copy-start.6 = (f32[16]{0:T(128)S(1)}, f32[16]{0:T(128)}, u32[]{:S(2)}) copy-start(f32[16]{0:T(128)} %weight_ref.1) | copy-start | bytes 196
  14.6 5.9 %collective-permute-start.3 = (bf16[36,16,128]{2,1,0:T(8,128)(2,1)S(1)}, bf16[36,16,128]{2,1,0:T(8,128)(2,1)S(1)}, u32[]{:S(2)}, u32[]{:S(2)}) collective-permute-start(bf16[36,16,128]{2,1,0:T(8,128)(2,1)S(1)} %stack.1.mine_ref), channel_id=1, source_target_pairs={{0,1},{1,0},{2,3},{3,2},{4,5},{5,4},{6,7},{7,6},{8,9},{9,8},{10,11... | collective-permute-start | bytes 442376 | tf_op jit(solution)/shard_map/ppermute | solution.py:761

commit v4 on v3

--- a/solution.py
+++ b/solution.py
@@ -109,11 +109,11 @@
     near_out,
     far_small,
     own_ref,
+    slabs,
     border,
     blocks_of,
     ends,
     spread,
-    slabs,
     sem,
     end_sem,
     row_sem,
@@ -182,15 +182,19 @@
     tile = lambda n: jax.ShapeDtypeStruct((n, 16, LANES), BF16)
     return pl.pallas_call(
         pack_kernel,
-        out_shape=(tile(row_tiles + borders + 1), tile(borders + 1), tile(blocks)),
+        out_shape=(
+            tile(row_tiles + borders + 1),
+            tile(borders + 1),
+            tile(blocks),
+            jax.ShapeDtypeStruct((2, levels, width), F32),
+        ),
         in_specs=[PLACE] * 3,
-        out_specs=(WHOLE,) * 3,
+        out_specs=(WHOLE,) * 4,
         scratch_shapes=[
             SMEM(border_list.shape, border_list.dtype),
             VMEM(radiosity.shape, BF16),
             VMEM((2, 2, levels, LANES), F32),
             VMEM((2, LANES, LANES), F32),
-            VMEM((2, levels, width), F32),
             DMA((2,)),
             DMA((2, 2)),
             DMA((2,)),
@@ -265,10 +269,13 @@
     count = 2 * (width // LANES) * (levels // 16)
     return pl.pallas_call(
         rows_kernel,
-        out_shape=jax.ShapeDtypeStruct((count, 16, LANES), BF16),
+        out_shape=(
+            jax.ShapeDtypeStruct((count, 16, LANES), BF16),
+            jax.ShapeDtypeStruct((2, levels, width), F32),
+        ),
         in_specs=[WHOLE, PLACE],
-        out_specs=WHOLE,
-        scratch_shapes=[VMEM((2, levels, width), F32), DMA((2,))],
+        out_specs=(WHOLE, WHOLE),
+        scratch_shapes=[DMA((2,))],
         compiler_params=params(8),
         cost_estimate=cost(ROWS_COST),
         name="rows",
@@ -336,7 +343,7 @@
     return at_low, spots == (y_of // LANES) * depth + x_of
 
 
-def stencil_level(z, src, store, beyond):
+def stencil_level(z, src, store):
     levels, depth, width = src.shape
     tiles = width // LANES
     half = depth // 2
@@ -353,8 +360,8 @@
         back = [pltpu.roll(c, LANES - 1, 1) for c in centre[x]]
         for t in range(tiles):
             c = centre[x][t]
-            before = pltpu.roll(centre[0][t], 1, 0) if x else beyond(0, t)
-            after = beyond(1, t) if x else pltpu.roll(centre[1][t], half - 1, 0)
+            before = pltpu.roll(centre[0][t], 1, 0) if x else zero
+            after = zero if x else pltpu.roll(centre[1][t], half - 1, 0)
             total = src[below, at_x[x], at[t]] * under + src[above, at_x[x], at[t]] * over
             total = total + jnp.where(sub == 0, before, pltpu.roll(c, 1, 0))
             total = total + jnp.where(sub == half - 1, after, pltpu.roll(c, half - 1, 0))
@@ -369,13 +376,12 @@
     del after_ref
     levels, depth, _ = air_ref.shape
     half = depth // 2
-    zero = jnp.zeros((half, LANES), F32)
 
     def level(z, carry):
         def store(x, t, total):
             once[z, x * half : (x + 1) * half, t * LANES : (t + 1) * LANES] = total
 
-        stencil_level(z, air_ref, store, lambda x, t: zero)
+        stencil_level(z, air_ref, store)
         return carry
 
     lax.fori_loop(0, levels, level, 0, unroll=levels // 2)
@@ -411,22 +417,17 @@
     levels, depth, width = once.shape
     tiles = width // LANES
     half = depth // 2
-    district = lax.axis_index("district")
-    has_top, has_bottom = flag(district > 0), flag(district < lax.axis_size("district") - 1)
     at = [slice(t * LANES, (t + 1) * LANES) for t in range(tiles)]
     at_x = [slice(x * half, (x + 1) * half) for x in range(2)]
 
     def level(z, carry):
-        def beyond(x, t):
-            return air_ref[z, at_x[x], at[t]] * (has_bottom if x else has_top)
-
         def store(x, t, total):
             total = SQUARE * total
             result[z, at_x[x], at[t]] = total
             if t in (0, tiles - 1):
                 sides_out[0 if t == 0 else 1, z, at_x[x]] = total
 
-        stencil_level(z, once, store, beyond)
+        stencil_level(z, once, store)
         return carry
 
     writes = []
@@ -686,6 +687,8 @@
     surface_ref,
     near_ref,
     far_ref,
+    near_own,
+    far_own,
     out_ref,
     radiosity_out,
     surface_out,
@@ -697,7 +700,9 @@
     levels, depth, width = out_ref.shape
     parts = levels // 16
     tiles = width // LANES
-    odd = lax.rem(lax.axis_index("district"), 2)
+    district = lax.axis_index("district")
+    odd = lax.rem(district, 2)
+    has = flag(district > 0), flag(district < lax.axis_size("district") - 1)
     ground = iota((levels, LANES), 0) == 0
     copies = [
         pltpu.make_async_copy(ground_ref.at[x], out_ref.at[0, x], sem.at[2 + x])
@@ -727,7 +732,8 @@
         outer, inner = (0, 1) if side == 0 else (3, 2)
         for i, (c, around) in enumerate(plane_neighbours(functools.partial(received, 0), tiles)):
             at = slice(i * LANES, (i + 1) * LANES)
-            reach = (2.0 * CENTRE) * c + 2.0 * around + received(1, i)
+            own = jnp.where(use_near, near_own[0, :, at], far_own[0, :, at]) * has[side]
+            reach = (2.0 * CENTRE) * c + 2.0 * around + received(1, i) + own
             slabs[outer, :, at] = base(outer, i) + SQUARE * reach
             slabs[inner, :, at] = base(inner, i) + SQUARE * c
         for i in (outer, inner):
@@ -739,7 +745,7 @@
         c.wait()
 
 
-def finish(air, edge, side, source, ground, radiosity, surface, near, far):
+def finish(air, edge, side, source, ground, radiosity, surface, near, far, near_own, far_own):
     levels, depth, width = air.shape
     return pl.pallas_call(
         finish_kernel,
@@ -748,13 +754,13 @@
             jax.ShapeDtypeStruct(radiosity.shape, F32),
             jax.ShapeDtypeStruct(surface.shape[1:], F32),
         ),
-        in_specs=[PLACE] + [WHOLE] * 8,
+        in_specs=[PLACE] + [WHOLE] * 10,
         out_specs=(PLACE,) * 3,
         scratch_shapes=[VMEM((4, levels, width), F32), DMA((depth,)), DMA((2,))],
         input_output_aliases={0: 0},
         compiler_params=params(8),
         name="finish",
-    )(in_hbm(air), edge, side, source, ground, radiosity, surface, near, far)
+    )(in_hbm(air), edge, side, source, ground, radiosity, surface, near, far, near_own, far_own)
 
 
 def swap(value, axis, pairs):
@@ -776,13 +782,13 @@
     districts, blks = lax.axis_size("district"), lax.axis_size("blk")
     near_pairs = [(i, i + 1) for i in range(0, districts - 1, 2)]
     far_pairs = [(i, i + 1) for i in range(1, districts - 1, 2)]
-    near, far_small, own = pack(border_list, radiosity, air)
+    near, far_small, own, near_own = pack(border_list, radiosity, air)
     near = swap(near, "district", near_pairs)
     far_small = swap(hold(far_small, own), "district", far_pairs)
     columns = end_columns(air, own)
     once = first(air, columns)
     following, ground, sides, edge, air_cell = second(air, once, patch_cell)
-    far = rows(air, once)
+    far, far_own = rows(air, once)
     own = join(own, columns, near, far_small, far)
     far = hold(far, own)
     across = swap(own, "blk", [(i, i ^ 2) for i in range(blks) if i < i ^ 2])
@@ -805,7 +811,7 @@
         following,
     )
     air_next, radiosity_next, surface_next = finish(
-        air_next, edge, side, source, ground, radiosity, surface, near, far
+        air_next, edge, side, source, ground, radiosity, surface, near, far, near_own, far_own
     )
     return radiosity_next, surface_next, air_next
 

time: 25.4 us -> 25.3 us (level)
  transfers between devices with their start and end apart: 5 -> 5, of which waited for: 1 -> 1; matrix products, arithmetic and copies ran while one was open for 0% -> 0% of each run, Pallas kernels for 40% -> 39%
where the time goes in v4:
time: 25.3 us; the launch traced here: 25.1 us
  Pallas kernels  13 us (51%)
  starting transfers between devices  11 us (43%)
  between operations  0.87 us (3%)
    ppermute x5, starting transfers between devices, swap(): lax.ppermute(value, axis, [p for a, b in pairs for p in ((a, b), (b, a))])  11 us
    pallas_call x1, Pallas kernels, second(): pl.pallas_call(functools.partial(second_kernel, spans=spans), out_shape=(...  3.28 us
    pallas_call x1, Pallas kernels, main(): pl.pallas_call(main_kernel, out_shape=(jax.ShapeDtypeStruct((bands, patch...  3.18 us
    pallas_call x1, Pallas kernels, first(): pl.pallas_call(first_kernel, out_shape=jax.ShapeDtypeStruct(air.shape, F3...  2.33 us
    pallas_call x1, Pallas kernels, pack(): pl.pallas_call(pack_kernel, out_shape=(tile(row_tiles + borders + 1), til...  1.64 us
    pallas_call x1, Pallas kernels, finish(): pl.pallas_call(finish_kernel, out_shape=(jax.ShapeDtypeStruct(air.shape,...  1.56 us
    pallas_call x1, Pallas kernels, rows(): pl.pallas_call(rows_kernel, out_shape=(jax.ShapeDtypeStruct((count, 16, L...  0.65 us
  transfers between devices with their start and end apart: 5, of which 1 were waited for; matrix products, arithmetic and copies ran while one was open for 0% of the time, Pallas kernels for 39%

profile of v4, /device:TPU:13, one launch (start us, length us, event | category | flops | bytes accessed | tf_op | source)
XLA Modules:
  0.0 25.1 jit_solution(14695581252183720856)
XLA Ops:
  0.6 0.0 copy-start
  0.6 1.6 %pack.1 = (bf16[68,16,128]{2,1,0:T(8,128)(2,1)S(1)}, bf16[4,16,128]{2,1,0:T(8,128)(2,1)S(1)}, bf16[6,16,128]{2,1,0:T(8,128)(2,1)S(1)}, f32[2,64,1024]{2,1,0:T(8,128)S(1)}) custom-call(s32[3]{0:T(128)} %border_ref.1, bf16[16,768]{1,0:T(8,128)(2,1)} %radiosity_ref.1, f32[64,16,1024]{2,1,0:T(8,128)} %air_ref.9), custom_call_target="tpu_custom_call" | custom-call | flops 2000000000 | tf_op jit(solution)/shard_map/pack/pallas_call | solution.py:183
  2.3 0.3 %collective-permute-start = (bf16[68,16,128]{2,1,0:T(8,128)(2,1)S(1)}, bf16[68,16,128]{2,1,0:T(8,128)(2,1)S(1)}, u32[]{:S(2)}, u32[]{:S(2)}) collective-permute-start(bf16[68,16,128]{2,1,0:T(8,128)(2,1)S(1)} %get-tuple-element.24), channel_id=1, source_target_pairs={{0,4},{4,0},{8,12},{12,8},{16,20},{20,16},{24,28},{28,24},{1,5},{5... | collective-permute-start | bytes 835592 | tf_op jit(solution)/shard_map/ppermute | solution.py:767
  2.6 4.2 %collective-permute-start.1 = (bf16[4,16,128]{2,1,0:T(8,128)(2,1)S(1)}, bf16[4,16,128]{2,1,0:T(8,128)(2,1)S(1)}, u32[]{:S(2)}, u32[]{:S(2)}) collective-permute-start(bf16[4,16,128]{2,1,0:T(8,128)(2,1)S(1)} %hold.2), channel_id=1, source_target_pairs={{4,8},{8,4},{12,16},{16,12},{20,24},{24,20},{5,9},{9,5},{13,17},{1... | collective-permute-start | bytes 49160 | tf_op jit(solution)/shard_map/ppermute | solution.py:767
  6.7 0.0 copy-done
  6.7 0.3 %columns.1.after_ref.columns_ref = bf16[4,16,128]{2,1,0:T(8,128)(2,1)S(1)} custom-call(f32[64,16,1024]{2,1,0:T(8,128)S(1)} %copy-done, bf16[6,16,128]{2,1,0:T(8,128)(2,1)S(1)} %get-tuple-element.23.after_ref.own_ref), custom_call_target="tpu_custom_call" | custom-call | flops 100000000 | tf_op jit(solution)/shard_map/columns/pallas_call | solution.py:223
  7.1 2.3 %first.1.after_ref.once = f32[64,16,1024]{2,1,0:T(8,128)S(1)} custom-call(f32[64,16,1024]{2,1,0:T(8,128)S(1)} %copy-done, bf16[4,16,128]{2,1,0:T(8,128)(2,1)S(1)} %columns.1.after_ref.columns_ref), custom_call_target="tpu_custom_call" | custom-call | flops 1000000000 | tf_op jit(solution)/shard_map/first/pallas_call | solution.py:391
  9.4 0.7 %rows.1 = (bf16[64,16,128]{2,1,0:T(8,128)(2,1)S(1)}, f32[2,64,1024]{2,1,0:T(8,128)S(1)}) custom-call(f32[64,16,1024]{2,1,0:T(8,128)S(1)} %copy-done, f32[64,16,1024]{2,1,0:T(8,128)S(1)} %first.1.after_ref.once), custom_call_target="tpu_custom_call" | custom-call | flops 1000000000 | tf_op jit(solution)/shard_map/rows/pallas_call | solution.py:270
  10.1 0.0 copy-start.2
  10.1 0.0 collective-permute-done.1.far_ref
  10.1 0.1 collective-permute-done.near_ref
  10.2 1.3 %collective-permute-start.2 = (bf16[18,16,128]{2,1,0:T(8,128)(2,1)S(1)}, bf16[18,16,128]{2,1,0:T(8,128)(2,1)S(1)}, u32[]{:S(2)}, u32[]{:S(2)}) collective-permute-start(bf16[18,16,128]{2,1,0:T(8,128)(2,1)S(1)} %join.1.after_ref.one_ref), channel_id=1, source_target_pairs={{0,2},{2,0},{1,3},{3,1},{4,6},{6,4},{5,7},{7,5},{8,10},{10,8},{9,1... | collective-permute-start | bytes 221192 | tf_op jit(solution)/shard_map/ppermute | solution.py:767
  11.5 3.0 %collective-permute-start.4 = (bf16[64,16,128]{2,1,0:T(8,128)(2,1)S(1)}, bf16[64,16,128]{2,1,0:T(8,128)(2,1)S(1)}, u32[]{:S(2)}, u32[]{:S(2)}) collective-permute-start(bf16[64,16,128]{2,1,0:T(8,128)(2,1)S(1)} %hold.3.after_ref), channel_id=1, source_target_pairs={{4,8},{8,4},{12,16},{16,12},{20,24},{24,20},{5,9},{9,5},{13,17},{1... | collective-permute-start | bytes 786440 | tf_op jit(solution)/shard_map/ppermute | solution.py:767
  14.5 0.0 collective-permute-done.2.two_ref
  14.5 0.0 slice-start
  14.6 0.0 slice-start.1
  14.6 0.0 copy-start.1
  14.6 0.0 copy-start.3
  14.6 0.0 copy-start.4
  14.6 0.0 copy-start.5
  14.6 0.0 copy-start.6
  14.6 2.3 %collective-permute-start.3 = (bf16[36,16,128]{2,1,0:T(8,128)(2,1)S(1)}, bf16[36,16,128]{2,1,0:T(8,128)(2,1)S(1)}, u32[]{:S(2)}, u32[]{:S(2)}) collective-permute-start(bf16[36,16,128]{2,1,0:T(8,128)(2,1)S(1)} %stack.1.mine_ref), channel_id=1, source_target_pairs={{0,1},{1,0},{2,3},{3,2},{4,5},{5,4},{6,7},{7,6},{8,9},{9,8},{10,11... | collective-permute-start | bytes 442376 | tf_op jit(solution)/shard_map/ppermute | solution.py:767
  17.0 0.0 copy-done.2
  17.0 3.3 %second.1 = (f32[64,16,1024]{2,1,0:T(8,128)}, f32[16,1024]{1,0:T(8,128)S(1)}, f32[2,64,16,128]{3,2,1,0:T(8,128)S(1)}, f32[4,64,768]{2,1,0:T(8,128)S(1)}, f32[1,768]{1,0:T(1,128)S(1)}) custom-call(f32[64,16,1024]{2,1,0:T(8,128)S(1)} %copy-done, f32[64,16,1024]{2,1,0:T(8,128)S(1)} %first.1.after_ref.once, s32[768]{0:T(1024)S(1)} %copy-done.2), custom_call_target="tpu_custom_call" | custom-call | flops 1000000000 | tf_op jit(solution)/shard_map/second/pallas_call | solution.py:463
  20.3 0.0 collective-permute-done.3.theirs_ref
  20.3 0.0 slice-done
  20.3 0.0 slice-done.1
  20.3 0.0 copy-done.1
  20.3 0.0 copy-done.3
  20.3 0.0 copy-done.4
  20.3 0.0 copy-done.5
  20.3 0.0 copy-done.6
  20.4 3.2 %main.1 = (f32[16,768]{1,0:T(8,128)S(1)}, f32[1,768]{1,0:T(1,128)S(1)}, f32[64,16,1024]{2,1,0:T(8,128)}, f32[2,4,64,128]{3,2,1,0:T(8,128)S(1)}, f32[4,1024]{1,0:T(4,128)S(1)}, /*index=5*/f32[16,1024]{1,0:T(8,128)S(1)}) custom-call(s32[6,24]{1,0:T(8,128)S(1)} %copy-done.3, f32[16]{0:T(128)S(1)} %copy-done.6, ...), custom_call_target="tpu_custom_call", output_to_operand_aliasing={{2}: (12, {})} | custom-call | flops 1000000000 | tf_op jit(solution)/shard_map/main/pallas_call | solution.py:642
  23.5 0.0 collective-permute-done.4.far_ref
  23.5 1.6 %finish.1 = (f32[64,16,1024]{2,1,0:T(8,128)}, f32[16,768]{1,0:T(8,128)}, f32[768]{0:T(1024)}) custom-call(f32[64,16,1024]{2,1,0:T(8,128)} %get-tuple-element.31.air_ref, f32[4,64,768]{2,1,0:T(8,128)S(1)} %get-tuple-element.32.edge_ref, f32[2,4,64,128]{3,2,1,0:T(8,128)S(1)} %get-tuple-element.33.side_ref, ...), custom_call_target="tpu_custom_call", output_to_operand_aliasing={{0}: (0, {})} | custom-call | tf_op jit(solution)/shard_map/finish/pallas_call | solution.py:750
  (5 shorter events, 0.1 us)
Async XLA Ops:
  0.6 6.1 %copy-start = (f32[64,16,1024]{2,1,0:T(8,128)S(1)}, f32[64,16,1024]{2,1,0:T(8,128)}, u32[]{:S(2)}) copy-start(f32[64,16,1024]{2,1,0:T(8,128)} %air_ref.9) | copy-start | bytes 12582916
  2.3 7.9 %collective-permute-start = (bf16[68,16,128]{2,1,0:T(8,128)(2,1)S(1)}, bf16[68,16,128]{2,1,0:T(8,128)(2,1)S(1)}, u32[]{:S(2)}, u32[]{:S(2)}) collective-permute-start(bf16[68,16,128]{2,1,0:T(8,128)(2,1)S(1)} %get-tuple-element.24), channel_id=1, source_target_pairs={{0,4},{4,0},{8,12},{12,8},{16,20},{20,16},{24,28},{28,24},{1,5},{5... | collective-permute-start | bytes 835592 | tf_op jit(solution)/shard_map/ppermute | solution.py:767
  2.6 7.5 %collective-permute-start.1 = (bf16[4,16,128]{2,1,0:T(8,128)(2,1)S(1)}, bf16[4,16,128]{2,1,0:T(8,128)(2,1)S(1)}, u32[]{:S(2)}, u32[]{:S(2)}) collective-permute-start(bf16[4,16,128]{2,1,0:T(8,128)(2,1)S(1)} %hold.2), channel_id=1, source_target_pairs={{4,8},{8,4},{12,16},{16,12},{20,24},{24,20},{5,9},{9,5},{13,17},{1... | collective-permute-start | bytes 49160 | tf_op jit(solution)/shard_map/ppermute | solution.py:767
  10.1 6.9 %copy-start.2 = (s32[768]{0:T(1024)S(1)}, s32[768]{0:T(1024)}, u32[]{:S(2)}) copy-start(s32[768]{0:T(1024)} %cell_ref.3) | copy-start | bytes 9220
  10.2 4.3 %collective-permute-start.2 = (bf16[18,16,128]{2,1,0:T(8,128)(2,1)S(1)}, bf16[18,16,128]{2,1,0:T(8,128)(2,1)S(1)}, u32[]{:S(2)}, u32[]{:S(2)}) collective-permute-start(bf16[18,16,128]{2,1,0:T(8,128)(2,1)S(1)} %join.1.after_ref.one_ref), channel_id=1, source_target_pairs={{0,2},{2,0},{1,3},{3,1},{4,6},{6,4},{5,7},{7,5},{8,10},{10,8},{9,1... | collective-permute-start | bytes 221192 | tf_op jit(solution)/shard_map/ppermute | solution.py:767
  11.5 12.0 %collective-permute-start.4 = (bf16[64,16,128]{2,1,0:T(8,128)(2,1)S(1)}, bf16[64,16,128]{2,1,0:T(8,128)(2,1)S(1)}, u32[]{:S(2)}, u32[]{:S(2)}) collective-permute-start(bf16[64,16,128]{2,1,0:T(8,128)(2,1)S(1)} %hold.3.after_ref), channel_id=1, source_target_pairs={{4,8},{8,4},{12,16},{16,12},{20,24},{24,20},{5,9},{9,5},{13,17},{1... | collective-permute-start | bytes 786440 | tf_op jit(solution)/shard_map/ppermute | solution.py:767
  14.5 5.8 %slice-start = ((s8[4718592]{0:T(1024)(128)(4,1)}), s8[4194304]{0:T(1024)(128)(4,1)S(1)}, s32[]{:S(2)}) async-start(s8[4718592]{0:T(1024)(128)(4,1)} %bitcast), calls=%async_computation | async-start | bytes 8388608
  14.6 5.7 %slice-start.1 = ((s8[4718592]{0:T(1024)(128)(4,1)}), s8[524288]{0:T(1024)(128)(4,1)S(1)}, s32[]{:S(2)}) async-start(s8[4718592]{0:T(1024)(128)(4,1)} %bitcast), calls=%async_computation.1 | async-start | bytes 1048576
  14.6 5.7 %copy-start.1 = (bf16[16,768]{1,0:T(8,128)(2,1)S(1)}, bf16[16,768]{1,0:T(8,128)(2,1)}, u32[]{:S(2)}) copy-start(bf16[16,768]{1,0:T(8,128)(2,1)} %reflectance_ref.1) | copy-start | bytes 73732
  14.6 5.7 %copy-start.3 = (s32[6,24]{1,0:T(8,128)S(1)}, s32[6,24]{1,0:T(8,128)}, u32[]{:S(2)}) copy-start(s32[6,24]{1,0:T(8,128)} %cols_ref.1) | copy-start | bytes 1732
  14.6 5.7 %copy-start.4 = (f32[768]{0:T(1024)S(1)}, f32[768]{0:T(1024)}, u32[]{:S(2)}) copy-start(f32[768]{0:T(1024)} %emissivity_ref.1) | copy-start | bytes 9220
  14.6 5.7 %copy-start.5 = (f32[768]{0:T(1024)S(1)}, f32[768]{0:T(1024)}, u32[]{:S(2)}) copy-start(f32[768]{0:T(1024)} %temp_ref.1) | copy-start | bytes 9220
  14.6 5.7 %copy-start.6 = (f32[16]{0:T(128)S(1)}, f32[16]{0:T(128)}, u32[]{:S(2)}) copy-start(f32[16]{0:T(128)} %weight_ref.1) | copy-start | bytes 196
  14.6 5.6 %collective-permute-start.3 = (bf16[36,16,128]{2,1,0:T(8,128)(2,1)S(1)}, bf16[36,16,128]{2,1,0:T(8,128)(2,1)S(1)}, u32[]{:S(2)}, u32[]{:S(2)}) collective-permute-start(bf16[36,16,128]{2,1,0:T(8,128)(2,1)S(1)} %stack.1.mine_ref), channel_id=1, source_target_pairs={{0,1},{1,0},{2,3},{3,2},{4,5},{5,4},{6,7},{7,6},{8,9},{9,8},{10,11... | collective-permute-start | bytes 442376 | tf_op jit(solution)/shard_map/ppermute | solution.py:767

commit v5 on v4

--- a/solution.py
+++ b/solution.py
@@ -618,7 +618,7 @@
             (((1,), (1,)), ((), ())),
             preferred_element_type=F32,
         )
-        for piece in split(flux, 3)
+        for piece in split(flux, 2)
     )
 
     for t in range(tiles):

time: 25.3 us -> 25.1 us (level)
  no operation moved by 1% of the time
where the time goes in v5:
time: 25.1 us; the launch traced here: 24.9 us
  Pallas kernels  12.8 us (51%)
  starting transfers between devices  11 us (44%)
  between operations  0.87 us (3%)
    ppermute x5, starting transfers between devices, swap(): lax.ppermute(value, axis, [p for a, b in pairs for p in ((a, b), (b, a))])  11 us
    pallas_call x1, Pallas kernels, second(): pl.pallas_call(functools.partial(second_kernel, spans=spans), out_shape=(...  3.28 us
    pallas_call x1, Pallas kernels, main(): pl.pallas_call(main_kernel, out_shape=(jax.ShapeDtypeStruct((bands, patch...  3.01 us
    pallas_call x1, Pallas kernels, first(): pl.pallas_call(first_kernel, out_shape=jax.ShapeDtypeStruct(air.shape, F3...  2.33 us
    pallas_call x1, Pallas kernels, pack(): pl.pallas_call(pack_kernel, out_shape=(tile(row_tiles + borders + 1), til...  1.64 us
    pallas_call x1, Pallas kernels, finish(): pl.pallas_call(finish_kernel, out_shape=(jax.ShapeDtypeStruct(air.shape,...  1.56 us
    pallas_call x1, Pallas kernels, rows(): pl.pallas_call(rows_kernel, out_shape=(jax.ShapeDtypeStruct((count, 16, L...  0.65 us
  transfers between devices with their start and end apart: 5, of which 1 were waited for; matrix products, arithmetic and copies ran while one was open for 0% of the time, Pallas kernels for 39%

profile of v5, /device:TPU:13, one launch (start us, length us, event | category | flops | bytes accessed | tf_op | source)
XLA Modules:
  0.0 24.9 jit_solution(17984522404679462221)
XLA Ops:
  0.6 0.0 copy-start
  0.6 1.6 %pack.1 = (bf16[68,16,128]{2,1,0:T(8,128)(2,1)S(1)}, bf16[4,16,128]{2,1,0:T(8,128)(2,1)S(1)}, bf16[6,16,128]{2,1,0:T(8,128)(2,1)S(1)}, f32[2,64,1024]{2,1,0:T(8,128)S(1)}) custom-call(s32[3]{0:T(128)} %border_ref.1, bf16[16,768]{1,0:T(8,128)(2,1)} %radiosity_ref.1, f32[64,16,1024]{2,1,0:T(8,128)} %air_ref.9), custom_call_target="tpu_custom_call" | custom-call | flops 2000000000 | tf_op jit(solution)/shard_map/pack/pallas_call | solution.py:183
  2.3 0.3 %collective-permute-start = (bf16[68,16,128]{2,1,0:T(8,128)(2,1)S(1)}, bf16[68,16,128]{2,1,0:T(8,128)(2,1)S(1)}, u32[]{:S(2)}, u32[]{:S(2)}) collective-permute-start(bf16[68,16,128]{2,1,0:T(8,128)(2,1)S(1)} %get-tuple-element.24), channel_id=1, source_target_pairs={{0,4},{4,0},{8,12},{12,8},{16,20},{20,16},{24,28},{28,24},{1,5},{5... | collective-permute-start | bytes 835592 | tf_op jit(solution)/shard_map/ppermute | solution.py:767
  2.6 4.2 %collective-permute-start.1 = (bf16[4,16,128]{2,1,0:T(8,128)(2,1)S(1)}, bf16[4,16,128]{2,1,0:T(8,128)(2,1)S(1)}, u32[]{:S(2)}, u32[]{:S(2)}) collective-permute-start(bf16[4,16,128]{2,1,0:T(8,128)(2,1)S(1)} %hold.2), channel_id=1, source_target_pairs={{4,8},{8,4},{12,16},{16,12},{20,24},{24,20},{5,9},{9,5},{13,17},{1... | collective-permute-start | bytes 49160 | tf_op jit(solution)/shard_map/ppermute | solution.py:767
  6.7 0.0 copy-done
  6.7 0.3 %columns.1.after_ref.columns_ref = bf16[4,16,128]{2,1,0:T(8,128)(2,1)S(1)} custom-call(f32[64,16,1024]{2,1,0:T(8,128)S(1)} %copy-done, bf16[6,16,128]{2,1,0:T(8,128)(2,1)S(1)} %get-tuple-element.23.after_ref.own_ref), custom_call_target="tpu_custom_call" | custom-call | flops 100000000 | tf_op jit(solution)/shard_map/columns/pallas_call | solution.py:223
  7.1 2.3 %first.1.after_ref.once = f32[64,16,1024]{2,1,0:T(8,128)S(1)} custom-call(f32[64,16,1024]{2,1,0:T(8,128)S(1)} %copy-done, bf16[4,16,128]{2,1,0:T(8,128)(2,1)S(1)} %columns.1.after_ref.columns_ref), custom_call_target="tpu_custom_call" | custom-call | flops 1000000000 | tf_op jit(solution)/shard_map/first/pallas_call | solution.py:391
  9.4 0.7 %rows.1 = (bf16[64,16,128]{2,1,0:T(8,128)(2,1)S(1)}, f32[2,64,1024]{2,1,0:T(8,128)S(1)}) custom-call(f32[64,16,1024]{2,1,0:T(8,128)S(1)} %copy-done, f32[64,16,1024]{2,1,0:T(8,128)S(1)} %first.1.after_ref.once), custom_call_target="tpu_custom_call" | custom-call | flops 1000000000 | tf_op jit(solution)/shard_map/rows/pallas_call | solution.py:270
  10.1 0.0 copy-start.2
  10.1 0.0 collective-permute-done.1.far_ref
  10.1 0.1 collective-permute-done.near_ref
  10.2 1.3 %collective-permute-start.2 = (bf16[18,16,128]{2,1,0:T(8,128)(2,1)S(1)}, bf16[18,16,128]{2,1,0:T(8,128)(2,1)S(1)}, u32[]{:S(2)}, u32[]{:S(2)}) collective-permute-start(bf16[18,16,128]{2,1,0:T(8,128)(2,1)S(1)} %join.1.after_ref.one_ref), channel_id=1, source_target_pairs={{0,2},{2,0},{1,3},{3,1},{4,6},{6,4},{5,7},{7,5},{8,10},{10,8},{9,1... | collective-permute-start | bytes 221192 | tf_op jit(solution)/shard_map/ppermute | solution.py:767
  11.5 3.0 %collective-permute-start.4 = (bf16[64,16,128]{2,1,0:T(8,128)(2,1)S(1)}, bf16[64,16,128]{2,1,0:T(8,128)(2,1)S(1)}, u32[]{:S(2)}, u32[]{:S(2)}) collective-permute-start(bf16[64,16,128]{2,1,0:T(8,128)(2,1)S(1)} %hold.3.after_ref), channel_id=1, source_target_pairs={{4,8},{8,4},{12,16},{16,12},{20,24},{24,20},{5,9},{9,5},{13,17},{1... | collective-permute-start | bytes 786440 | tf_op jit(solution)/shard_map/ppermute | solution.py:767
  14.5 0.0 collective-permute-done.2.two_ref
  14.5 0.0 slice-start
  14.6 0.0 slice-start.1
  14.6 0.0 copy-start.1
  14.6 0.0 copy-start.3
  14.6 0.0 copy-start.4
  14.6 0.0 copy-start.5
  14.6 0.0 copy-start.6
  14.6 2.3 %collective-permute-start.3 = (bf16[36,16,128]{2,1,0:T(8,128)(2,1)S(1)}, bf16[36,16,128]{2,1,0:T(8,128)(2,1)S(1)}, u32[]{:S(2)}, u32[]{:S(2)}) collective-permute-start(bf16[36,16,128]{2,1,0:T(8,128)(2,1)S(1)} %stack.1.mine_ref), channel_id=1, source_target_pairs={{0,1},{1,0},{2,3},{3,2},{4,5},{5,4},{6,7},{7,6},{8,9},{9,8},{10,11... | collective-permute-start | bytes 442376 | tf_op jit(solution)/shard_map/ppermute | solution.py:767
  17.0 0.0 copy-done.2
  17.0 3.3 %second.1 = (f32[64,16,1024]{2,1,0:T(8,128)}, f32[16,1024]{1,0:T(8,128)S(1)}, f32[2,64,16,128]{3,2,1,0:T(8,128)S(1)}, f32[4,64,768]{2,1,0:T(8,128)S(1)}, f32[1,768]{1,0:T(1,128)S(1)}) custom-call(f32[64,16,1024]{2,1,0:T(8,128)S(1)} %copy-done, f32[64,16,1024]{2,1,0:T(8,128)S(1)} %first.1.after_ref.once, s32[768]{0:T(1024)S(1)} %copy-done.2), custom_call_target="tpu_custom_call" | custom-call | flops 1000000000 | tf_op jit(solution)/shard_map/second/pallas_call | solution.py:463
  20.3 0.0 collective-permute-done.3.theirs_ref
  20.3 0.0 slice-done
  20.3 0.0 slice-done.1
  20.3 0.0 copy-done.1
  20.3 0.0 copy-done.3
  20.3 0.0 copy-done.4
  20.3 0.0 copy-done.5
  20.3 0.0 copy-done.6
  20.4 3.0 %main.1 = (f32[16,768]{1,0:T(8,128)S(1)}, f32[1,768]{1,0:T(1,128)S(1)}, f32[64,16,1024]{2,1,0:T(8,128)}, f32[2,4,64,128]{3,2,1,0:T(8,128)S(1)}, f32[4,1024]{1,0:T(4,128)S(1)}, /*index=5*/f32[16,1024]{1,0:T(8,128)S(1)}) custom-call(s32[6,24]{1,0:T(8,128)S(1)} %copy-done.3, f32[16]{0:T(128)S(1)} %copy-done.6, ...), custom_call_target="tpu_custom_call", output_to_operand_aliasing={{2}: (12, {})} | custom-call | flops 1000000000 | tf_op jit(solution)/shard_map/main/pallas_call | solution.py:642
  23.4 0.0 collective-permute-done.4.far_ref
  23.4 1.6 %finish.1 = (f32[64,16,1024]{2,1,0:T(8,128)}, f32[16,768]{1,0:T(8,128)}, f32[768]{0:T(1024)}) custom-call(f32[64,16,1024]{2,1,0:T(8,128)} %get-tuple-element.31.air_ref, f32[4,64,768]{2,1,0:T(8,128)S(1)} %get-tuple-element.32.edge_ref, f32[2,4,64,128]{3,2,1,0:T(8,128)S(1)} %get-tuple-element.33.side_ref, ...), custom_call_target="tpu_custom_call", output_to_operand_aliasing={{0}: (0, {})} | custom-call | tf_op jit(solution)/shard_map/finish/pallas_call | solution.py:750
  (5 shorter events, 0.1 us)
Async XLA Ops:
  0.6 6.1 %copy-start = (f32[64,16,1024]{2,1,0:T(8,128)S(1)}, f32[64,16,1024]{2,1,0:T(8,128)}, u32[]{:S(2)}) copy-start(f32[64,16,1024]{2,1,0:T(8,128)} %air_ref.9) | copy-start | bytes 12582916
  2.3 7.9 %collective-permute-start = (bf16[68,16,128]{2,1,0:T(8,128)(2,1)S(1)}, bf16[68,16,128]{2,1,0:T(8,128)(2,1)S(1)}, u32[]{:S(2)}, u32[]{:S(2)}) collective-permute-start(bf16[68,16,128]{2,1,0:T(8,128)(2,1)S(1)} %get-tuple-element.24), channel_id=1, source_target_pairs={{0,4},{4,0},{8,12},{12,8},{16,20},{20,16},{24,28},{28,24},{1,5},{5... | collective-permute-start | bytes 835592 | tf_op jit(solution)/shard_map/ppermute | solution.py:767
  2.6 7.5 %collective-permute-start.1 = (bf16[4,16,128]{2,1,0:T(8,128)(2,1)S(1)}, bf16[4,16,128]{2,1,0:T(8,128)(2,1)S(1)}, u32[]{:S(2)}, u32[]{:S(2)}) collective-permute-start(bf16[4,16,128]{2,1,0:T(8,128)(2,1)S(1)} %hold.2), channel_id=1, source_target_pairs={{4,8},{8,4},{12,16},{16,12},{20,24},{24,20},{5,9},{9,5},{13,17},{1... | collective-permute-start | bytes 49160 | tf_op jit(solution)/shard_map/ppermute | solution.py:767
  10.1 6.9 %copy-start.2 = (s32[768]{0:T(1024)S(1)}, s32[768]{0:T(1024)}, u32[]{:S(2)}) copy-start(s32[768]{0:T(1024)} %cell_ref.3) | copy-start | bytes 9220
  10.2 4.3 %collective-permute-start.2 = (bf16[18,16,128]{2,1,0:T(8,128)(2,1)S(1)}, bf16[18,16,128]{2,1,0:T(8,128)(2,1)S(1)}, u32[]{:S(2)}, u32[]{:S(2)}) collective-permute-start(bf16[18,16,128]{2,1,0:T(8,128)(2,1)S(1)} %join.1.after_ref.one_ref), channel_id=1, source_target_pairs={{0,2},{2,0},{1,3},{3,1},{4,6},{6,4},{5,7},{7,5},{8,10},{10,8},{9,1... | collective-permute-start | bytes 221192 | tf_op jit(solution)/shard_map/ppermute | solution.py:767
  11.5 11.8 %collective-permute-start.4 = (bf16[64,16,128]{2,1,0:T(8,128)(2,1)S(1)}, bf16[64,16,128]{2,1,0:T(8,128)(2,1)S(1)}, u32[]{:S(2)}, u32[]{:S(2)}) collective-permute-start(bf16[64,16,128]{2,1,0:T(8,128)(2,1)S(1)} %hold.3.after_ref), channel_id=1, source_target_pairs={{4,8},{8,4},{12,16},{16,12},{20,24},{24,20},{5,9},{9,5},{13,17},{1... | collective-permute-start | bytes 786440 | tf_op jit(solution)/shard_map/ppermute | solution.py:767
  14.5 5.8 %slice-start = ((s8[4718592]{0:T(1024)(128)(4,1)}), s8[4194304]{0:T(1024)(128)(4,1)S(1)}, s32[]{:S(2)}) async-start(s8[4718592]{0:T(1024)(128)(4,1)} %bitcast), calls=%async_computation | async-start | bytes 8388608
  14.6 5.7 %slice-start.1 = ((s8[4718592]{0:T(1024)(128)(4,1)}), s8[524288]{0:T(1024)(128)(4,1)S(1)}, s32[]{:S(2)}) async-start(s8[4718592]{0:T(1024)(128)(4,1)} %bitcast), calls=%async_computation.1 | async-start | bytes 1048576
  14.6 5.7 %copy-start.1 = (bf16[16,768]{1,0:T(8,128)(2,1)S(1)}, bf16[16,768]{1,0:T(8,128)(2,1)}, u32[]{:S(2)}) copy-start(bf16[16,768]{1,0:T(8,128)(2,1)} %reflectance_ref.1) | copy-start | bytes 73732
  14.6 5.7 %copy-start.3 = (s32[6,24]{1,0:T(8,128)S(1)}, s32[6,24]{1,0:T(8,128)}, u32[]{:S(2)}) copy-start(s32[6,24]{1,0:T(8,128)} %cols_ref.1) | copy-start | bytes 1732
  14.6 5.7 %copy-start.4 = (f32[768]{0:T(1024)S(1)}, f32[768]{0:T(1024)}, u32[]{:S(2)}) copy-start(f32[768]{0:T(1024)} %emissivity_ref.1) | copy-start | bytes 9220
  14.6 5.7 %copy-start.5 = (f32[768]{0:T(1024)S(1)}, f32[768]{0:T(1024)}, u32[]{:S(2)}) copy-start(f32[768]{0:T(1024)} %temp_ref.1) | copy-start | bytes 9220
  14.6 5.7 %copy-start.6 = (f32[16]{0:T(128)S(1)}, f32[16]{0:T(128)}, u32[]{:S(2)}) copy-start(f32[16]{0:T(128)} %weight_ref.1) | copy-start | bytes 196
  14.6 5.6 %collective-permute-start.3 = (bf16[36,16,128]{2,1,0:T(8,128)(2,1)S(1)}, bf16[36,16,128]{2,1,0:T(8,128)(2,1)S(1)}, u32[]{:S(2)}, u32[]{:S(2)}) collective-permute-start(bf16[36,16,128]{2,1,0:T(8,128)(2,1)S(1)} %stack.1.mine_ref), channel_id=1, source_target_pairs={{0,1},{1,0},{2,3},{3,2},{4,5},{5,4},{6,7},{7,6},{8,9},{9,8},{10,11... | collective-permute-start | bytes 442376 | tf_op jit(solution)/shard_map/ppermute | solution.py:767

commit v6 on v5

--- a/solution.py
+++ b/solution.py
@@ -704,16 +704,7 @@
     odd = lax.rem(district, 2)
     has = flag(district > 0), flag(district < lax.axis_size("district") - 1)
     ground = iota((levels, LANES), 0) == 0
-    copies = [
-        pltpu.make_async_copy(ground_ref.at[x], out_ref.at[0, x], sem.at[2 + x])
-        for x in range(2, depth - 2)
-    ]
-    copies += [
-        pltpu.make_async_copy(radiosity_ref, radiosity_out, value_sem.at[0]),
-        pltpu.make_async_copy(surface_ref.at[0], surface_out, value_sem.at[1]),
-    ]
-    for c in copies:
-        c.start()
+    copies = []
     for side in range(2):
         use_near = (odd == 1) if side == 0 else (odd == 0)
 
@@ -741,7 +732,17 @@
             c = pltpu.make_async_copy(slabs.at[i], out_ref.at[:, x, :], sem.at[i])
             c.start()
             copies.append(c)
-    for c in copies:
+    small = [
+        pltpu.make_async_copy(ground_ref.at[x], out_ref.at[0, x], sem.at[2 + x])
+        for x in range(2, depth - 2)
+    ]
+    small += [
+        pltpu.make_async_copy(radiosity_ref, radiosity_out, value_sem.at[0]),
+        pltpu.make_async_copy(surface_ref.at[0], surface_out, value_sem.at[1]),
+    ]
+    for c in small:
+        c.start()
+    for c in copies + small:
         c.wait()
 
 

time: 25.1 us -> 25.2 us (level)
  no operation moved by 1% of the time
where the time goes in v6:
time: 25.2 us; the launch traced here: 25 us
  Pallas kernels  12.9 us (51%)
  starting transfers between devices  11 us (44%)
  between operations  0.87 us (3%)
    ppermute x5, starting transfers between devices, swap(): lax.ppermute(value, axis, [p for a, b in pairs for p in ((a, b), (b, a))])  11 us
    pallas_call x1, Pallas kernels, second(): pl.pallas_call(functools.partial(second_kernel, spans=spans), out_shape=(...  3.28 us
    pallas_call x1, Pallas kernels, main(): pl.pallas_call(main_kernel, out_shape=(jax.ShapeDtypeStruct((bands, patch...  3 us
    pallas_call x1, Pallas kernels, first(): pl.pallas_call(first_kernel, out_shape=jax.ShapeDtypeStruct(air.shape, F3...  2.33 us
    pallas_call x1, Pallas kernels, pack(): pl.pallas_call(pack_kernel, out_shape=(tile(row_tiles + borders + 1), til...  1.64 us
    pallas_call x1, Pallas kernels, finish(): pl.pallas_call(finish_kernel, out_shape=(jax.ShapeDtypeStruct(air.shape,...  1.61 us
    pallas_call x1, Pallas kernels, rows(): pl.pallas_call(rows_kernel, out_shape=(jax.ShapeDtypeStruct((count, 16, L...  0.65 us
  transfers between devices with their start and end apart: 5, of which 1 were waited for; matrix products, arithmetic and copies ran while one was open for 0% of the time, Pallas kernels for 39%

profile of v6, /device:TPU:13, one launch (start us, length us, event | category | flops | bytes accessed | tf_op | source)
XLA Modules:
  0.0 25.0 jit_solution(11507734764920304059)
XLA Ops:
  0.6 0.0 copy-start
  0.6 1.6 %pack.1 = (bf16[68,16,128]{2,1,0:T(8,128)(2,1)S(1)}, bf16[4,16,128]{2,1,0:T(8,128)(2,1)S(1)}, bf16[6,16,128]{2,1,0:T(8,128)(2,1)S(1)}, f32[2,64,1024]{2,1,0:T(8,128)S(1)}) custom-call(s32[3]{0:T(128)} %border_ref.1, bf16[16,768]{1,0:T(8,128)(2,1)} %radiosity_ref.1, f32[64,16,1024]{2,1,0:T(8,128)} %air_ref.9), custom_call_target="tpu_custom_call" | custom-call | flops 2000000000 | tf_op jit(solution)/shard_map/pack/pallas_call | solution.py:183
  2.3 0.3 %collective-permute-start = (bf16[68,16,128]{2,1,0:T(8,128)(2,1)S(1)}, bf16[68,16,128]{2,1,0:T(8,128)(2,1)S(1)}, u32[]{:S(2)}, u32[]{:S(2)}) collective-permute-start(bf16[68,16,128]{2,1,0:T(8,128)(2,1)S(1)} %get-tuple-element.24), channel_id=1, source_target_pairs={{0,4},{4,0},{8,12},{12,8},{16,20},{20,16},{24,28},{28,24},{1,5},{5... | collective-permute-start | bytes 835592 | tf_op jit(solution)/shard_map/ppermute | solution.py:768
  2.6 4.2 %collective-permute-start.1 = (bf16[4,16,128]{2,1,0:T(8,128)(2,1)S(1)}, bf16[4,16,128]{2,1,0:T(8,128)(2,1)S(1)}, u32[]{:S(2)}, u32[]{:S(2)}) collective-permute-start(bf16[4,16,128]{2,1,0:T(8,128)(2,1)S(1)} %hold.2), channel_id=1, source_target_pairs={{4,8},{8,4},{12,16},{16,12},{20,24},{24,20},{5,9},{9,5},{13,17},{1... | collective-permute-start | bytes 49160 | tf_op jit(solution)/shard_map/ppermute | solution.py:768
  6.7 0.0 copy-done
  6.7 0.3 %columns.1.after_ref.columns_ref = bf16[4,16,128]{2,1,0:T(8,128)(2,1)S(1)} custom-call(f32[64,16,1024]{2,1,0:T(8,128)S(1)} %copy-done, bf16[6,16,128]{2,1,0:T(8,128)(2,1)S(1)} %get-tuple-element.23.after_ref.own_ref), custom_call_target="tpu_custom_call" | custom-call | flops 100000000 | tf_op jit(solution)/shard_map/columns/pallas_call | solution.py:223
  7.1 2.3 %first.1.after_ref.once = f32[64,16,1024]{2,1,0:T(8,128)S(1)} custom-call(f32[64,16,1024]{2,1,0:T(8,128)S(1)} %copy-done, bf16[4,16,128]{2,1,0:T(8,128)(2,1)S(1)} %columns.1.after_ref.columns_ref), custom_call_target="tpu_custom_call" | custom-call | flops 1000000000 | tf_op jit(solution)/shard_map/first/pallas_call | solution.py:391
  9.4 0.7 %rows.1 = (bf16[64,16,128]{2,1,0:T(8,128)(2,1)S(1)}, f32[2,64,1024]{2,1,0:T(8,128)S(1)}) custom-call(f32[64,16,1024]{2,1,0:T(8,128)S(1)} %copy-done, f32[64,16,1024]{2,1,0:T(8,128)S(1)} %first.1.after_ref.once), custom_call_target="tpu_custom_call" | custom-call | flops 1000000000 | tf_op jit(solution)/shard_map/rows/pallas_call | solution.py:270
  10.1 0.0 copy-start.2
  10.1 0.0 collective-permute-done.1.far_ref
  10.1 0.1 collective-permute-done.near_ref
  10.2 1.3 %collective-permute-start.2 = (bf16[18,16,128]{2,1,0:T(8,128)(2,1)S(1)}, bf16[18,16,128]{2,1,0:T(8,128)(2,1)S(1)}, u32[]{:S(2)}, u32[]{:S(2)}) collective-permute-start(bf16[18,16,128]{2,1,0:T(8,128)(2,1)S(1)} %join.1.after_ref.one_ref), channel_id=1, source_target_pairs={{0,2},{2,0},{1,3},{3,1},{4,6},{6,4},{5,7},{7,5},{8,10},{10,8},{9,1... | collective-permute-start | bytes 221192 | tf_op jit(solution)/shard_map/ppermute | solution.py:768
  11.5 3.0 %collective-permute-start.4 = (bf16[64,16,128]{2,1,0:T(8,128)(2,1)S(1)}, bf16[64,16,128]{2,1,0:T(8,128)(2,1)S(1)}, u32[]{:S(2)}, u32[]{:S(2)}) collective-permute-start(bf16[64,16,128]{2,1,0:T(8,128)(2,1)S(1)} %hold.3.after_ref), channel_id=1, source_target_pairs={{4,8},{8,4},{12,16},{16,12},{20,24},{24,20},{5,9},{9,5},{13,17},{1... | collective-permute-start | bytes 786440 | tf_op jit(solution)/shard_map/ppermute | solution.py:768
  14.5 0.0 collective-permute-done.2.two_ref
  14.5 0.0 slice-start
  14.6 0.0 slice-start.1
  14.6 0.0 copy-start.1
  14.6 0.0 copy-start.3
  14.6 0.0 copy-start.4
  14.6 0.0 copy-start.5
  14.6 0.0 copy-start.6
  14.6 2.3 %collective-permute-start.3 = (bf16[36,16,128]{2,1,0:T(8,128)(2,1)S(1)}, bf16[36,16,128]{2,1,0:T(8,128)(2,1)S(1)}, u32[]{:S(2)}, u32[]{:S(2)}) collective-permute-start(bf16[36,16,128]{2,1,0:T(8,128)(2,1)S(1)} %stack.1.mine_ref), channel_id=1, source_target_pairs={{0,1},{1,0},{2,3},{3,2},{4,5},{5,4},{6,7},{7,6},{8,9},{9,8},{10,11... | collective-permute-start | bytes 442376 | tf_op jit(solution)/shard_map/ppermute | solution.py:768
  17.0 0.0 copy-done.2
  17.0 3.3 %second.1 = (f32[64,16,1024]{2,1,0:T(8,128)}, f32[16,1024]{1,0:T(8,128)S(1)}, f32[2,64,16,128]{3,2,1,0:T(8,128)S(1)}, f32[4,64,768]{2,1,0:T(8,128)S(1)}, f32[1,768]{1,0:T(1,128)S(1)}) custom-call(f32[64,16,1024]{2,1,0:T(8,128)S(1)} %copy-done, f32[64,16,1024]{2,1,0:T(8,128)S(1)} %first.1.after_ref.once, s32[768]{0:T(1024)S(1)} %copy-done.2), custom_call_target="tpu_custom_call" | custom-call | flops 1000000000 | tf_op jit(solution)/shard_map/second/pallas_call | solution.py:463
  20.3 0.0 collective-permute-done.3.theirs_ref
  20.3 0.0 slice-done
  20.3 0.0 slice-done.1
  20.3 0.0 copy-done.1
  20.3 0.0 copy-done.3
  20.3 0.0 copy-done.4
  20.3 0.0 copy-done.5
  20.3 0.0 copy-done.6
  20.4 3.0 %main.1 = (f32[16,768]{1,0:T(8,128)S(1)}, f32[1,768]{1,0:T(1,128)S(1)}, f32[64,16,1024]{2,1,0:T(8,128)}, f32[2,4,64,128]{3,2,1,0:T(8,128)S(1)}, f32[4,1024]{1,0:T(4,128)S(1)}, /*index=5*/f32[16,1024]{1,0:T(8,128)S(1)}) custom-call(s32[6,24]{1,0:T(8,128)S(1)} %copy-done.3, f32[16]{0:T(128)S(1)} %copy-done.6, ...), custom_call_target="tpu_custom_call", output_to_operand_aliasing={{2}: (12, {})} | custom-call | flops 1000000000 | tf_op jit(solution)/shard_map/main/pallas_call | solution.py:642
  23.4 0.0 collective-permute-done.4.far_ref
  23.4 1.6 %finish.1 = (f32[64,16,1024]{2,1,0:T(8,128)}, f32[16,768]{1,0:T(8,128)}, f32[768]{0:T(1024)}) custom-call(f32[64,16,1024]{2,1,0:T(8,128)} %get-tuple-element.31.air_ref, f32[4,64,768]{2,1,0:T(8,128)S(1)} %get-tuple-element.32.edge_ref, f32[2,4,64,128]{3,2,1,0:T(8,128)S(1)} %get-tuple-element.33.side_ref, ...), custom_call_target="tpu_custom_call", output_to_operand_aliasing={{0}: (0, {})} | custom-call | tf_op jit(solution)/shard_map/finish/pallas_call | solution.py:751
  (5 shorter events, 0.1 us)
Async XLA Ops:
  0.6 6.1 %copy-start = (f32[64,16,1024]{2,1,0:T(8,128)S(1)}, f32[64,16,1024]{2,1,0:T(8,128)}, u32[]{:S(2)}) copy-start(f32[64,16,1024]{2,1,0:T(8,128)} %air_ref.9) | copy-start | bytes 12582916
  2.3 7.9 %collective-permute-start = (bf16[68,16,128]{2,1,0:T(8,128)(2,1)S(1)}, bf16[68,16,128]{2,1,0:T(8,128)(2,1)S(1)}, u32[]{:S(2)}, u32[]{:S(2)}) collective-permute-start(bf16[68,16,128]{2,1,0:T(8,128)(2,1)S(1)} %get-tuple-element.24), channel_id=1, source_target_pairs={{0,4},{4,0},{8,12},{12,8},{16,20},{20,16},{24,28},{28,24},{1,5},{5... | collective-permute-start | bytes 835592 | tf_op jit(solution)/shard_map/ppermute | solution.py:768
  2.6 7.5 %collective-permute-start.1 = (bf16[4,16,128]{2,1,0:T(8,128)(2,1)S(1)}, bf16[4,16,128]{2,1,0:T(8,128)(2,1)S(1)}, u32[]{:S(2)}, u32[]{:S(2)}) collective-permute-start(bf16[4,16,128]{2,1,0:T(8,128)(2,1)S(1)} %hold.2), channel_id=1, source_target_pairs={{4,8},{8,4},{12,16},{16,12},{20,24},{24,20},{5,9},{9,5},{13,17},{1... | collective-permute-start | bytes 49160 | tf_op jit(solution)/shard_map/ppermute | solution.py:768
  10.1 6.9 %copy-start.2 = (s32[768]{0:T(1024)S(1)}, s32[768]{0:T(1024)}, u32[]{:S(2)}) copy-start(s32[768]{0:T(1024)} %cell_ref.3) | copy-start | bytes 9220
  10.2 4.3 %collective-permute-start.2 = (bf16[18,16,128]{2,1,0:T(8,128)(2,1)S(1)}, bf16[18,16,128]{2,1,0:T(8,128)(2,1)S(1)}, u32[]{:S(2)}, u32[]{:S(2)}) collective-permute-start(bf16[18,16,128]{2,1,0:T(8,128)(2,1)S(1)} %join.1.after_ref.one_ref), channel_id=1, source_target_pairs={{0,2},{2,0},{1,3},{3,1},{4,6},{6,4},{5,7},{7,5},{8,10},{10,8},{9,1... | collective-permute-start | bytes 221192 | tf_op jit(solution)/shard_map/ppermute | solution.py:768
  11.5 11.8 %collective-permute-start.4 = (bf16[64,16,128]{2,1,0:T(8,128)(2,1)S(1)}, bf16[64,16,128]{2,1,0:T(8,128)(2,1)S(1)}, u32[]{:S(2)}, u32[]{:S(2)}) collective-permute-start(bf16[64,16,128]{2,1,0:T(8,128)(2,1)S(1)} %hold.3.after_ref), channel_id=1, source_target_pairs={{4,8},{8,4},{12,16},{16,12},{20,24},{24,20},{5,9},{9,5},{13,17},{1... | collective-permute-start | bytes 786440 | tf_op jit(solution)/shard_map/ppermute | solution.py:768
  14.5 5.8 %slice-start = ((s8[4718592]{0:T(1024)(128)(4,1)}), s8[4194304]{0:T(1024)(128)(4,1)S(1)}, s32[]{:S(2)}) async-start(s8[4718592]{0:T(1024)(128)(4,1)} %bitcast), calls=%async_computation | async-start | bytes 8388608
  14.6 5.7 %slice-start.1 = ((s8[4718592]{0:T(1024)(128)(4,1)}), s8[524288]{0:T(1024)(128)(4,1)S(1)}, s32[]{:S(2)}) async-start(s8[4718592]{0:T(1024)(128)(4,1)} %bitcast), calls=%async_computation.1 | async-start | bytes 1048576
  14.6 5.7 %copy-start.1 = (bf16[16,768]{1,0:T(8,128)(2,1)S(1)}, bf16[16,768]{1,0:T(8,128)(2,1)}, u32[]{:S(2)}) copy-start(bf16[16,768]{1,0:T(8,128)(2,1)} %reflectance_ref.1) | copy-start | bytes 73732
  14.6 5.7 %copy-start.3 = (s32[6,24]{1,0:T(8,128)S(1)}, s32[6,24]{1,0:T(8,128)}, u32[]{:S(2)}) copy-start(s32[6,24]{1,0:T(8,128)} %cols_ref.1) | copy-start | bytes 1732
  14.6 5.7 %copy-start.4 = (f32[768]{0:T(1024)S(1)}, f32[768]{0:T(1024)}, u32[]{:S(2)}) copy-start(f32[768]{0:T(1024)} %emissivity_ref.1) | copy-start | bytes 9220
  14.6 5.7 %copy-start.5 = (f32[768]{0:T(1024)S(1)}, f32[768]{0:T(1024)}, u32[]{:S(2)}) copy-start(f32[768]{0:T(1024)} %temp_ref.1) | copy-start | bytes 9220
  14.6 5.7 %copy-start.6 = (f32[16]{0:T(128)S(1)}, f32[16]{0:T(128)}, u32[]{:S(2)}) copy-start(f32[16]{0:T(128)} %weight_ref.1) | copy-start | bytes 196
  14.6 5.6 %collective-permute-start.3 = (bf16[36,16,128]{2,1,0:T(8,128)(2,1)S(1)}, bf16[36,16,128]{2,1,0:T(8,128)(2,1)S(1)}, u32[]{:S(2)}, u32[]{:S(2)}) collective-permute-start(bf16[36,16,128]{2,1,0:T(8,128)(2,1)S(1)} %stack.1.mine_ref), channel_id=1, source_target_pairs={{0,1},{1,0},{2,3},{3,2},{4,5},{5,4},{6,7},{7,6},{8,9},{9,8},{10,11... | collective-permute-start | bytes 442376 | tf_op jit(solution)/shard_map/ppermute | solution.py:768
